TPU v7x, 32 devices: a whole 2x2x4 slice. The times are simulated.
32 devices in a mesh: ctx: 8 (over y, x, core), fsdp: 4 (over z).
Axes of the slice: x: 2, y: 2, z: 4, core: 2. Of those that a mesh axis runs over, the one named last changes fastest.
Arguments:
- states: bfloat16 [4, 4096, 1024], P('fsdp', 'ctx'), may hold values from -6 to 6
- positions: int32 [4, 4096], P('fsdp', 'ctx'), may hold values from 0 to 2303, as said below
- segments: int32 [4, 4096], P('fsdp', 'ctx'), may hold values from 0 to 8, as said below
- encoded: bfloat16 [4, 512, 1024], P('fsdp', 'ctx'), may hold values from -6 to 6
- cotangent: bfloat16 [4, 4096, 1024], P('fsdp', 'ctx'), may hold values from -6 to 6
- self_gain: bfloat16 [1024], P('fsdp'), may hold values from 0.099609375 to 1.8984375
- self_query: bfloat16 [1024, 1024], P('fsdp'), may hold values from -0.0234375 to 0.0234375
- self_key: bfloat16 [1024, 1024], P('fsdp'), may hold values from -0.1875 to 0.1875
- self_value: bfloat16 [1024, 1024], P('fsdp'), may hold values from -0.1875 to 0.1875
- self_output: bfloat16 [1024, 1024], P('fsdp'), may hold values from -3 to 3
- bias_table: bfloat16 [32, 16], P('fsdp'), may hold values from -4 to 4
- cross_gain: bfloat16 [1024], P('fsdp'), may hold values from 0.099609375 to 1.8984375
- cross_query: bfloat16 [1024, 1024], P('fsdp'), may hold values from -0.0234375 to 0.0234375
- cross_key: bfloat16 [1024, 1024], P('fsdp'), may hold values from -0.1875 to 0.1875
- cross_value: bfloat16 [1024, 1024], P('fsdp'), may hold values from -0.1875 to 0.1875
- cross_output: bfloat16 [1024, 1024], P('fsdp'), may hold values from -2 to 2
- feed_gain: bfloat16 [1024], P('fsdp'), may hold values from 0.099609375 to 1.8984375
- gate_weight: bfloat16 [1024, 2816], P('fsdp'), may hold values from -0.1875 to 0.1875
- up_weight: bfloat16 [1024, 2816], P('fsdp'), may hold values from -0.1875 to 0.1875
- down_weight: bfloat16 [2816, 1024], P('fsdp'), may hold values from -0.109375 to 0.109375
Outputs:
- layer_out: bfloat16 [4, 4096, 1024], P('fsdp', 'ctx')
- states_grad: float32 [4, 4096, 1024], P('fsdp', 'ctx')
- encoded_grad: float32 [4, 512, 1024], P('fsdp', 'ctx')
- self_gain_grad: float32 [1024], P('fsdp')
- self_query_grad: float32 [1024, 1024], P('fsdp')
- self_key_grad: float32 [1024, 1024], P('fsdp')
- self_value_grad: float32 [1024, 1024], P('fsdp')
- self_output_grad: float32 [1024, 1024], P('fsdp')
- bias_table_grad: float32 [32, 16], P('fsdp')
- cross_gain_grad: float32 [1024], P('fsdp')
- cross_query_grad: float32 [1024, 1024], P('fsdp')
- cross_key_grad: float32 [1024, 1024], P('fsdp')
- cross_value_grad: float32 [1024, 1024], P('fsdp')
- cross_output_grad: float32 [1024, 1024], P('fsdp')
- feed_gain_grad: float32 [1024], P('fsdp')
- gate_weight_grad: float32 [1024, 2816], P('fsdp')
- up_weight_grad: float32 [1024, 2816], P('fsdp')
- down_weight_grad: float32 [2816, 1024], P('fsdp')
Inputs may be any that keep to these rules, and one draw needn't show every extreme that they name: In each group the 4096 tokens come in aligned blocks of 128; a block holds 128 consecutive tokens of the prompt (segment 0, positions 0 to 2047) or of one continuation c (segment c, positions 2048 to 2303); every block of the group occurs once, in an order drawn from the seed, and the first and the last block are prompt blocks. `segments`: the segment of each token, laid out as described for positions.
All inputs are finite; a program needn't handle non-finite values.
Results may differ from a plain program's by a relative error of at most 0.028.
Values may be sent and summed in bfloat16 or wider, within the bound.
No kernel may reach another device: no remote copies, remote signals or barrier semaphores. Data moves between devices by JAX's collectives and lax.ppermute only.
A program may use at most 320 MiB of HBM per device.

v0:
```python
import math

import jax
import jax.numpy as jnp
from jax import lax
from jax.sharding import PartitionSpec as P

BUCKETS = 32
DISTANCE = 128


epsilon = 1e-06
masked_value = -1e30
gelu_scale = math.sqrt(2.0 / math.pi)


def norm_rows(value, gain):
    return value * lax.rsqrt(jnp.mean(value * value, axis=-1, keepdims=True) + epsilon) * gain


def geglu(gate, up_part):
    return (
        0.5 * gate * (1.0 + jnp.tanh(gelu_scale * (gate + 0.044715 * gate * gate * gate))) * up_part
    )


def project(left, right):
    return jnp.einsum("gtd,de->gte", left, right, preferred_element_type=jnp.float32)


def project_back(left, right):
    return jnp.einsum("gte,de->gtd", left, right, preferred_element_type=jnp.float32)


def weight_grad(left, right):
    return jnp.einsum("gtd,gte->de", left, right, preferred_element_type=jnp.float32)


def bucket_edges():
    half_count = BUCKETS // 2
    return [
        math.ceil(half_count * (DISTANCE / half_count) ** (edge_number / half_count))
        for edge_number in range(1, half_count)
    ]


def relative_bucket(distance):
    bucket = jnp.minimum(distance, BUCKETS // 2)
    for edge_value in bucket_edges():
        bucket = bucket + (distance >= edge_value).astype(jnp.int32)
    return bucket


def pair_terms(query_heads, key_heads, query_pos, query_seg, key_pos, key_seg, table):
    raw = jnp.einsum("gqhd,gkhd->ghqk", query_heads, key_heads, preferred_element_type=jnp.float32)
    distance = jnp.maximum(query_pos[:, :, None] - key_pos[:, None, :], 0)
    onehot = (relative_bucket(distance)[..., None] == jnp.arange(BUCKETS, dtype=jnp.int32)).astype(
        jnp.bfloat16
    )
    bias = jnp.einsum("gqkb,bh->ghqk", onehot, table, preferred_element_type=jnp.float32)
    allowed = ((key_seg[:, None, :] == 0) | (key_seg[:, None, :] == query_seg[:, :, None])) & (
        key_pos[:, None, :] <= query_pos[:, :, None]
    )
    scores = jnp.where(allowed[:, None], raw + bias, masked_value)
    return (scores, onehot)


def block_grads(scores, onehot, log_total, delta, dout_heads, value_heads):
    probs = jnp.exp(scores - log_total[..., None])
    dprob = jnp.einsum(
        "gqhd,gkhd->ghqk", dout_heads, value_heads, preferred_element_type=jnp.float32
    )
    dscore = (probs * (dprob - delta[..., None])).astype(jnp.bfloat16)
    table_part = jnp.einsum("gqkb,ghqk->bh", onehot, dscore, preferred_element_type=jnp.float32)
    return (probs.astype(jnp.bfloat16), dscore, table_part)


def self_forward(query_heads, key_heads, value_heads, positions, segments, key_pos, key_seg, table):
    groups, local_rows, head_count, head_size = query_heads.shape
    key_count = key_heads.shape[1]
    stride = math.gcd(1024, key_count)

    def scores_at(block_index):
        offset = block_index * stride
        block_keys = lax.dynamic_slice_in_dim(key_heads, offset, stride, 1)
        block_pos = lax.dynamic_slice_in_dim(key_pos, offset, stride, 1)
        block_seg = lax.dynamic_slice_in_dim(key_seg, offset, stride, 1)
        scores, onehot = pair_terms(
            query_heads, block_keys, positions, segments, block_pos, block_seg, table
        )
        return (scores, offset)

    def running(block_index, carried):
        running_max, running_sum = carried
        scores, offset = scores_at(block_index)
        fresh_max = jnp.maximum(running_max, jnp.max(scores, axis=-1))
        running_sum = running_sum * jnp.exp(running_max - fresh_max) + jnp.sum(
            jnp.exp(scores - fresh_max[..., None]), axis=-1
        )
        return (fresh_max, running_sum)

    start_max = jnp.full((groups, head_count, local_rows), masked_value, jnp.float32)
    running_max, running_sum = lax.fori_loop(
        0, key_count // stride, running, (start_max, jnp.zeros_like(start_max))
    )
    log_total = running_max + jnp.log(running_sum)

    def weighted(block_index, accumulated):
        scores, offset = scores_at(block_index)
        block_values = lax.dynamic_slice_in_dim(value_heads, offset, stride, 1)
        weights_low = jnp.exp(scores - log_total[..., None]).astype(jnp.bfloat16)
        return accumulated + jnp.einsum(
            "ghqk,gkhd->gqhd", weights_low, block_values, preferred_element_type=jnp.float32
        )

    attended = lax.fori_loop(
        0, key_count // stride, weighted, jnp.zeros(query_heads.shape, jnp.float32)
    )
    return (attended, log_total)


def keys_backward(
    query_heads,
    dout_heads,
    log_total,
    delta,
    key_heads,
    value_heads,
    positions,
    segments,
    key_pos,
    key_seg,
    table,
):
    key_count = key_heads.shape[1]
    stride = math.gcd(1024, key_count)

    def turn(block_index, carried):
        query_acc, key_acc, value_acc, table_acc = carried
        offset = block_index * stride
        block_keys = lax.dynamic_slice_in_dim(key_heads, offset, stride, 1)
        block_values = lax.dynamic_slice_in_dim(value_heads, offset, stride, 1)
        block_pos = lax.dynamic_slice_in_dim(key_pos, offset, stride, 1)
        block_seg = lax.dynamic_slice_in_dim(key_seg, offset, stride, 1)
        scores, onehot = pair_terms(
            query_heads, block_keys, positions, segments, block_pos, block_seg, table
        )
        weights_low, dscore, table_part = block_grads(
            scores, onehot, log_total, delta, dout_heads, block_values
        )
        query_acc = query_acc + jnp.einsum(
            "ghqk,gkhd->gqhd", dscore, block_keys, preferred_element_type=jnp.float32
        )
        key_part = jnp.einsum(
            "ghqk,gqhd->gkhd", dscore, query_heads, preferred_element_type=jnp.float32
        )
        value_part = jnp.einsum(
            "ghqk,gqhd->gkhd", weights_low, dout_heads, preferred_element_type=jnp.float32
        )
        key_acc = lax.dynamic_update_slice_in_dim(key_acc, key_part, offset, 1)
        value_acc = lax.dynamic_update_slice_in_dim(value_acc, value_part, offset, 1)
        return (query_acc, key_acc, value_acc, table_acc + table_part)

    start = (
        jnp.zeros(query_heads.shape, jnp.float32),
        jnp.zeros(key_heads.shape, jnp.float32),
        jnp.zeros(value_heads.shape, jnp.float32),
        jnp.zeros((BUCKETS, query_heads.shape[2]), jnp.float32),
    )
    return lax.fori_loop(0, key_count // stride, turn, start)


def on_device(
    states,
    positions,
    segments,
    encoded,
    cotangent,
    self_gain,
    self_query,
    self_key,
    self_value,
    self_output,
    bias_table,
    cross_gain,
    cross_query,
    cross_key,
    cross_value,
    cross_output,
    feed_gain,
    gate_weight,
    up_weight,
    down_weight,
):
    (
        self_gain_full,
        self_query_full,
        self_key_full,
        self_value_full,
        self_output_full,
        table_full,
        cross_gain_full,
        cross_query_full,
        cross_key_full,
        cross_value_full,
        cross_output_full,
        feed_gain_full,
        gate_full,
        up_full,
        down_full,
    ) = (
        lax.all_gather(self_gain, "fsdp", axis=0, tiled=True),
        lax.all_gather(self_query, "fsdp", axis=0, tiled=True),
        lax.all_gather(self_key, "fsdp", axis=0, tiled=True),
        lax.all_gather(self_value, "fsdp", axis=0, tiled=True),
        lax.all_gather(self_output, "fsdp", axis=0, tiled=True),
        lax.all_gather(bias_table, "fsdp", axis=0, tiled=True),
        lax.all_gather(cross_gain, "fsdp", axis=0, tiled=True),
        lax.all_gather(cross_query, "fsdp", axis=0, tiled=True),
        lax.all_gather(cross_key, "fsdp", axis=0, tiled=True),
        lax.all_gather(cross_value, "fsdp", axis=0, tiled=True),
        lax.all_gather(cross_output, "fsdp", axis=0, tiled=True),
        lax.all_gather(feed_gain, "fsdp", axis=0, tiled=True),
        lax.all_gather(gate_weight, "fsdp", axis=0, tiled=True),
        lax.all_gather(up_weight, "fsdp", axis=0, tiled=True),
        lax.all_gather(down_weight, "fsdp", axis=0, tiled=True),
    )
    groups, local_rows, model_width = states.shape
    head_count = table_full.shape[1]
    inner_width = self_query_full.shape[1]
    head_size = inner_width // head_count

    def heads_of(value):
        return value.reshape(value.shape[0], value.shape[1], head_count, head_size)

    key_pos, key_seg = (
        lax.all_gather(positions, "ctx", axis=1, tiled=True),
        lax.all_gather(segments, "ctx", axis=1, tiled=True),
    )
    inputs = states.astype(jnp.float32)
    first_norm, first_back = jax.vjp(norm_rows, inputs, self_gain_full.astype(jnp.float32))
    first_low = first_norm.astype(jnp.bfloat16)
    queries = project(first_low, self_query_full).astype(jnp.bfloat16)
    keys_local = project(first_low, self_key_full).astype(jnp.bfloat16)
    values_local = project(first_low, self_value_full).astype(jnp.bfloat16)
    key_whole, value_whole = (
        lax.all_gather(keys_local, "ctx", axis=1, tiled=True),
        lax.all_gather(values_local, "ctx", axis=1, tiled=True),
    )
    attended, log_total = self_forward(
        heads_of(queries),
        heads_of(key_whole),
        heads_of(value_whole),
        positions,
        segments,
        key_pos,
        key_seg,
        table_full,
    )
    attended_low = attended.reshape(groups, local_rows, inner_width).astype(jnp.bfloat16)
    after_self = inputs + project(attended_low, self_output_full)
    second_norm, second_back = jax.vjp(norm_rows, after_self, cross_gain_full.astype(jnp.float32))
    second_low = second_norm.astype(jnp.bfloat16)
    cross_queries = project(second_low, cross_query_full).astype(jnp.bfloat16)
    cross_keys, cross_values = (
        lax.all_gather(
            project(encoded, cross_key_full).astype(jnp.bfloat16), "ctx", axis=1, tiled=True
        ),
        lax.all_gather(
            project(encoded, cross_value_full).astype(jnp.bfloat16), "ctx", axis=1, tiled=True
        ),
    )
    cross_scores = jnp.einsum(
        "gqhd,gkhd->ghqk",
        heads_of(cross_queries),
        heads_of(cross_keys),
        preferred_element_type=jnp.float32,
    )
    expo = jnp.exp(cross_scores - jnp.max(cross_scores, axis=-1, keepdims=True))
    cross_probs = expo / jnp.sum(expo, axis=-1, keepdims=True)
    cross_probs_low = cross_probs.astype(jnp.bfloat16)
    cross_attended = jnp.einsum(
        "ghqk,gkhd->gqhd",
        cross_probs_low,
        heads_of(cross_values),
        preferred_element_type=jnp.float32,
    )
    cross_low = cross_attended.reshape(groups, local_rows, inner_width).astype(jnp.bfloat16)
    after_cross = after_self + project(cross_low, cross_output_full)
    third_norm, third_back = jax.vjp(norm_rows, after_cross, feed_gain_full.astype(jnp.float32))
    third_low = third_norm.astype(jnp.bfloat16)
    gate = project(third_low, gate_full)
    up_part = project(third_low, up_full)
    hidden, hidden_back = jax.vjp(geglu, gate, up_part)
    hidden_low = hidden.astype(jnp.bfloat16)
    result = after_cross + project(hidden_low, down_full)
    layer_out = result.astype(jnp.bfloat16)
    grad_down = weight_grad(hidden_low, cotangent)
    grad_gate, grad_up = hidden_back(project_back(cotangent, down_full))
    gate_low = grad_gate.astype(jnp.bfloat16)
    up_low = grad_up.astype(jnp.bfloat16)
    grad_gate_weight = weight_grad(third_low, gate_low)
    grad_up_weight = weight_grad(third_low, up_low)
    third_in, grad_feed_gain = third_back(
        project_back(gate_low, gate_full) + project_back(up_low, up_full)
    )
    carry_two = cotangent.astype(jnp.float32) + third_in
    branch_two = carry_two.astype(jnp.bfloat16)
    grad_cross_output = weight_grad(cross_low, branch_two)
    cross_dout = heads_of(project_back(branch_two, cross_output_full).astype(jnp.bfloat16))
    cross_delta = jnp.swapaxes(
        jnp.sum(cross_dout.astype(jnp.float32) * cross_attended, axis=-1), 1, 2
    )
    cross_dprob = jnp.einsum(
        "gqhd,gkhd->ghqk", cross_dout, heads_of(cross_values), preferred_element_type=jnp.float32
    )
    cross_dscore = (cross_probs * (cross_dprob - cross_delta[..., None])).astype(jnp.bfloat16)
    cross_query_low = (
        jnp.einsum(
            "ghqk,gkhd->gqhd",
            cross_dscore,
            heads_of(cross_keys),
            preferred_element_type=jnp.float32,
        )
        .reshape(groups, local_rows, inner_width)
        .astype(jnp.bfloat16)
    )
    key_terms = jnp.einsum(
        "ghqk,gqhd->gkhd", cross_dscore, heads_of(cross_queries), preferred_element_type=jnp.float32
    )
    value_terms = jnp.einsum(
        "ghqk,gqhd->gkhd", cross_probs_low, cross_dout, preferred_element_type=jnp.float32
    )
    encoder_count = key_terms.shape[1]
    key_share, value_share = (
        lax.psum_scatter(
            key_terms.reshape(groups, encoder_count, inner_width).astype(jnp.bfloat16),
            "ctx",
            scatter_dimension=1,
            tiled=True,
        ).astype(jnp.float32),
        lax.psum_scatter(
            value_terms.reshape(groups, encoder_count, inner_width).astype(jnp.bfloat16),
            "ctx",
            scatter_dimension=1,
            tiled=True,
        ).astype(jnp.float32),
    )
    key_share_low = key_share.astype(jnp.bfloat16)
    value_share_low = value_share.astype(jnp.bfloat16)
    grad_cross_key = weight_grad(encoded, key_share_low)
    grad_cross_value = weight_grad(encoded, value_share_low)
    encoded_grad = project_back(key_share_low, cross_key_full) + project_back(
        value_share_low, cross_value_full
    )
    grad_cross_query = weight_grad(second_low, cross_query_low)
    second_in, grad_cross_gain = second_back(project_back(cross_query_low, cross_query_full))
    carry_one = carry_two + second_in
    branch_one = carry_one.astype(jnp.bfloat16)
    grad_self_output = weight_grad(attended_low, branch_one)
    self_dout_flat = project_back(branch_one, self_output_full).astype(jnp.bfloat16)
    self_dout = heads_of(self_dout_flat)
    self_delta = jnp.swapaxes(jnp.sum(self_dout.astype(jnp.float32) * attended, axis=-1), 1, 2)
    query_grad, key_terms_all, value_terms_all, grad_table = keys_backward(
        heads_of(queries),
        self_dout,
        log_total,
        self_delta,
        heads_of(key_whole),
        heads_of(value_whole),
        positions,
        segments,
        key_pos,
        key_seg,
        table_full,
    )
    total_keys = key_terms_all.shape[1]
    key_grad, value_grad = (
        lax.psum_scatter(
            key_terms_all.reshape(groups, total_keys, inner_width).astype(jnp.bfloat16),
            "ctx",
            scatter_dimension=1,
            tiled=True,
        ).astype(jnp.float32),
        lax.psum_scatter(
            value_terms_all.reshape(groups, total_keys, inner_width).astype(jnp.bfloat16),
            "ctx",
            scatter_dimension=1,
            tiled=True,
        ).astype(jnp.float32),
    )
    query_grad = query_grad.reshape(groups, local_rows, inner_width)
    query_low = query_grad.astype(jnp.bfloat16)
    key_low = key_grad.astype(jnp.bfloat16)
    value_low = value_grad.astype(jnp.bfloat16)
    grad_self_query = weight_grad(first_low, query_low)
    grad_self_key = weight_grad(first_low, key_low)
    grad_self_value = weight_grad(first_low, value_low)
    first_in, grad_self_gain = first_back(
        project_back(query_low, self_query_full)
        + project_back(key_low, self_key_full)
        + project_back(value_low, self_value_full)
    )
    states_grad = carry_one + first_in
    full_grads = (
        grad_self_gain,
        grad_self_query,
        grad_self_key,
        grad_self_value,
        grad_self_output,
        grad_table,
        grad_cross_gain,
        grad_cross_query,
        grad_cross_key,
        grad_cross_value,
        grad_cross_output,
        grad_feed_gain,
        grad_gate_weight,
        grad_up_weight,
        grad_down,
    )
    shares = (
        lax.psum_scatter(
            full_grads[0].astype(jnp.bfloat16), "fsdp", scatter_dimension=0, tiled=True
        ).astype(jnp.float32),
        lax.psum_scatter(
            full_grads[1].astype(jnp.bfloat16), "fsdp", scatter_dimension=0, tiled=True
        ).astype(jnp.float32),
        lax.psum_scatter(
            full_grads[2].astype(jnp.bfloat16), "fsdp", scatter_dimension=0, tiled=True
        ).astype(jnp.float32),
        lax.psum_scatter(
            full_grads[3].astype(jnp.bfloat16), "fsdp", scatter_dimension=0, tiled=True
        ).astype(jnp.float32),
        lax.psum_scatter(
            full_grads[4].astype(jnp.bfloat16), "fsdp", scatter_dimension=0, tiled=True
        ).astype(jnp.float32),
        lax.psum_scatter(
            full_grads[5].astype(jnp.bfloat16), "fsdp", scatter_dimension=0, tiled=True
        ).astype(jnp.float32),
        lax.psum_scatter(
            full_grads[6].astype(jnp.bfloat16), "fsdp", scatter_dimension=0, tiled=True
        ).astype(jnp.float32),
        lax.psum_scatter(
            full_grads[7].astype(jnp.bfloat16), "fsdp", scatter_dimension=0, tiled=True
        ).astype(jnp.float32),
        lax.psum_scatter(
            full_grads[8].astype(jnp.bfloat16), "fsdp", scatter_dimension=0, tiled=True
        ).astype(jnp.float32),
        lax.psum_scatter(
            full_grads[9].astype(jnp.bfloat16), "fsdp", scatter_dimension=0, tiled=True
        ).astype(jnp.float32),
        lax.psum_scatter(
            full_grads[10].astype(jnp.bfloat16), "fsdp", scatter_dimension=0, tiled=True
        ).astype(jnp.float32),
        lax.psum_scatter(
            full_grads[11].astype(jnp.bfloat16), "fsdp", scatter_dimension=0, tiled=True
        ).astype(jnp.float32),
        lax.psum_scatter(
            full_grads[12].astype(jnp.bfloat16), "fsdp", scatter_dimension=0, tiled=True
        ).astype(jnp.float32),
        lax.psum_scatter(
            full_grads[13].astype(jnp.bfloat16), "fsdp", scatter_dimension=0, tiled=True
        ).astype(jnp.float32),
        lax.psum_scatter(
            full_grads[14].astype(jnp.bfloat16), "fsdp", scatter_dimension=0, tiled=True
        ).astype(jnp.float32),
    )
    totals = (
        lax.psum(shares[0].astype(jnp.bfloat16), "ctx").astype(jnp.float32),
        lax.psum(shares[1].astype(jnp.bfloat16), "ctx").astype(jnp.float32),
        lax.psum(shares[2].astype(jnp.bfloat16), "ctx").astype(jnp.float32),
        lax.psum(shares[3].astype(jnp.bfloat16), "ctx").astype(jnp.float32),
        lax.psum(shares[4].astype(jnp.bfloat16), "ctx").astype(jnp.float32),
        lax.psum(shares[5].astype(jnp.bfloat16), "ctx").astype(jnp.float32),
        lax.psum(shares[6].astype(jnp.bfloat16), "ctx").astype(jnp.float32),
        lax.psum(shares[7].astype(jnp.bfloat16), "ctx").astype(jnp.float32),
        lax.psum(shares[8].astype(jnp.bfloat16), "ctx").astype(jnp.float32),
        lax.psum(shares[9].astype(jnp.bfloat16), "ctx").astype(jnp.float32),
        lax.psum(shares[10].astype(jnp.bfloat16), "ctx").astype(jnp.float32),
        lax.psum(shares[11].astype(jnp.bfloat16), "ctx").astype(jnp.float32),
        lax.psum(shares[12].astype(jnp.bfloat16), "ctx").astype(jnp.float32),
        lax.psum(shares[13].astype(jnp.bfloat16), "ctx").astype(jnp.float32),
        lax.psum(shares[14].astype(jnp.bfloat16), "ctx").astype(jnp.float32),
    )
    return (layer_out, states_grad, encoded_grad) + tuple(totals)


def solution(mesh):
    return jax.shard_map(
        on_device,
        mesh=mesh,
        in_specs=(
            P("fsdp", "ctx", None),
            P("fsdp", "ctx"),
            P("fsdp", "ctx"),
            P("fsdp", "ctx", None),
            P("fsdp", "ctx", None),
            P("fsdp"),
            P("fsdp", None),
            P("fsdp", None),
            P("fsdp", None),
            P("fsdp", None),
            P("fsdp", None),
            P("fsdp"),
            P("fsdp", None),
            P("fsdp", None),
            P("fsdp", None),
            P("fsdp", None),
            P("fsdp"),
            P("fsdp", None),
            P("fsdp", None),
            P("fsdp", None),
        ),
        out_specs=(
            P("fsdp", "ctx", None),
            P("fsdp", "ctx", None),
            P("fsdp", "ctx", None),
            P("fsdp"),
            P("fsdp", None),
            P("fsdp", None),
            P("fsdp", None),
            P("fsdp", None),
            P("fsdp", None),
            P("fsdp"),
            P("fsdp", None),
            P("fsdp", None),
            P("fsdp", None),
            P("fsdp", None),
            P("fsdp"),
            P("fsdp", None),
            P("fsdp", None),
            P("fsdp", None),
        ),
        check_vma=False,
    )
```

profile of v0, /device:TPU:0, one launch (start us, length us, event | category | flops | bytes accessed | tf_op | source)
XLA Modules:
  0.0 2729.6 jit_solution(12277255297981142517)
XLA Ops:
  10.7 47.6 %all-gather.31.cloned.1.call-done = bf16[1024,1024]{1,0:T(8,128)(2,1)} async-done(((bf16[256,1024]{1,0:T(8,128)(2,1)}), bf16[1024,1024]{1,0:T(8,128)(2,1)}) %all-gather.31.cloned.1.call-update) | async-done | bytes 2097168 | tf_op jit(solution)/shard_map/all_gather | solution.py:221
  61.1 43.4 %all-gather.35.cloned.1.call-done = bf16[1024,1024]{1,0:T(8,128)(2,1)} async-done(((bf16[256,1024]{1,0:T(8,128)(2,1)}), bf16[1024,1024]{1,0:T(8,128)(2,1)}) %all-gather.35.cloned.1.call-update) | async-done | bytes 2097168 | tf_op jit(solution)/shard_map/all_gather | solution.py:220
  116.4 34.4 %all-gather.25.cloned.1.call-done = bf16[1024,1024]{1,0:T(8,128)(2,1)} async-done(((bf16[256,1024]{1,0:T(8,128)(2,1)}), bf16[1024,1024]{1,0:T(8,128)(2,1)}) %all-gather.25.cloned.1.call-update) | async-done | bytes 2097168 | tf_op jit(solution)/shard_map/all_gather | solution.py:214
  154.7 42.2 %all-gather.23.cloned.1.call-done = bf16[1024,1024]{1,0:T(8,128)(2,1)} async-done(((bf16[256,1024]{1,0:T(8,128)(2,1)}), bf16[1024,1024]{1,0:T(8,128)(2,1)}) %all-gather.23.cloned.1.call-update) | async-done | bytes 2097168 | tf_op jit(solution)/shard_map/all_gather | solution.py:215
  270.1 23.7 all-gather.51.cloned.1.call-done
  296.1 54.6 %all-gather.47.cloned.1.call-done = bf16[4096,1024]{1,0:T(8,128)(2,1)} async-done(((bf16[512,1024]{1,0:T(8,128)(2,1)}), bf16[4096,1024]{1,0:T(8,128)(2,1)}) %all-gather.47.cloned.1.call-update) | async-done | bytes 8388624 | tf_op jit(solution)/shard_map/all_gather | solution.py:247
  362.1 373.3 %while.50 = (s32[]{:T(128)}, f32[1,16,512]{2,1,0:T(8,128)S(1)}, f32[1,16,512]{2,1,0:T(8,128)S(1)}, s32[1,4096]{1,0:T(1,128)S(1)}, s32[1,512]{1,0:T(1,128)S(1)}, ...) while((s32[]{:T(128)}, f32[1,16,512]{2,1,0:T(8,128)S(1)}, ...), condition=%wide.region_4.5_spmd.clone, body=%wide.region_1.4_spmd.clone.sunk | while | flops 1696637952 | bytes 214377680 | solution.py:103
  385.7 34.0 %copy.193 = f32[512,1024,16]{0,1,2:T(8,128)} copy(f32[512,1024,16]{1,2,0:T(8,128)} %fusion.318) | data formatting | bytes 67108864 | tf_op jit(solution)/shard_map/while/body/eval_jaxpr/gqkb,bh->ghqk/dot_general | solution.py:60
  419.7 22.4 fusion.319
  479.0 34.2 %copy.193 = f32[512,1024,16]{0,1,2:T(8,128)} copy(f32[512,1024,16]{1,2,0:T(8,128)} %fusion.318) | data formatting | bytes 67108864 | tf_op jit(solution)/shard_map/while/body/eval_jaxpr/gqkb,bh->ghqk/dot_general | solution.py:60
  513.1 22.4 fusion.319
  572.5 34.0 %copy.193 = f32[512,1024,16]{0,1,2:T(8,128)} copy(f32[512,1024,16]{1,2,0:T(8,128)} %fusion.318) | data formatting | bytes 67108864 | tf_op jit(solution)/shard_map/while/body/eval_jaxpr/gqkb,bh->ghqk/dot_general | solution.py:60
  606.5 22.4 fusion.319
  665.9 34.0 %copy.193 = f32[512,1024,16]{0,1,2:T(8,128)} copy(f32[512,1024,16]{1,2,0:T(8,128)} %fusion.318) | data formatting | bytes 67108864 | tf_op jit(solution)/shard_map/while/body/eval_jaxpr/gqkb,bh->ghqk/dot_general | solution.py:60
  699.9 22.4 fusion.319
  747.5 305.2 %while.51 = (s32[]{:T(128)}, f32[1,512,16,64]{1,3,2,0:T(8,128)}, bf16[1,4096,16,64]{1,3,2,0:T(8,128)(2,1)}, s32[1,4096]{1,0:T(1,128)S(1)}, s32[1,512]{1,0:T(1,12...) while((s32[]{:T(128)}, f32[1,512,16,64]{1,3,2,0:T(8,128)}, ...), condition=%wide.region_6.7_spmd.clone, body=%wide.region_5.6_spmd.clone.sunk | while | flops 2762998784 | bytes 169945872 | solution.py:116
  755.3 16.4 fusion.326
  771.7 34.2 %copy.195 = f32[512,1024,16]{0,1,2:T(8,128)} copy(f32[512,1024,16]{1,2,0:T(8,128)} %fusion.326) | data formatting | bytes 67108864 | tf_op jit(solution)/shard_map/while/body/eval_jaxpr/gqkb,bh->ghqk/dot_general | solution.py:60
  805.9 17.2 bitcast_add_fusion.12
  848.0 34.0 %copy.195 = f32[512,1024,16]{0,1,2:T(8,128)} copy(f32[512,1024,16]{1,2,0:T(8,128)} %fusion.326) | data formatting | bytes 67108864 | tf_op jit(solution)/shard_map/while/body/eval_jaxpr/gqkb,bh->ghqk/dot_general | solution.py:60
  882.0 17.0 bitcast_add_fusion.12
  923.9 34.0 %copy.195 = f32[512,1024,16]{0,1,2:T(8,128)} copy(f32[512,1024,16]{1,2,0:T(8,128)} %fusion.326) | data formatting | bytes 67108864 | tf_op jit(solution)/shard_map/while/body/eval_jaxpr/gqkb,bh->ghqk/dot_general | solution.py:60
  958.0 17.0 bitcast_add_fusion.12
  999.9 34.0 %copy.195 = f32[512,1024,16]{0,1,2:T(8,128)} copy(f32[512,1024,16]{1,2,0:T(8,128)} %fusion.326) | data formatting | bytes 67108864 | tf_op jit(solution)/shard_map/while/body/eval_jaxpr/gqkb,bh->ghqk/dot_general | solution.py:60
  1033.9 17.0 bitcast_add_fusion.12
  1206.5 532.4 %while.52 = (s32[]{:T(128)}, f32[1,512,16,64]{1,3,2,0:T(8,128)}, bf16[1,4096,16,64]{1,3,2,0:T(8,128)(2,1)}, bf16[1,4096,16,64]{1,3,2,0:T(8,128)(2,1)}, f32[32,16...) while((s32[]{:T(128)}, f32[1,512,16,64]{1,3,2,0:T(8,128)}, ...), condition=%wide.region_16.17_spmd.clone, body=%wide.region_15.16_spmd.clone.sunk | while | flops 6563039232 | bytes 273790240 | solution.py:170
  1245.4 37.3 %fusion.341 = f32[16,512,1024]{1,2,0:T(8,128)} fusion(f32[512,1024,16]{0,2,1:T(8,128)} %fusion.340, f32[16,512]{1,0:T(8,128)S(1)} %bitcast.446, pred[512,1024]{0,1:T(8,128)(4,1)S(1)} %compare_and_fusion.8, bf16[1,4096,16,64]{1,3,2,0:T(8,128)(2,1)} %get-tuple-element.1449, s32[]{:T(128)S(6)} %select_n.87, ...), kind=kOutput, calls=%fused_computation.114.clone.1 | convolution fusion | flops 1098907648 | bytes 70811648 | tf_op jit(solution)/shard_map/while/body/eval_jaxpr/gqhd,gkhd->ghqk/dot_general | solution.py:55
  1310.6 26.9 fusion.343
  1371.5 37.2 %fusion.341 = f32[16,512,1024]{1,2,0:T(8,128)} fusion(f32[512,1024,16]{0,2,1:T(8,128)} %fusion.340, f32[16,512]{1,0:T(8,128)S(1)} %bitcast.446, pred[512,1024]{0,1:T(8,128)(4,1)S(1)} %compare_and_fusion.8, bf16[1,4096,16,64]{1,3,2,0:T(8,128)(2,1)} %get-tuple-element.1449, s32[]{:T(128)S(6)} %select_n.87, ...), kind=kOutput, calls=%fused_computation.114.clone.1 | convolution fusion | flops 1098907648 | bytes 70811648 | tf_op jit(solution)/shard_map/while/body/eval_jaxpr/gqhd,gkhd->ghqk/dot_general | solution.py:55
  1436.7 26.9 fusion.343
  1498.2 37.2 %fusion.341 = f32[16,512,1024]{1,2,0:T(8,128)} fusion(f32[512,1024,16]{0,2,1:T(8,128)} %fusion.340, f32[16,512]{1,0:T(8,128)S(1)} %bitcast.446, pred[512,1024]{0,1:T(8,128)(4,1)S(1)} %compare_and_fusion.8, bf16[1,4096,16,64]{1,3,2,0:T(8,128)(2,1)} %get-tuple-element.1449, s32[]{:T(128)S(6)} %select_n.87, ...), kind=kOutput, calls=%fused_computation.114.clone.1 | convolution fusion | flops 1098907648 | bytes 70811648 | tf_op jit(solution)/shard_map/while/body/eval_jaxpr/gqhd,gkhd->ghqk/dot_general | solution.py:55
  1563.5 26.9 fusion.343
  1625.1 37.2 %fusion.341 = f32[16,512,1024]{1,2,0:T(8,128)} fusion(f32[512,1024,16]{0,2,1:T(8,128)} %fusion.340, f32[16,512]{1,0:T(8,128)S(1)} %bitcast.446, pred[512,1024]{0,1:T(8,128)(4,1)S(1)} %compare_and_fusion.8, bf16[1,4096,16,64]{1,3,2,0:T(8,128)(2,1)} %get-tuple-element.1449, s32[]{:T(128)S(6)} %select_n.87, ...), kind=kOutput, calls=%fused_computation.114.clone.1 | convolution fusion | flops 1098907648 | bytes 70811648 | tf_op jit(solution)/shard_map/while/body/eval_jaxpr/gqhd,gkhd->ghqk/dot_general | solution.py:55
  1690.3 26.9 fusion.343
  1815.3 71.1 %reduce-scatter.22.cloned.1.call-done = bf16[1,512,1024]{1,2,0:T(8,128)(2,1)} async-done(((bf16[1,4096,1024]{1,2,0:T(8,128)(2,1)}), bf16[1,512,1024]{1,2,0:T(8,128)(2,1)}) %reduce-scatter.22.cloned.1.call-update) | async-done | bytes 1048592 | tf_op jit(solution)/shard_map/reduce_scatter | solution.py:385
  1890.7 41.7 %reduce-scatter.38.cloned.1.call-done = bf16[256,1024]{1,0:T(8,128)(2,1)} async-done(((bf16[1024,1024]{1,0:T(8,128)(2,1)}), bf16[256,1024]{1,0:T(8,128)(2,1)}) %reduce-scatter.38.cloned.1.call-update) | async-done | bytes 524304 | tf_op jit(solution)/shard_map/reduce_scatter | solution.py:453
  1932.4 45.6 %reduce-scatter.32.cloned.1.call-done = bf16[256,1024]{1,0:T(8,128)(2,1)} async-done(((bf16[1024,1024]{1,0:T(8,128)(2,1)}), bf16[256,1024]{1,0:T(8,128)(2,1)}) %reduce-scatter.32.cloned.1.call-update) | async-done | bytes 524304 | tf_op jit(solution)/shard_map/reduce_scatter | solution.py:444
  1978.0 45.5 %reduce-scatter.30.cloned.1.call-done = bf16[256,1024]{1,0:T(8,128)(2,1)} async-done(((bf16[1024,1024]{1,0:T(8,128)(2,1)}), bf16[256,1024]{1,0:T(8,128)(2,1)}) %reduce-scatter.30.cloned.1.call-update) | async-done | bytes 524304 | tf_op jit(solution)/shard_map/reduce_scatter | solution.py:435
  2023.6 45.6 %reduce-scatter.24.cloned.1.call-done = bf16[256,1024]{1,0:T(8,128)(2,1)} async-done(((bf16[1024,1024]{1,0:T(8,128)(2,1)}), bf16[256,1024]{1,0:T(8,128)(2,1)}) %reduce-scatter.24.cloned.1.call-update) | async-done | bytes 524304 | tf_op jit(solution)/shard_map/reduce_scatter | solution.py:426
  2069.2 45.4 %reduce-scatter.36.cloned.1.call-done = bf16[256,1024]{0,1:T(8,128)(2,1)} async-done(((bf16[1024,1024]{0,1:T(8,128)(2,1)}), bf16[256,1024]{0,1:T(8,128)(2,1)}) %reduce-scatter.36.cloned.1.call-update) | async-done | bytes 524304 | tf_op jit(solution)/shard_map/reduce_scatter | solution.py:450
  2114.6 46.2 %reduce-scatter.34.cloned.1.call-done = bf16[256,1024]{0,1:T(8,128)(2,1)} async-done(((bf16[1024,1024]{0,1:T(8,128)(2,1)}), bf16[256,1024]{0,1:T(8,128)(2,1)}) %reduce-scatter.34.cloned.1.call-update) | async-done | bytes 524304 | tf_op jit(solution)/shard_map/reduce_scatter | solution.py:447
  2160.7 103.8 %reduce-scatter.44.cloned.1.call-done = bf16[704,1024]{1,0:T(8,128)(2,1)} async-done(((bf16[2816,1024]{1,0:T(8,128)(2,1)}), bf16[704,1024]{1,0:T(8,128)(2,1)}) %reduce-scatter.44.cloned.1.call-update) | async-done | bytes 1441808 | tf_op jit(solution)/shard_map/reduce_scatter | solution.py:465
  2264.5 104.9 %reduce-scatter.42.cloned.1.call-done = bf16[256,2816]{1,0:T(8,128)(2,1)} async-done(((bf16[1024,2816]{1,0:T(8,128)(2,1)}), bf16[256,2816]{1,0:T(8,128)(2,1)}) %reduce-scatter.42.cloned.1.call-update) | async-done | bytes 1441808 | tf_op jit(solution)/shard_map/reduce_scatter | solution.py:462
  2369.5 105.1 %reduce-scatter.40.cloned.1.call-done = bf16[256,2816]{1,0:T(8,128)(2,1)} async-done(((bf16[1024,2816]{1,0:T(8,128)(2,1)}), bf16[256,2816]{1,0:T(8,128)(2,1)}) %reduce-scatter.40.cloned.1.call-update) | async-done | bytes 1441808 | tf_op jit(solution)/shard_map/reduce_scatter | solution.py:459
  2474.6 47.3 %reduce-scatter.26.cloned.1.call-done = bf16[256,1024]{1,0:T(8,128)(2,1)} async-done(((bf16[1024,1024]{1,0:T(8,128)(2,1)}), bf16[256,1024]{1,0:T(8,128)(2,1)}) %reduce-scatter.26.cloned.1.call-update) | async-done | bytes 524304 | tf_op jit(solution)/shard_map/reduce_scatter | solution.py:429
  2521.9 46.0 %reduce-scatter.28.cloned.1.call-done = bf16[256,1024]{1,0:T(8,128)(2,1)} async-done(((bf16[1024,1024]{1,0:T(8,128)(2,1)}), bf16[256,1024]{1,0:T(8,128)(2,1)}) %reduce-scatter.28.cloned.1.call-update) | async-done | bytes 524304 | tf_op jit(solution)/shard_map/reduce_scatter | solution.py:432
  2590.4 16.9 all-reduce.6
  2625.9 79.7 %all-reduce.9.cloned.1.call-done = (bf16[256,1024]{0,1:T(8,128)(2,1)}, bf16[256,1024]{0,1:T(8,128)(2,1)}, bf16[256,1024]{1,0:T(8,128)(2,1)}, bf16[256,1024]{1,0:...) async-done(((bf16[256,1024]{0,1:T(8,128)(2,1)}, ...) | async-done | bytes 8519696 | tf_op jit(solution)/shard_map/psum | solution.py:478
  (459 shorter events, 891.9 us)
Async XLA Ops:
  7.2 51.1 %copy-start = (bf16[1,64,1024]{2,1,0:T(8,128)(2,1)S(1)}, bf16[1,64,1024]{2,1,0:T(8,128)(2,1)}, u32[]{:S(2)}) copy-start(bf16[1,64,1024]{2,1,0:T(8,128)(2,1)} %param.29) | copy-start | bytes 393220
  7.2 51.1 %all-gather.31.cloned.1.call-start = ((), (), s32[]{:S(2)}) async-start(), calls=%async_computation.19 | async-start | bytes 2621440 | tf_op jit(solution)/shard_map/all_gather | solution.py:221
  7.9 96.6 %all-gather.35.cloned.1.call-start = ((), (), s32[]{:S(2)}) async-start(), calls=%async_computation.21 | async-start | bytes 2621440 | tf_op jit(solution)/shard_map/all_gather | solution.py:220
  8.7 142.1 %all-gather.25.cloned.1.call-start = ((), (), s32[]{:S(2)}) async-start(), calls=%async_computation.16 | async-start | bytes 2621440 | tf_op jit(solution)/shard_map/all_gather | solution.py:214
  9.4 187.5 %all-gather.23.cloned.1.call-start = ((), (), s32[]{:S(2)}) async-start(), calls=%async_computation.15 | async-start | bytes 2621440 | tf_op jit(solution)/shard_map/all_gather | solution.py:215
  10.0 243.9 %all-gather.27.cloned.1.call-start = ((), (), s32[]{:S(2)}) async-start(), calls=%async_computation.17 | async-start | bytes 2621440 | tf_op jit(solution)/shard_map/all_gather | solution.py:213
  10.6 96.8 %copy-start.70 = (bf16[256]{0:T(256)(128)(2,1)S(1)}, bf16[256]{0:T(256)(128)(2,1)}, u32[]{:S(2)}) copy-start(bf16[256]{0:T(256)(128)(2,1)} %param.31) | copy-start | bytes 1540
  10.6 105.5 %copy-start.4 = (bf16[1,512,1024]{2,1,0:T(8,128)(2,1)S(1)}, bf16[1,512,1024]{2,1,0:T(8,128)(2,1)}, u32[]{:S(2)}) copy-start(bf16[1,512,1024]{2,1,0:T(8,128)(2,1)} %param.26) | copy-start | bytes 3145732
  10.6 257.3 %all-gather.49.cloned.1.call-start = ((), (), s32[]{:S(2)}) async-start(), calls=%async_computation.41 | async-start | bytes 1179648 | tf_op jit(solution)/shard_map/all_gather | solution.py:269
  61.0 232.8 %all-gather.51.cloned.1.call-start = ((), (), s32[]{:S(2)}) async-start(), calls=%async_computation.42 | async-start | bytes 1179648 | tf_op jit(solution)/shard_map/all_gather | solution.py:266
  107.3 243.4 %all-gather.47.cloned.1.call-start = ((), (), s32[]{:S(2)}) async-start(), calls=%async_computation.40 | async-start | bytes 9437184 | tf_op jit(solution)/shard_map/all_gather | solution.py:247
  116.1 137.9 %copy-start.50 = (f32[4,1,256]{2,1,0:T(1,128)}, f32[4,1,256]{2,1,0:T(1,128)S(1)}, u32[]{:S(2)}) copy-start(f32[4,1,256]{2,1,0:T(1,128)S(1)} %convert_element_type.1076) | copy-start | bytes 12292
  116.4 38.3 %copy-start.55 = (f32[512]{0:T(512)}, f32[512]{0:T(512)S(1)}, u32[]{:S(2)}) copy-start(f32[512]{0:T(512)S(1)} %fusion.178) | copy-start | bytes 6148
  116.4 137.6 %copy-start.53 = (f32[512]{0:T(512)}, f32[512]{0:T(512)S(1)}, u32[]{:S(2)}) copy-start(f32[512]{0:T(512)S(1)} %fusion.217) | copy-start | bytes 6148
  154.7 580.9 %all-gather.45.cloned.1.call-start = ((), (), s32[]{:S(2)}) async-start(), calls=%async_computation.39 | async-start | bytes 9437184 | tf_op jit(solution)/shard_map/all_gather | solution.py:248
  200.8 853.7 %all-gather.29.cloned.1.call-start = ((), (), s32[]{:S(2)}) async-start(), calls=%async_computation.18 | async-start | bytes 2621440 | tf_op jit(solution)/shard_map/all_gather | solution.py:216
  201.4 857.8 %all-gather.33.cloned.1.call-start = ((), (), s32[]{:S(2)}) async-start(), calls=%async_computation.20 | async-start | bytes 2621440 | tf_op jit(solution)/shard_map/all_gather | solution.py:219
  202.1 884.2 %all-gather.37.cloned.1.call-start = ((), (), s32[]{:S(2)}) async-start(), calls=%async_computation.22 | async-start | bytes 2621440 | tf_op jit(solution)/shard_map/all_gather | solution.py:222
  202.7 21.4 copy-start.62
  202.7 33.5 %copy-start.36 = (s32[1,512]{1,0:T(1,128)S(1)}, s32[1,512]{1,0:T(1,128)}, u32[]{:S(2)}) copy-start(s32[1,512]{1,0:T(1,128)} %param.27) | copy-start | bytes 6148
  202.7 42.4 %copy-start.43 = (s32[1,512]{1,0:T(1,128)S(1)}, s32[1,512]{1,0:T(1,128)}, u32[]{:S(2)}) copy-start(s32[1,512]{1,0:T(1,128)} %param.28) | copy-start | bytes 6148
  202.8 890.1 %all-gather.41.cloned.1.call-start = ((), (), s32[]{:S(2)}) async-start(), calls=%async_computation.24 | async-start | bytes 7208960 | tf_op jit(solution)/shard_map/all_gather | solution.py:225
  203.5 898.0 %all-gather.39.cloned.1.call-start = ((), (), s32[]{:S(2)}) async-start(), calls=%async_computation.23 | async-start | bytes 7208960 | tf_op jit(solution)/shard_map/all_gather | solution.py:224
  204.1 906.1 %all-gather.43.cloned.1.call-start = ((), (), s32[]{:S(2)}) async-start(), calls=%async_computation.25 | async-start | bytes 7208960 | tf_op jit(solution)/shard_map/all_gather | solution.py:226
  204.7 1556.8 %reduce-scatter.48.cloned.1.call-start = ((), (), s32[]{:S(2)}) async-start(), calls=%async_computation.44 | async-start | bytes 1179648
  771.7 34.2 %copy-start.14 = (f32[1,512,16,64]{1,3,2,0:T(8,128)S(1)}, f32[1,512,16,64]{1,3,2,0:T(8,128)}, u32[]{:S(2)}) copy-start(f32[1,512,16,64]{1,3,2,0:T(8,128)} %get-tuple-element.1375) | copy-start | bytes 6291460 | tf_op jit(solution)/shard_map/while
  848.0 34.0 %copy-start.14 = (f32[1,512,16,64]{1,3,2,0:T(8,128)S(1)}, f32[1,512,16,64]{1,3,2,0:T(8,128)}, u32[]{:S(2)}) copy-start(f32[1,512,16,64]{1,3,2,0:T(8,128)} %get-tuple-element.1375) | copy-start | bytes 6291460 | tf_op jit(solution)/shard_map/while
  923.9 34.0 %copy-start.14 = (f32[1,512,16,64]{1,3,2,0:T(8,128)S(1)}, f32[1,512,16,64]{1,3,2,0:T(8,128)}, u32[]{:S(2)}) copy-start(f32[1,512,16,64]{1,3,2,0:T(8,128)} %get-tuple-element.1375) | copy-start | bytes 6291460 | tf_op jit(solution)/shard_map/while
  999.9 34.0 %copy-start.14 = (f32[1,512,16,64]{1,3,2,0:T(8,128)S(1)}, f32[1,512,16,64]{1,3,2,0:T(8,128)}, u32[]{:S(2)}) copy-start(f32[1,512,16,64]{1,3,2,0:T(8,128)} %get-tuple-element.1375) | copy-start | bytes 6291460 | tf_op jit(solution)/shard_map/while
  1059.1 118.5 %copy-start.59 = (f32[512]{0:T(512)}, f32[512]{0:T(512)S(1)}, u32[]{:S(2)}) copy-start(f32[512]{0:T(512)S(1)} %fusion.218) | copy-start | bytes 6148
  1159.7 606.8 %reduce-scatter.46.cloned.1.call-start = ((), (), s32[]{:S(2)}) async-start(), calls=%async_computation.43 | async-start | bytes 1179648
  1197.6 613.6 %reduce-scatter.20.cloned.1.call-start = ((), (), s32[]{:S(2)}) async-start(), calls=%async_computation.26 | async-start | bytes 9437184 | tf_op jit(solution)/shard_map/reduce_scatter | solution.py:379
  1482.3 15.9 copy-start.1
  1609.1 15.9 copy-start.1
  1738.9 147.5 %reduce-scatter.22.cloned.1.call-start = ((), (), s32[]{:S(2)}) async-start(), calls=%async_computation.27 | async-start | bytes 9437184 | tf_op jit(solution)/shard_map/reduce_scatter | solution.py:385
  1739.7 192.8 %reduce-scatter.38.cloned.1.call-start = ((), (), s32[]{:S(2)}) async-start(), calls=%async_computation.35 | async-start | bytes 2621440 | tf_op jit(solution)/shard_map/reduce_scatter | solution.py:453
  1744.5 233.5 %reduce-scatter.32.cloned.1.call-start = ((), (), s32[]{:S(2)}) async-start(), calls=%async_computation.32 | async-start | bytes 2621440 | tf_op jit(solution)/shard_map/reduce_scatter | solution.py:444
  1749.5 274.1 %reduce-scatter.30.cloned.1.call-start = ((), (), s32[]{:S(2)}) async-start(), calls=%async_computation.31 | async-start | bytes 2621440 | tf_op jit(solution)/shard_map/reduce_scatter | solution.py:435
  1755.6 313.6 %reduce-scatter.24.cloned.1.call-start = ((), (), s32[]{:S(2)}) async-start(), calls=%async_computation.28 | async-start | bytes 2621440 | tf_op jit(solution)/shard_map/reduce_scatter | solution.py:426
  1761.4 353.2 %reduce-scatter.36.cloned.1.call-start = ((), (), s32[]{:S(2)}) async-start(), calls=%async_computation.34 | async-start | bytes 2621440 | tf_op jit(solution)/shard_map/reduce_scatter | solution.py:450
  1766.4 394.3 %reduce-scatter.34.cloned.1.call-start = ((), (), s32[]{:S(2)}) async-start(), calls=%async_computation.33 | async-start | bytes 2621440 | tf_op jit(solution)/shard_map/reduce_scatter | solution.py:447
  1771.4 493.1 %reduce-scatter.44.cloned.1.call-start = ((), (), s32[]{:S(2)}) async-start(), calls=%async_computation.38 | async-start | bytes 7208960 | tf_op jit(solution)/shard_map/reduce_scatter | solution.py:465
  1779.3 590.1 %reduce-scatter.42.cloned.1.call-start = ((), (), s32[]{:S(2)}) async-start(), calls=%async_computation.37 | async-start | bytes 7208960 | tf_op jit(solution)/shard_map/reduce_scatter | solution.py:462
  1787.6 687.0 %reduce-scatter.40.cloned.1.call-start = ((), (), s32[]{:S(2)}) async-start(), calls=%async_computation.36 | async-start | bytes 7208960 | tf_op jit(solution)/shard_map/reduce_scatter | solution.py:459
  1795.5 726.4 %reduce-scatter.26.cloned.1.call-start = ((), (), s32[]{:S(2)}) async-start(), calls=%async_computation.29 | async-start | bytes 2621440 | tf_op jit(solution)/shard_map/reduce_scatter | solution.py:429
  1815.2 752.6 %reduce-scatter.28.cloned.1.call-start = ((), (), s32[]{:S(2)}) async-start(), calls=%async_computation.30 | async-start | bytes 2621440 | tf_op jit(solution)/shard_map/reduce_scatter | solution.py:432
  1890.4 815.2 %all-reduce.9.cloned.1.call-start = ((), (), s32[]{:S(2)}) async-start(), calls=%async_computation.45 | async-start | bytes 17039360 | tf_op jit(solution)/shard_map/psum | solution.py:478
  2587.3 34.8 %copy-start.56 = (f32[512]{0:T(512)S(1)}, f32[512]{0:T(512)}, u32[]{:S(2)}) copy-start(f32[512]{0:T(512)} %copy-done.55) | copy-start | bytes 6148
  (68 other events, 250.5 us)
Sparse Core Ops, SparseCore 0:
  9.6 48.6 all-gather.30
  59.8 44.6 all-gather.34
  106.1 44.6 all-gather.24
  152.2 44.6 all-gather.22
  198.3 44.8 all-gather.26
  245.6 22.2 all-gather.48
  270.3 23.4 all-gather.50
  296.3 54.3 all-gather.46
  353.2 54.3 all-gather.44
  409.0 45.9 all-gather.28
  456.6 44.6 all-gather.32
  502.7 44.6 all-gather.36
  549.0 105.4 all-gather.40
  655.9 104.9 all-gather.38
  762.3 104.9 all-gather.42
  1159.8 36.8 reduce-scatter.47
  1200.3 35.9 reduce-scatter.45
  1739.0 72.1 reduce-scatter.19
  1815.1 71.2 reduce-scatter.21
  1888.5 43.8 reduce-scatter.37
  1934.8 43.1 reduce-scatter.31
  1980.3 43.1 reduce-scatter.29
  2026.0 43.1 reduce-scatter.23
  2071.3 43.1 reduce-scatter.35
  2117.5 43.1 reduce-scatter.33
  2162.9 101.5 reduce-scatter.43
  2266.7 102.7 reduce-scatter.41
  2371.8 102.7 reduce-scatter.39
  2477.4 44.3 reduce-scatter.25
  2524.7 43.1 reduce-scatter.27
  2573.6 131.9 all-reduce.8
where the time goes:
time: 2740 us; the launch traced here: 2730 us
  waiting for transfers between devices  1110 us (41%)
  matrix products  952 us (35%)
  local copies, waits for them, and re-layouts  387 us (14%)
  other arithmetic  152 us (6%)
  blocking collectives  85.7 us (3%)
    dot_general x8, local copies, waits for them, and re-layouts, pair_terms(): jnp.einsum('gqkb,bh->ghqk', onehot, table, preferred_element_type=jnp.flo...  272 us
    dot_general x8, matrix products, pair_terms(): jnp.einsum('gqhd,gkhd->ghqk', query_heads, key_heads, preferred_element_t...  238 us
    dot_general x12, matrix products, pair_terms(): jnp.einsum('gqkb,bh->ghqk', onehot, table, preferred_element_type=jnp.flo...  193 us
    dot_general x4, matrix products, block_grads(): jnp.einsum('gqkb,ghqk->bh', onehot, dscore, preferred_element_type=jnp.fl...  108 us
    reduce_scatter x1, waiting for transfers between devices, on_device(): lax.psum_scatter(full_grads[12].astype(jnp.bfloat16), 'fsdp', scatter_dim...  105 us
    reduce_scatter x1, waiting for transfers between devices, on_device(): lax.psum_scatter(full_grads[13].astype(jnp.bfloat16), 'fsdp', scatter_dim...  105 us
    reduce_scatter x1, waiting for transfers between devices, on_device(): lax.psum_scatter(full_grads[14].astype(jnp.bfloat16), 'fsdp', scatter_dim...  104 us
    psum x1, waiting for transfers between devices, on_device(): lax.psum(shares[8].astype(jnp.bfloat16), 'ctx').astype(jnp.float32)  79.7 us
  transfers between devices with their start and end apart: 31, of which 21 were waited for; matrix products, arithmetic and copies ran while one was open for 51% of the time, Pallas kernels for 0%

commit v1 on v0

v1 whole, which is shorter than its diff:
```python
import functools
import math

import jax
import jax.numpy as jnp
from jax import lax
from jax.experimental import pallas as pl
from jax.experimental.pallas import tpu as pltpu
from jax.sharding import Mesh
from jax.sharding import PartitionSpec as P

BUCKETS = 32
DISTANCE = 128
PROMPT = 2048
CLEN = 256
BLK = 128
TILE = 256
NEG = -1e30
F32 = jnp.float32
BF = jnp.bfloat16
epsilon = 1e-06
gelu_scale = math.sqrt(2.0 / math.pi)
VMEM_LIMIT = 56 * 1024 * 1024


def bucket_starts():
    half=BUCKETS//2
    edges=[math.ceil(half*(DISTANCE/half)**(e/half)) for e in range(1,half)]
    return list(range(half+1))+edges

def nt(a,b):
    return lax.dot_general(a,b,(((1,),(1,)),((),())),preferred_element_type=F32)
def nn(a,b):
    return lax.dot_general(a,b,(((1,),(0,)),((),())),preferred_element_type=F32)

def head_mask(value,head,heads):
    if heads==1: return value
    size=value.shape[-1]//heads
    lane=lax.broadcasted_iota(jnp.int32,value.shape,1)
    return jnp.where((lane>=head*size)&(lane<(head+1)*size),value,jnp.zeros_like(value))

def build_bias(tab_ref,bias_ref,heads):
    starts=bucket_starts()
    key=lax.broadcasted_iota(jnp.int32,(BLK,BLK),0)
    query=lax.broadcasted_iota(jnp.int32,(BLK,BLK),1)
    for h in range(heads):
        last=tab_ref[(BUCKETS-1)*heads+h]
        for sub in (0,1):
            dist=query-key+BLK*sub
            val=jnp.full((BLK,BLK),tab_ref[h]-last,F32)
            for b in range(1,BUCKETS):
                val=jnp.where(dist>=starts[b],tab_ref[b*heads+h]-last,val)
            if sub==0:
                val=jnp.where(dist>=0,val,NEG)
                bias_ref[h,0:BLK,0:BLK]=val
                bias_ref[h,BLK:,BLK:]=val
            else:
                bias_ref[h,0:BLK,BLK:]=val
        bias_ref[h,BLK:,0:BLK]=jnp.full((BLK,BLK),NEG,F32)

def load_tile(src,slots,tile,lo,hi):
    a=src[slots[2*tile],:,lo:hi]
    b=src[slots[2*tile+1],:,lo:hi]
    return jnp.concatenate([a,b],axis=0)

def fwd_kernel(heads,prompt_tiles,slots,tab,qkv,o_ref,ot_ref,lse_ref,bias,kc,vt,qm,s_scr):
    tiles=kc.shape[0]//TILE
    width=kc.shape[1]
    size=width//heads
    build_bias(tab,bias,heads)
    def arrange(t,_):
        rows=pl.ds(pl.multiple_of(t*TILE,TILE),TILE)
        kc[rows,:]=load_tile(qkv,slots,t,width,2*width)
        vt[t]=jnp.transpose(load_tile(qkv,slots,t,2*width,3*width),(1,0))
        return 0
    lax.fori_loop(0,tiles,arrange,0)

    def scores(t_rows,h,kind,qh):
        s=nt(kc[t_rows,:],qh)
        if kind=="own":
            s=s+bias[h]
        elif kind=="prev":
            top=s[:BLK]
            low=jnp.concatenate([s[BLK:,:BLK]+bias[h,0:BLK,BLK:],s[BLK:,BLK:]],axis=1)
            s=jnp.concatenate([top,low],axis=0)
        return s

    def tile_body(t,n_far,own_static):
        q=load_tile(qkv,slots,t,0,width)
        outs=[]
        for h in range(heads):
            qh=head_mask(q,h,heads)
            m=None
            for j in range(n_far+1):
                if j<n_far:
                    rows=pl.ds(j*TILE,TILE); kind="prev" if j==n_far-1 else "far"
                else:
                    rows=pl.ds(pl.multiple_of(t*TILE,TILE),TILE) if not own_static else pl.ds(t*TILE,TILE); kind="own"
                s=scores(rows,h,kind,qh)
                s_scr[h,j]=s
                part=jnp.max(s.reshape(TILE//8,8,TILE),axis=0)
                m=part if m is None else jnp.maximum(m,part)
            m=jnp.max(m,axis=0,keepdims=True)
            l=None; acc=None
            for j in range(n_far+1):
                p=jnp.exp(s_scr[h,j]-m)
                part=jnp.sum(p.reshape(TILE//8,8,TILE),axis=0)
                l=part if l is None else l+part
                vrow=j if j<n_far else t
                a=nn(vt[vrow,h*size:(h+1)*size,:],p.astype(BF))
                acc=a if acc is None else acc+a
            l=jnp.sum(l,axis=0,keepdims=True)
            o=acc*(1.0/l)
            cols=pl.ds(t*TILE if own_static else pl.multiple_of(t*TILE,TILE),TILE)
            ot_ref[h*size:(h+1)*size,cols]=o
            lse_ref[h:h+1,cols]=m+jnp.log(l)
            outs.append(o)
        o=jnp.concatenate(outs,axis=0) if heads>1 else outs[0]
        o=jnp.transpose(o,(1,0)).astype(BF)
        o_ref[slots[2*t]]=o[:BLK]
        o_ref[slots[2*t+1]]=o[BLK:]
    for t in range(prompt_tiles):
        tile_body(t,t,True)
    def cont(c,_):
        tile_body(c,prompt_tiles,False)
        return 0
    lax.fori_loop(prompt_tiles,tiles,cont,0)

def sa_fwd(slots,tab,qkv,heads,prompt_tiles):
    nb,_,w3=qkv.shape; w=w3//3; n=nb*BLK; tiles=n//TILE
    return pl.pallas_call(
        functools.partial(fwd_kernel,heads,prompt_tiles),
        out_shape=(jax.ShapeDtypeStruct((nb,BLK,w),BF),jax.ShapeDtypeStruct((w,n),F32),jax.ShapeDtypeStruct((heads,n),F32)),
        in_specs=[pl.BlockSpec(memory_space=pltpu.SMEM),pl.BlockSpec(memory_space=pltpu.SMEM),pl.BlockSpec(memory_space=pltpu.VMEM)],
        out_specs=[pl.BlockSpec(memory_space=pltpu.VMEM)]*3,
        scratch_shapes=[pltpu.VMEM((heads,TILE,TILE),F32),pltpu.VMEM((n,w),BF),pltpu.VMEM((tiles,w,TILE),BF),pltpu.VMEM((8,128),F32),pltpu.VMEM((heads,prompt_tiles+1,TILE,TILE),F32)],
        compiler_params=pltpu.CompilerParams(vmem_limit_bytes=VMEM_LIMIT),
        name="self_attention_forward",
    )(slots,tab,qkv)

def bwd_kernel(heads,prompt_tiles,unroll,slots,tab,qkv,do_ref,ot_ref,lse_ref,dqkv_ref,dtab_ref,bias,kc,vc,kt,dkv,dqt,near,far):
    tiles=kc.shape[0]//TILE
    width=kc.shape[1]
    size=width//heads
    build_bias(tab,bias,heads)
    near[...]=jnp.zeros_like(near)
    far[...]=jnp.zeros_like(far)
    dkv[...]=jnp.zeros_like(dkv)
    def arrange(t,_):
        rows=pl.ds(pl.multiple_of(t*TILE,TILE),TILE)
        k=load_tile(qkv,slots,t,width,2*width)
        kc[rows,:]=k
        kt[t]=jnp.transpose(k,(1,0))
        vc[rows,:]=load_tile(qkv,slots,t,2*width,3*width)
        return 0
    lax.fori_loop(0,tiles,arrange,0)

    def query_tile(t,_):
        cols=pl.ds(pl.multiple_of(t*TILE,TILE),TILE)
        q=load_tile(qkv,slots,t,0,width)
        do=load_tile(do_ref,slots,t,0,width)
        dot=jnp.transpose(do.astype(F32),(1,0))*ot_ref[:,cols]
        qh=[head_mask(q,h,heads) for h in range(heads)]
        doh=[head_mask(do,h,heads) for h in range(heads)]
        lse=[lse_ref[h:h+1,cols] for h in range(heads)]
        delta=[jnp.sum(dot[h*size:(h+1)*size],axis=0,keepdims=True) for h in range(heads)]
        dqt[...]=jnp.zeros_like(dqt)

        def piece(j,kind):
            rows=pl.ds(pl.multiple_of(j*TILE,TILE),TILE)
            k=kc[rows,:]; v=vc[rows,:]
            dv=None; dk=None
            for h in range(heads):
                s=nt(k,qh[h])
                if kind=="own":
                    s=s+bias[h]
                elif kind=="prev":
                    low=jnp.concatenate([s[BLK:,:BLK]+bias[h,0:BLK,BLK:],s[BLK:,BLK:]],axis=1)
                    s=jnp.concatenate([s[:BLK],low],axis=0)
                p=jnp.exp(s-lse[h])
                dp=nt(v,doh[h])
                ds=p*(dp-delta[h])
                if kind=="own":
                    near[h,0]+=ds[:BLK,:BLK]+ds[BLK:,BLK:]
                    near[h,1]+=ds[:BLK,BLK:]
                elif kind=="prev":
                    near[h,1]+=ds[BLK:,:BLK]
                    f=jnp.sum(ds[:BLK].reshape(BLK//8,8,TILE),axis=0)
                    f2=jnp.sum(ds[BLK:,BLK:].reshape(BLK//8,8,BLK),axis=0)
                    far[h]+=f
                    far[h,:,BLK:]+=f2
                else:
                    far[h]+=jnp.sum(ds.reshape(TILE//8,8,TILE),axis=0)
                pb=p.astype(BF); db=ds.astype(BF)
                a=nn(pb,doh[h]); dv=a if dv is None else dv+a
                b=nn(db,qh[h]); dk=b if dk is None else dk+b
                dqt[h*size:(h+1)*size,:]+=nn(kt[j,h*size:(h+1)*size,:],db)
            dkv[rows,0:width]+=dk
            dkv[rows,width:2*width]+=dv
        n_far=jnp.minimum(t,prompt_tiles)-1
        def far_step(j,_):
            piece(j,"far"); return 0
        def far_many(j,_):
            for u in range(unroll): piece(j*unroll+u,"far")
            return 0
        if unroll>1:
            lax.fori_loop(0,n_far//unroll,far_many,0)
            lax.fori_loop((n_far//unroll)*unroll,n_far,far_step,0)
        else:
            lax.fori_loop(0,n_far,far_step,0)
        @pl.when(t>0)
        def _():
            piece(n_far,"prev")
        piece(t,"own")
        dq=jnp.transpose(dqt[...],(1,0)).astype(BF)
        dqkv_ref[slots[2*t],:,0:width]=dq[:BLK]
        dqkv_ref[slots[2*t+1],:,0:width]=dq[BLK:]
        return 0
    lax.fori_loop(0,tiles,query_tile,0)
    def finish(t,_):
        g=dkv[pl.ds(pl.multiple_of(t*TILE,TILE),TILE),:].astype(BF)
        dqkv_ref[slots[2*t],:,width:3*width]=g[:BLK]
        dqkv_ref[slots[2*t+1],:,width:3*width]=g[BLK:]
        return 0
    lax.fori_loop(0,tiles,finish,0)
    starts=bucket_starts()
    key=lax.broadcasted_iota(jnp.int32,(BLK,BLK),0)
    query=lax.broadcasted_iota(jnp.int32,(BLK,BLK),1)
    for h in range(heads):
        for b in range(BUCKETS):
            total=jnp.zeros((8,BLK),F32)
            for sub in (0,1):
                dist=query-key+BLK*sub
                inside=dist>=starts[b]
                if b<BUCKETS-1: inside=inside&(dist<starts[b+1])
                total=total+jnp.sum(jnp.where(inside,near[h,sub],0.0).reshape(BLK//8,8,BLK),axis=0)
            if b==BUCKETS-1:
                total=total+far[h,:,0:BLK]+far[h,:,BLK:]
            row=jnp.sum(total,axis=0,keepdims=True)
            dtab_ref[h,b:b+1,:]=jnp.broadcast_to(jnp.sum(row,axis=1,keepdims=True),(1,BLK))

def sa_bwd(slots,tab,qkv,do,ot,lse,heads,prompt_tiles,unroll=1):
    nb,_,w3=qkv.shape; w=w3//3; n=nb*BLK; tiles=n//TILE
    return pl.pallas_call(
        functools.partial(bwd_kernel,heads,prompt_tiles,unroll),
        out_shape=(jax.ShapeDtypeStruct((nb,BLK,w3),BF),jax.ShapeDtypeStruct((heads,BUCKETS,BLK),F32)),
        in_specs=[pl.BlockSpec(memory_space=pltpu.SMEM)]*2+[pl.BlockSpec(memory_space=pltpu.VMEM)]*4,
        out_specs=[pl.BlockSpec(memory_space=pltpu.VMEM)]*2,
        scratch_shapes=[pltpu.VMEM((heads,TILE,TILE),F32),pltpu.VMEM((n,w),BF),pltpu.VMEM((n,w),BF),pltpu.VMEM((tiles,w,TILE),BF),pltpu.VMEM((n,2*w),F32),pltpu.VMEM((w,TILE),F32),pltpu.VMEM((heads,2,BLK,BLK),F32),pltpu.VMEM((heads,8,TILE),F32)],
        compiler_params=pltpu.CompilerParams(vmem_limit_bytes=VMEM_LIMIT),
        name="self_attention_backward",
    )(slots,tab,qkv,do,ot,lse)


def first_kernel(states_ref, gain_ref, w_ref, out_ref):
    x = states_ref[...].astype(F32)
    r = lax.rsqrt(jnp.mean(x * x, axis=-1, keepdims=True) + epsilon)
    n = (x * r * gain_ref[...]).astype(BF)
    out_ref[...] = nn(n, w_ref[...]).astype(BF)


def first_projection(states_all, gain, weight, rows=512):
    tokens, width = states_all.shape
    cols = weight.shape[1]
    return pl.pallas_call(
        first_kernel,
        grid=(tokens // rows,),
        out_shape=jax.ShapeDtypeStruct((tokens, cols), BF),
        in_specs=[
            pl.BlockSpec((rows, width), lambda i: (i, 0)),
            pl.BlockSpec((1, width), lambda i: (0, 0)),
            pl.BlockSpec((width, cols), lambda i: (0, 0)),
        ],
        out_specs=pl.BlockSpec((rows, cols), lambda i: (i, 0)),
        compiler_params=pltpu.CompilerParams(vmem_limit_bytes=VMEM_LIMIT),
        cost_estimate=pl.CostEstimate(
            flops=2 * tokens * width * cols, bytes_accessed=2 * tokens * (width + cols), transcendentals=0
        ),
        name="first_projection",
    )(states_all, gain, weight)


def last_kernel(states_ref, gain_ref, w_ref, d_ref, dn_ref, gw_ref, acc_ref):
    step = pl.program_id(0)
    x = states_ref[...].astype(F32)
    r = lax.rsqrt(jnp.mean(x * x, axis=-1, keepdims=True) + epsilon)
    n = (x * r * gain_ref[...]).astype(BF)
    d = d_ref[...]
    dn_ref[...] = nt(d, w_ref[...]).astype(BF)
    g = lax.dot_general(n, d, (((0,), (0,)), ((), ())), preferred_element_type=F32)

    @pl.when(step == 0)
    def _():
        acc_ref[...] = g

    @pl.when(step > 0)
    def _():
        acc_ref[...] += g

    @pl.when(step == pl.num_programs(0) - 1)
    def _():
        gw_ref[...] = acc_ref[...].astype(BF)


def last_projection(states_all, gain, weight, grads, rows=512):
    tokens, width = states_all.shape
    cols = weight.shape[1]
    return pl.pallas_call(
        last_kernel,
        grid=(tokens // rows,),
        out_shape=(jax.ShapeDtypeStruct((tokens, width), BF), jax.ShapeDtypeStruct((width, cols), BF)),
        in_specs=[
            pl.BlockSpec((rows, width), lambda i: (i, 0)),
            pl.BlockSpec((1, width), lambda i: (0, 0)),
            pl.BlockSpec((width, cols), lambda i: (0, 0)),
            pl.BlockSpec((rows, cols), lambda i: (i, 0)),
        ],
        out_specs=[
            pl.BlockSpec((rows, width), lambda i: (i, 0)),
            pl.BlockSpec((width, cols), lambda i: (0, 0)),
        ],
        scratch_shapes=[pltpu.VMEM((width, cols), F32)],
        compiler_params=pltpu.CompilerParams(vmem_limit_bytes=VMEM_LIMIT),
        cost_estimate=pl.CostEstimate(
            flops=4 * tokens * width * cols, bytes_accessed=2 * tokens * (2 * width + cols), transcendentals=0
        ),
        name="last_projection",
    )(states_all, gain, weight, grads)


def norm_rows(value, gain):
    return value * lax.rsqrt(jnp.mean(value * value, axis=-1, keepdims=True) + epsilon) * gain


def geglu(gate, up_part):
    return 0.5 * gate * (1.0 + jnp.tanh(gelu_scale * (gate + 0.044715 * gate * gate * gate))) * up_part


def project(left, right):
    return jnp.einsum("td,de->te", left, right, preferred_element_type=F32)


def project_back(left, right):
    return jnp.einsum("te,de->td", left, right, preferred_element_type=F32)


def weight_grad(left, right):
    return jnp.einsum("td,te->de", left, right, preferred_element_type=F32).astype(BF)


CTX = ("plane", "core")


def gather_all(shard):
    parts = lax.axis_size(CTX)
    own = shard.shape[0] // parts
    piece = lax.dynamic_slice_in_dim(shard, lax.axis_index(CTX) * own, own, 0)
    return lax.all_gather(piece, ("fsdp",) + CTX, axis=0, tiled=True)


def reduce_all(grad):
    parts, shards = lax.axis_size(CTX), lax.axis_size("fsdp")
    own = grad.shape[0] // (parts * shards)
    g = grad.reshape(shards, parts, own, grad.shape[1]).transpose(1, 0, 2, 3)
    g = lax.psum_scatter(g, CTX, scatter_dimension=0, tiled=True)
    g = lax.psum_scatter(g.reshape(shards, own, grad.shape[1]), "fsdp", scatter_dimension=0, tiled=True)
    return lax.all_gather(g[0], CTX, axis=0, tiled=True).astype(F32)


def on_device(
    states, positions, segments, encoded, cotangent,
    self_gain, self_query, self_key, self_value, self_output, bias_table,
    cross_gain, cross_query, cross_key, cross_value, cross_output,
    feed_gain, gate_weight, up_weight, down_weight,
):
    parts, shards = lax.axis_size(CTX), lax.axis_size("fsdp")
    place = lax.axis_index(CTX)
    local, width = states.shape[1:]
    head_count = bias_table.shape[1]
    size = width // head_count
    heads = head_count // parts
    inner = heads * size
    blocks = local // BLK
    table_rows = bias_table.shape[0]
    shard_width = self_gain.shape[0]

    states_all = lax.all_gather(states[0], CTX, axis=0, tiled=True)
    columns = lax.dynamic_slice_in_dim(
        jnp.stack([self_query, self_key, self_value], axis=1), place * inner, inner, 2
    ).reshape(self_query.shape[0], 3 * inner)
    qkv_weight = lax.all_gather(columns, "fsdp", axis=0, tiled=True)
    small = jnp.concatenate([self_gain, cross_gain, feed_gain, bias_table.reshape(-1)])
    small = lax.all_gather(small, "fsdp", axis=0, tiled=False).astype(F32)
    gains = [small[:, i * shard_width : (i + 1) * shard_width].reshape(1, width) for i in range(3)]
    table = small[:, 3 * shard_width :].reshape(BUCKETS, head_count)
    own_table = lax.dynamic_slice_in_dim(table, place * heads, heads, 1).reshape(-1)
    first_pos, first_seg = positions[0, ::BLK], segments[0, ::BLK]
    canon = jnp.where(
        first_seg == 0,
        first_pos // BLK,
        PROMPT // BLK + (first_seg - 1) * (CLEN // BLK) + (first_pos - PROMPT) // BLK,
    )
    canon_all = lax.all_gather(canon, CTX, axis=0, tiled=True)
    slots = jnp.argmax(canon_all[None, :] == jnp.arange(blocks * parts)[:, None], axis=1).astype(jnp.int32)
    encoded_all = lax.all_gather(encoded[0], CTX, axis=0, tiled=True)
    out_full = gather_all(self_output)
    cq_full, ck_full, cv_full, co_full = [gather_all(w) for w in (cross_query, cross_key, cross_value, cross_output)]
    gate_full, up_full, down_full = gather_all(gate_weight), gather_all(up_weight), gather_all(down_weight)

    prompt_tiles = PROMPT // TILE
    qkv = first_projection(states_all, gains[0], qkv_weight).reshape(parts * blocks, BLK, 3 * inner)
    o, ot, lse = sa_fwd(slots, own_table, qkv, heads, prompt_tiles)
    o = lax.all_to_all(o.reshape(parts, local, inner), CTX, 0, 0, tiled=True)
    attended_low = o.transpose(1, 0, 2).reshape(local, width)

    inputs = states[0].astype(F32)
    cot = cotangent[0]
    after_self = inputs + project(attended_low, out_full)
    second_norm, second_back = jax.vjp(norm_rows, after_self, gains[1][0])
    second_low = second_norm.astype(BF)
    heads_of = lambda v: v.reshape(v.shape[0], head_count, size)
    cross_queries = project(second_low, cq_full).astype(BF)
    cross_keys = project(encoded_all, ck_full).astype(BF)
    cross_values = project(encoded_all, cv_full).astype(BF)
    scores = jnp.einsum("qhd,khd->hqk", heads_of(cross_queries), heads_of(cross_keys), preferred_element_type=F32)
    expo = jnp.exp(scores - jnp.max(scores, axis=-1, keepdims=True))
    probs = expo / jnp.sum(expo, axis=-1, keepdims=True)
    probs_low = probs.astype(BF)
    cross_attended = jnp.einsum("hqk,khd->qhd", probs_low, heads_of(cross_values), preferred_element_type=F32)
    cross_low = cross_attended.reshape(local, width).astype(BF)
    after_cross = after_self + project(cross_low, co_full)
    third_norm, third_back = jax.vjp(norm_rows, after_cross, gains[2][0])
    third_low = third_norm.astype(BF)
    gate = project(third_low, gate_full)
    up_part = project(third_low, up_full)
    hidden, hidden_back = jax.vjp(geglu, gate, up_part)
    hidden_low = hidden.astype(BF)
    layer_out = (after_cross + project(hidden_low, down_full)).astype(BF)
    grad_gate, grad_up = hidden_back(project_back(cot, down_full))
    gate_low, up_low = grad_gate.astype(BF), grad_up.astype(BF)
    g_down = reduce_all(weight_grad(hidden_low, cot))
    g_gate = reduce_all(weight_grad(third_low, gate_low))
    g_up = reduce_all(weight_grad(third_low, up_low))
    third_in, feed_gain_part = third_back(project_back(gate_low, gate_full) + project_back(up_low, up_full))
    carry_two = cot.astype(F32) + third_in
    branch_two = carry_two.astype(BF)
    g_cross_output = reduce_all(weight_grad(cross_low, branch_two))
    cross_dout = heads_of(project_back(branch_two, co_full).astype(BF))
    cross_delta = jnp.sum(cross_dout.astype(F32) * cross_attended, axis=-1).T
    dprob = jnp.einsum("qhd,khd->hqk", cross_dout, heads_of(cross_values), preferred_element_type=F32)
    dscore = (probs * (dprob - cross_delta[..., None])).astype(BF)
    dcq = jnp.einsum("hqk,khd->qhd", dscore, heads_of(cross_keys), preferred_element_type=F32)
    dcq = dcq.reshape(local, width).astype(BF)
    dck = jnp.einsum("hqk,qhd->khd", dscore, heads_of(cross_queries), preferred_element_type=F32)
    dcv = jnp.einsum("hqk,qhd->khd", probs_low, cross_dout, preferred_element_type=F32)
    dck = dck.reshape(-1, width).astype(BF)
    dcv = dcv.reshape(-1, width).astype(BF)
    g_cross_key = reduce_all(weight_grad(encoded_all, dck))
    g_cross_value = reduce_all(weight_grad(encoded_all, dcv))
    encoded_part = (project_back(dck, ck_full) + project_back(dcv, cv_full)).astype(BF)
    encoded_grad = lax.psum_scatter(encoded_part, CTX, scatter_dimension=0, tiled=True).astype(F32)
    g_cross_query = reduce_all(weight_grad(second_low, dcq))
    second_in, cross_gain_part = second_back(project_back(dcq, cq_full))
    carry_one = carry_two + second_in
    branch_one = carry_one.astype(BF)
    g_self_output = reduce_all(weight_grad(attended_low, branch_one))
    dso = project_back(branch_one, out_full).astype(BF)

    dso = dso.reshape(local, parts, inner).transpose(1, 0, 2)
    dso = lax.all_to_all(dso, CTX, 0, 0, tiled=True).reshape(parts * blocks, BLK, inner)
    dqkv, dtable = sa_bwd(slots, own_table, qkv, dso, ot, lse, heads, prompt_tiles)
    dn1, g_qkv = last_projection(states_all, gains[0], qkv_weight, dqkv.reshape(parts * local, 3 * inner))
    dn1 = lax.psum_scatter(dn1, CTX, scatter_dimension=0, tiled=True).astype(F32)
    first_back = jax.vjp(norm_rows, inputs, gains[0][0])[1]
    first_in, self_gain_part = first_back(dn1)
    states_grad = carry_one + first_in
    g_qkv = lax.psum_scatter(g_qkv, "fsdp", scatter_dimension=0, tiled=True)
    g_qkv = lax.all_gather(g_qkv, CTX, axis=0, tiled=False).astype(F32)
    g_qkv = g_qkv.reshape(parts, -1, 3, inner).transpose(2, 1, 0, 3).reshape(3, -1, width)

    table_part = jnp.zeros((BUCKETS, head_count), F32)
    table_part = lax.dynamic_update_slice_in_dim(table_part, dtable[:, :, 0].T, place * heads, 1)
    sums = jnp.concatenate([self_gain_part, cross_gain_part, feed_gain_part, table_part.reshape(-1)])
    sums = lax.psum(sums, CTX + ("fsdp",))
    mine = lax.axis_index("fsdp")
    gain_grads = [lax.dynamic_slice_in_dim(sums, i * width + mine * shard_width, shard_width) for i in range(3)]
    table_grad = lax.dynamic_slice_in_dim(sums[3 * width :].reshape(BUCKETS, head_count), mine * table_rows, table_rows, 0)
    return (
        layer_out[None], states_grad[None], encoded_grad[None],
        gain_grads[0], g_qkv[0], g_qkv[1], g_qkv[2], g_self_output, table_grad,
        gain_grads[1], g_cross_query, g_cross_key, g_cross_value, g_cross_output,
        gain_grads[2], g_gate, g_up, g_down,
    )


def solution(mesh):
    ctx, fsdp = mesh.devices.shape
    split = Mesh(mesh.devices.reshape(ctx // 2, 2, fsdp), ("plane", "core", "fsdp"))
    tokens, matrix, vector = P("fsdp", CTX, None), P("fsdp", None), P("fsdp")
    place = P("fsdp", CTX)
    return jax.shard_map(
        on_device,
        mesh=split,
        in_specs=(tokens, place, place, tokens, tokens)
        + (vector, matrix, matrix, matrix, matrix, matrix)
        + (vector, matrix, matrix, matrix, matrix)
        + (vector, matrix, matrix, matrix),
        out_specs=(tokens, tokens, tokens)
        + (vector, matrix, matrix, matrix, matrix, matrix)
        + (vector, matrix, matrix, matrix, matrix)
        + (vector, matrix, matrix, matrix),
        check_vma=False,
    )
```

time: 2740 us -> 1530 us (0.56)
  matrix products: 952 us -> 144 us
  local copies, waits for them, and re-layouts: 387 us -> 71.7 us
  waiting for transfers between devices: 1110 us -> 947 us
  Pallas kernels: 0 us -> 130 us
  other arithmetic: 152 us -> 34.3 us
  blocking collectives: 85.7 us -> 156 us
    dot_general x82 -> x29, matrix products: 944 us -> 135 us  [the longest x8 44.5 us: project(): return jnp.einsum('td,de->te', left, right, preferred_element_type=F32)]
    reduce_scatter x13 -> x19, waiting for transfers between devices: 764 us -> 464 us  [the longest x8 205 us: reduce_all(): g = lax.psum_scatter(g, CTX, scatter_dimension=0, tiled=True)]
    dot_general x8 -> x0, local copies, waits for them, and re-layouts: 272 us -> none  [pair_terms(): jnp.einsum('gqkb,bh->ghqk', onehot, table, preferred_element_type=jnp.flo...]
    all_gather x15 -> x14, waiting for transfers between devices: 256 us -> 479 us  [the longest x8 407 us: gather_all(): return lax.all_gather(piece, ('fsdp',) + CTX, axis=0, tiled=True)]
    pallas_call x0 -> x4, Pallas kernels: none -> 130 us  [the longest x1 75.4 us: sa_bwd(): pl.pallas_call(functools.partial(bwd_kernel, heads, prompt_tiles, unroll)...]
    psum x1 -> x0, waiting for transfers between devices: 79.7 us -> none  [on_device(): lax.psum(shares[8].astype(jnp.bfloat16), 'ctx').astype(jnp.float32)]
    add x19 -> x1, other arithmetic: 55.5 us -> 0.54 us  [on_device(): carry_two = cot.astype(F32) + third_in]
    reduce_sum x6 -> x2, other arithmetic: 56.4 us -> 4 us  [the longest x1 2.24 us: norm_rows(): value * lax.rsqrt(jnp.mean(value * value, axis=-1, keepdims=True) + epsilon)]
  transfers between devices with their start and end apart: 31 -> 34, of which waited for: 21 -> 28; matrix products, arithmetic and copies ran while one was open for 51% -> 13% of each run, Pallas kernels for 0% -> 9%
where the time goes in v1:
time: 1530 us; the launch traced here: 1520 us
  waiting for transfers between devices  947 us (62%)
  blocking collectives  156 us (10%)
  matrix products  144 us (9%)
  Pallas kernels  130 us (8%)
  local copies, waits for them, and re-layouts  71.7 us (5%)
  other arithmetic  34.3 us (2%)
  between operations  16.2 us (1%)
  starting transfers between devices  15.7 us (1%)
    all_gather x8, waiting for transfers between devices, gather_all(): return lax.all_gather(piece, ('fsdp',) + CTX, axis=0, tiled=True)  407 us
    reduce_scatter x8, waiting for transfers between devices, reduce_all(): g = lax.psum_scatter(g, CTX, scatter_dimension=0, tiled=True)  205 us
    reduce_scatter x8, waiting for transfers between devices, reduce_all(): lax.psum_scatter(g.reshape(shards, own, grad.shape[1]), 'fsdp', scatter_d...  132 us
    pallas_call x1, Pallas kernels, sa_bwd(): pl.pallas_call(functools.partial(bwd_kernel, heads, prompt_tiles, unroll)...  75.4 us
    reduce_scatter x1, waiting for transfers between devices, on_device(): lax.psum_scatter(dn1, CTX, scatter_dimension=0, tiled=True).astype(F32)  71.9 us
    all_gather x3, waiting for transfers between devices, reduce_all(): return lax.all_gather(g[0], CTX, axis=0, tiled=True).astype(F32)  61.2 us
    all_gather x5, blocking collectives, reduce_all(): return lax.all_gather(g[0], CTX, axis=0, tiled=True).astype(F32)  50.6 us
    dot_general x8, matrix products, project(): return jnp.einsum('td,de->te', left, right, preferred_element_type=F32)  44.5 us
  transfers between devices with their start and end apart: 34, of which 28 were waited for; matrix products, arithmetic and copies ran while one was open for 13% of the time, Pallas kernels for 9%

profile of v1, /device:TPU:0, one launch (start us, length us, event | category | flops | bytes accessed | tf_op | source)
XLA Modules:
  0.0 1515.0 jit_solution(5932407833637222744)
XLA Ops:
  22.5 14.8 all-gather.12
  41.5 8.1 all-reduce
  50.3 19.6 %all_gather.76.w_ref = bf16[1024,384]{1,0:T(8,128)(2,1)} all-gather(bf16[256,384]{1,0:T(8,128)(2,1)S(1)} %copy.147), channel_id=1, replica_groups=mesh['plane'=4,'core'=2,'fsdp'=4] {'fsdp'}, dimensions={0}, use_global_device_ids=true | all-gather | bytes 983040 | tf_op jit(solution)/shard_map/all_gather | solution.py:391
  69.9 11.0 first_projection.1
  80.9 28.2 %self_attention_forward.1 = (bf16[32,128,128]{2,1,0:T(8,128)(2,1)}, f32[128,4096]{1,0:T(8,128)}, f32[2,4096]{1,0:T(2,128)}) custom-call(s32[32]{0:T(128)} %get-tuple-element.26.slots, f32[64]{0:T(128)} %reshape.239.tab, bf16[32,128,384]{2,1,0:T(8,128)(2,1)} %bitcast.252), custom_call_target="tpu_custom_call" | custom-call | tf_op jit(solution)/shard_map/self_attention_forward/pallas_call | solution.py:131
  111.3 14.0 all-to-all-start
  125.5 26.9 %all-gather.30.cloned.1.call-done = bf16[1024,1024]{1,0:T(8,128)(2,1)} async-done(((bf16[32,1024]{1,0:T(8,128)(2,1)}), bf16[1024,1024]{1,0:T(8,128)(2,1)}) %all-gather.30.cloned.1.call-update) | async-done | bytes 2097168 | tf_op jit(solution)/shard_map/all_gather | solution.py:358
  156.6 54.4 %all-gather.34.cloned.1.call-done = bf16[1024,1024]{1,0:T(8,128)(2,1)} async-done(((bf16[32,1024]{1,0:T(8,128)(2,1)}), bf16[1024,1024]{1,0:T(8,128)(2,1)}) %all-gather.34.cloned.1.call-update) | async-done | bytes 2097168 | tf_op jit(solution)/shard_map/all_gather | solution.py:358
  214.9 54.7 %all-gather.28.cloned.1.call-done = bf16[1024,1024]{1,0:T(8,128)(2,1)} async-done(((bf16[32,1024]{1,0:T(8,128)(2,1)}), bf16[1024,1024]{1,0:T(8,128)(2,1)}) %all-gather.28.cloned.1.call-update) | async-done | bytes 2097168 | tf_op jit(solution)/shard_map/all_gather | solution.py:358
  273.8 54.3 %all-gather.32.cloned.1.call-done = bf16[1024,1024]{1,0:T(8,128)(2,1)} async-done(((bf16[32,1024]{1,0:T(8,128)(2,1)}), bf16[1024,1024]{1,0:T(8,128)(2,1)}) %all-gather.32.cloned.1.call-update) | async-done | bytes 2097168 | tf_op jit(solution)/shard_map/all_gather | solution.py:358
  333.4 9.4 fusion.42
  355.4 31.4 %all-gather.36.cloned.1.call-done = bf16[1024,1024]{1,0:T(8,128)(2,1)} async-done(((bf16[32,1024]{1,0:T(8,128)(2,1)}), bf16[1024,1024]{1,0:T(8,128)(2,1)}) %all-gather.36.cloned.1.call-update) | async-done | bytes 2097168 | tf_op jit(solution)/shard_map/all_gather | solution.py:358
  393.2 63.1 %all-gather.38.cloned.1.call-done = bf16[1024,2816]{1,0:T(8,128)(2,1)} async-done(((bf16[32,2816]{1,0:T(8,128)(2,1)}), bf16[1024,2816]{1,0:T(8,128)(2,1)}) %all-gather.38.cloned.1.call-update) | async-done | bytes 5767184 | tf_op jit(solution)/shard_map/all_gather | solution.py:358
  456.3 8.6 fusion.43
  464.9 61.1 %all-gather.40.cloned.1.call-done = bf16[1024,2816]{1,0:T(8,128)(2,1)} async-done(((bf16[32,2816]{1,0:T(8,128)(2,1)}), bf16[1024,2816]{1,0:T(8,128)(2,1)}) %all-gather.40.cloned.1.call-update) | async-done | bytes 5767184 | tf_op jit(solution)/shard_map/all_gather | solution.py:358
  526.0 8.6 fusion.44
  534.7 60.9 %all-gather.42.cloned.1.call-done = bf16[2816,1024]{1,0:T(8,128)(2,1)} async-done(((bf16[88,1024]{1,0:T(8,128)(2,1)}), bf16[2816,1024]{1,0:T(8,128)(2,1)}) %all-gather.42.cloned.1.call-update) | async-done | bytes 5767184 | tf_op jit(solution)/shard_map/all_gather | solution.py:358
  595.6 16.6 %fusion.8 = (bf16[512,2816]{1,0:T(8,128)(2,1)}, bf16[512,2816]{1,0:T(8,128)(2,1)}, bf16[512,2816]{1,0:T(8,128)(2,1)S(1)}) fusion(f32[512,2816]{1,0:T(8,128)} %fusion.43, f32[512,2816]{1,0:T(8,128)} %fusion.44, bf16[2816,1024]{1,0:T(8,128)(2,1)} %all-gather.42.cloned.1.call-done, bf16[1,512,1024]{2,1,0:T(8,128)(2,1)} %param.24), kind=kOutput, calls=%fused_computation.17 | convolution fusion | flops 2996043776 | bytes 27000832 | tf_op jit(solution)/shard_map/te,de->td/dot_general | solution.py:344
  710.0 23.8 %all_to_all.10 = bf16[8,512,128]{2,1,0:T(8,128)(2,1)} all-to-all(bf16[8,512,128]{2,1,0:T(8,128)(2,1)S(1)} %bitcast.275), channel_id=1, replica_groups=mesh['plane'=4,'core'=2,'fsdp'=4] {'plane','core'}, dimensions={0} | all-to-all | bytes 2097152 | tf_op jit(solution)/shard_map/all_to_all | solution.py:470
  733.8 75.4 %self_attention_backward.1 = (bf16[32,128,384]{2,1,0:T(8,128)(2,1)}, f32[2,32,128]{2,1,0:T(8,128)}) custom-call(s32[32]{0:T(128)} %get-tuple-element.26.slots, f32[64]{0:T(128)} %reshape.239.tab, bf16[32,128,384]{2,1,0:T(8,128)(2,1)} %bitcast.253, bf16[32,128,128]{2,1,0:T(8,128)(2,1)} %bitcast.281, f32[128,4096]{1,0:T(8,128)} %get-tuple-element.28.ot_ref, ...), custom_call_target="tpu_custom_call" | custom-call | tf_op jit(solution)/shard_map/self_attention_backward/pallas_call | solution.py:244
  809.2 15.5 %last_projection.1 = (bf16[4096,1024]{1,0:T(8,128)(2,1)}, bf16[1024,384]{1,0:T(8,128)(2,1)}) custom-call(bf16[4096,1024]{1,0:T(8,128)(2,1)} %bitcast.264, f32[1,1024]{1,0:T(1,128)} %bitcast.323, bf16[1024,384]{1,0:T(8,128)(2,1)} %all_gather.76.w_ref, bf16[4096,384]{1,0:T(8,128)(2,1)} %bitcast.325), custom_call_target="tpu_custom_call" | custom-call | flops 6442450944 | bytes 19922944 | tf_op jit(solution)/shard_map/last_projection/pallas_call | solution.py:308
  832.4 26.3 %reduce-scatter.26.cloned.1.call-done = bf16[1,4,32,1024]{3,2,1,0:T(8,128)(2,1)} async-done(((bf16[8,4,32,1024]{3,2,1,0:T(8,128)(2,1)}), bf16[1,4,32,1024]{3,2,1,0:T(8,128)(2,1)}) %reduce-scatter.26.cloned.1.call-update) | async-done | bytes 262160 | tf_op jit(solution)/shard_map/reduce_scatter | solution.py:365
  858.8 44.3 %reduce-scatter.30.cloned.1.call-done = bf16[1,4,32,1024]{3,2,1,0:T(8,128)(2,1)} async-done(((bf16[8,4,32,1024]{3,2,1,0:T(8,128)(2,1)}), bf16[1,4,32,1024]{3,2,1,0:T(8,128)(2,1)}) %reduce-scatter.30.cloned.1.call-update) | async-done | bytes 262160 | tf_op jit(solution)/shard_map/reduce_scatter | solution.py:365
  903.2 44.7 %reduce-scatter.34.cloned.1.call-done = bf16[1,4,32,1024]{3,2,1,0:T(8,128)(2,1)} async-done(((bf16[8,4,32,1024]{3,2,1,0:T(8,128)(2,1)}), bf16[1,4,32,1024]{3,2,1,0:T(8,128)(2,1)}) %reduce-scatter.34.cloned.1.call-update) | async-done | bytes 262160 | tf_op jit(solution)/shard_map/reduce_scatter | solution.py:365
  947.9 44.3 %reduce-scatter.38.cloned.1.call-done = bf16[1,4,32,1024]{3,2,1,0:T(8,128)(2,1)} async-done(((bf16[8,4,32,1024]{3,2,1,0:T(8,128)(2,1)}), bf16[1,4,32,1024]{3,2,1,0:T(8,128)(2,1)}) %reduce-scatter.38.cloned.1.call-update) | async-done | bytes 262160 | tf_op jit(solution)/shard_map/reduce_scatter | solution.py:365
  992.3 45.3 %reduce-scatter.42.cloned.1.call-done = bf16[1,4,32,1024]{3,2,1,0:T(8,128)(2,1)} async-done(((bf16[8,4,32,1024]{3,2,1,0:T(8,128)(2,1)}), bf16[1,4,32,1024]{3,2,1,0:T(8,128)(2,1)}) %reduce-scatter.42.cloned.1.call-update) | async-done | bytes 262160 | tf_op jit(solution)/shard_map/reduce_scatter | solution.py:365
  1037.6 26.2 %reduce-scatter.24.cloned.1.call-done = bf16[256,384]{1,0:T(8,128)(2,1)} async-done(((bf16[1024,384]{1,0:T(8,128)(2,1)}), bf16[256,384]{1,0:T(8,128)(2,1)}) %reduce-scatter.24.cloned.1.call-update) | async-done | bytes 196624 | tf_op jit(solution)/shard_map/reduce_scatter | solution.py:477
  1063.9 24.1 %reduce-scatter.56.cloned.1.call-done = bf16[1,88,1024]{2,1,0:T(8,128)(2,1)} async-done(((bf16[4,88,1024]{2,1,0:T(8,128)(2,1)}), bf16[1,88,1024]{2,1,0:T(8,128)(2,1)}) %reduce-scatter.56.cloned.1.call-update) | async-done | bytes 180240 | tf_op jit(solution)/shard_map/reduce_scatter | solution.py:366
  1088.0 24.1 %reduce-scatter.48.cloned.1.call-done = bf16[1,32,2816]{2,1,0:T(8,128)(2,1)} async-done(((bf16[4,32,2816]{2,1,0:T(8,128)(2,1)}), bf16[1,32,2816]{2,1,0:T(8,128)(2,1)}) %reduce-scatter.48.cloned.1.call-update) | async-done | bytes 180240 | tf_op jit(solution)/shard_map/reduce_scatter | solution.py:366
  1112.1 24.1 %reduce-scatter.52.cloned.1.call-done = bf16[1,32,2816]{2,1,0:T(8,128)(2,1)} async-done(((bf16[4,32,2816]{2,1,0:T(8,128)(2,1)}), bf16[1,32,2816]{2,1,0:T(8,128)(2,1)}) %reduce-scatter.52.cloned.1.call-update) | async-done | bytes 180240 | tf_op jit(solution)/shard_map/reduce_scatter | solution.py:366
  1137.8 8.2 fusion.21
  1146.5 28.6 %reduce-scatter.22.cloned.1.call-done = bf16[64,1024]{1,0:T(8,128)(2,1)} async-done(((bf16[512,1024]{1,0:T(8,128)(2,1)}), bf16[64,1024]{1,0:T(8,128)(2,1)}) %reduce-scatter.22.cloned.1.call-update) | async-done | bytes 131088 | tf_op jit(solution)/shard_map/reduce_scatter | solution.py:461
  1176.7 20.1 %reduce-scatter.28.cloned.1.call-done = bf16[1,32,1024]{2,1,0:T(8,128)(2,1)} async-done(((bf16[4,32,1024]{2,1,0:T(8,128)(2,1)}), bf16[1,32,1024]{2,1,0:T(8,128)(2,1)}) %reduce-scatter.28.cloned.1.call-update) | async-done | bytes 65552 | tf_op jit(solution)/shard_map/reduce_scatter | solution.py:366
  1196.8 10.1 all-gather.4
  1206.9 10.2 reduce-scatter.32.cloned.1.call-done
  1217.2 10.2 all-gather.5
  1227.4 9.8 reduce-scatter.36.cloned.1.call-done
  1237.2 10.1 all-gather.6
  1247.3 10.1 reduce-scatter.40.cloned.1.call-done
  1257.3 10.1 all-gather.7
  1267.4 10.1 reduce-scatter.44.cloned.1.call-done
  1277.5 10.1 all-gather.8
  1293.0 10.5 all-gather.48.cloned.1.call-done
  1317.4 13.2 all-gather.54.cloned.1.call-done
  1333.8 23.9 %all-gather.50.cloned.1.call-done = bf16[1,256,2816]{2,1,0:T(8,128)(2,1)} async-done(((bf16[1,32,2816]{2,1,0:T(8,128)(2,1)}), bf16[1,256,2816]{2,1,0:T(8,128)(2,1)}) %all-gather.50.cloned.1.call-update) | async-done | bytes 1441808 | tf_op jit(solution)/shard_map/all_gather | solution.py:367
  1360.9 24.1 %all-gather.52.cloned.1.call-done = bf16[1,256,2816]{2,1,0:T(8,128)(2,1)} async-done(((bf16[1,32,2816]{2,1,0:T(8,128)(2,1)}), bf16[1,256,2816]{2,1,0:T(8,128)(2,1)}) %all-gather.52.cloned.1.call-update) | async-done | bytes 1441808 | tf_op jit(solution)/shard_map/all_gather | solution.py:367
  1388.1 71.9 %reduce-scatter.20.cloned.1.call-done = bf16[512,1024]{1,0:T(8,128)(2,1)} async-done(((bf16[4096,1024]{1,0:T(8,128)(2,1)}), bf16[512,1024]{1,0:T(8,128)(2,1)}) %reduce-scatter.20.cloned.1.call-update) | async-done | bytes 1048592 | tf_op jit(solution)/shard_map/reduce_scatter | solution.py:473
  1462.3 39.5 %psum.7 = f32[3584]{0:T(1024)S(1)} all-reduce(f32[3584]{0:T(1024)S(1)} %pad_maximum_fusion), channel_id=1, replica_groups=mesh['plane'=4,'core'=2,'fsdp'=4] {'plane','core','fsdp'}, use_global_device_ids=true, to_apply=%region_15.16 | all-reduce | flops 3584 | bytes 28672 | tf_op jit(solution)/shard_map/psum | solution.py:484
  (279 shorter events, 204.4 us)
Async XLA Ops:
  7.2 15.1 copy-start.35
  7.2 15.2 %copy-start.36 = (bf16[256]{0:T(256)(128)(2,1)S(1)}, bf16[256]{0:T(256)(128)(2,1)}, u32[]{:S(2)}) copy-start(bf16[256]{0:T(256)(128)(2,1)} %param.36) | copy-start | bytes 1540
  7.2 15.2 %copy-start.37 = (bf16[256]{0:T(256)(128)(2,1)S(1)}, bf16[256]{0:T(256)(128)(2,1)}, u32[]{:S(2)}) copy-start(bf16[256]{0:T(256)(128)(2,1)} %param.31) | copy-start | bytes 1540
  7.2 15.2 %copy-start.38 = (bf16[256]{0:T(256)(128)(2,1)S(1)}, bf16[256]{0:T(256)(128)(2,1)}, u32[]{:S(2)}) copy-start(bf16[256]{0:T(256)(128)(2,1)} %param.25) | copy-start | bytes 1540
  7.2 32.0 %copy-start.29 = (bf16[256,1024]{1,0:T(8,128)(2,1)S(1)}, bf16[256,1024]{1,0:T(8,128)(2,1)}, u32[]{:S(2)}) copy-start(bf16[256,1024]{1,0:T(8,128)(2,1)} %param.28) | copy-start | bytes 1572868
  7.3 62.7 %all-gather.44.cloned.1.call-start = ((), (), s32[]{:S(2)}) async-start(), calls=%async_computation.48 | async-start | bytes 9437184 | tf_op jit(solution)/shard_map/all_gather | solution.py:387
  8.0 31.5 %copy-start.30 = (bf16[256,1024]{1,0:T(8,128)(2,1)S(1)}, bf16[256,1024]{1,0:T(8,128)(2,1)}, u32[]{:S(2)}) copy-start(bf16[256,1024]{1,0:T(8,128)(2,1)} %param.27) | copy-start | bytes 1572868
  8.0 117.5 %all-gather.46.cloned.1.call-start = ((), (), s32[]{:S(2)}) async-start(), calls=%async_computation.49 | async-start | bytes 1179648 | tf_op jit(solution)/shard_map/all_gather | solution.py:405
  8.8 143.7 %all-gather.30.cloned.1.call-start = ((), (), s32[]{:S(2)}) async-start(), calls=%async_computation.22 | async-start | bytes 2162688 | tf_op jit(solution)/shard_map/all_gather | solution.py:358
  10.3 200.7 %all-gather.34.cloned.1.call-start = ((), (), s32[]{:S(2)}) async-start(), calls=%async_computation.24 | async-start | bytes 2162688 | tf_op jit(solution)/shard_map/all_gather | solution.py:358
  11.9 257.7 %all-gather.28.cloned.1.call-start = ((), (), s32[]{:S(2)}) async-start(), calls=%async_computation.21 | async-start | bytes 2162688 | tf_op jit(solution)/shard_map/all_gather | solution.py:358
  13.4 314.7 %all-gather.32.cloned.1.call-start = ((), (), s32[]{:S(2)}) async-start(), calls=%async_computation.23 | async-start | bytes 2162688 | tf_op jit(solution)/shard_map/all_gather | solution.py:358
  14.9 24.7 %copy-start.31 = (bf16[256,1024]{1,0:T(8,128)(2,1)S(1)}, bf16[256,1024]{1,0:T(8,128)(2,1)}, u32[]{:S(2)}) copy-start(bf16[256,1024]{1,0:T(8,128)(2,1)} %param.26) | copy-start | bytes 1572868
  15.0 371.8 %all-gather.36.cloned.1.call-start = ((), (), s32[]{:S(2)}) async-start(), calls=%async_computation.25 | async-start | bytes 2162688 | tf_op jit(solution)/shard_map/all_gather | solution.py:358
  16.6 439.8 %all-gather.38.cloned.1.call-start = ((), (), s32[]{:S(2)}) async-start(), calls=%async_computation.26 | async-start | bytes 5947392 | tf_op jit(solution)/shard_map/all_gather | solution.py:358
  17.3 508.7 %all-gather.40.cloned.1.call-start = ((), (), s32[]{:S(2)}) async-start(), calls=%async_computation.27 | async-start | bytes 5947392 | tf_op jit(solution)/shard_map/all_gather | solution.py:358
  19.0 576.5 %all-gather.42.cloned.1.call-start = ((), (), s32[]{:S(2)}) async-start(), calls=%async_computation.28 | async-start | bytes 5947392 | tf_op jit(solution)/shard_map/all_gather | solution.py:358
  111.3 158.2 %all-to-all-start = ((bf16[8,512,128]{1,2,0:T(8,128)(2,1)}), bf16[8,512,128]{1,2,0:T(8,128)(2,1)S(1)}, u32[]{:S(2)}, u32[]{:S(2)}) async-start(bf16[8,512,128]{1,2,0:T(8,128)(2,1)} %copy.148), calls=%async_computation | async-start | bytes 2097152 | tf_op jit(solution)/shard_map/all_to_all | solution.py:413
  125.4 699.4 %reduce-scatter.54.cloned.1.call-start = ((), (), s32[]{:S(2)}) async-start(), calls=%async_computation.46 | async-start | bytes 6488064 | tf_op jit(solution)/shard_map/reduce_scatter | solution.py:365
  125.5 85.5 %copy-start.42 = (bf16[1,512,1024]{2,1,0:T(8,128)(2,1)S(1)}, bf16[1,512,1024]{2,1,0:T(8,128)(2,1)}, u32[]{:S(2)}) copy-start(bf16[1,512,1024]{2,1,0:T(8,128)(2,1)} %all-gather.46.cloned.1.call-done) | copy-start | bytes 3145732
  156.5 114.0 %copy-start.4 = (bf16[1,512,1024]{2,1,0:T(8,128)(2,1)S(1)}, bf16[1,512,1024]{2,1,0:T(8,128)(2,1)}, u32[]{:S(2)}) copy-start(bf16[1,512,1024]{2,1,0:T(8,128)(2,1)} %param.20) | copy-start | bytes 3145732
  273.8 58.2 %copy-start.9 = (f32[512,1024]{1,0:T(8,128)}, f32[512,1024]{1,0:T(8,128)S(1)}, u32[]{:S(2)}) copy-start(f32[512,1024]{1,0:T(8,128)S(1)} %get-tuple-element.108) | copy-start | bytes 6291460
  342.8 10.1 copy-start.21
  595.6 16.6 %copy-start.27 = (bf16[1,512,1024]{2,1,0:T(8,128)(2,1)S(1)}, bf16[1,512,1024]{2,1,0:T(8,128)(2,1)}, u32[]{:S(2)}) copy-start(bf16[1,512,1024]{2,1,0:T(8,128)(2,1)} %param.24) | copy-start | bytes 3145732
  618.8 206.6 %reduce-scatter.46.cloned.1.call-start = ((), (), s32[]{:S(2)}) async-start(), calls=%async_computation.42 | async-start | bytes 6488064 | tf_op jit(solution)/shard_map/reduce_scatter | solution.py:365
  627.6 198.5 %reduce-scatter.50.cloned.1.call-start = ((), (), s32[]{:S(2)}) async-start(), calls=%async_computation.44 | async-start | bytes 6488064 | tf_op jit(solution)/shard_map/reduce_scatter | solution.py:365
  636.5 222.2 %reduce-scatter.26.cloned.1.call-start = ((), (), s32[]{:S(2)}) async-start(), calls=%async_computation.32 | async-start | bytes 2359296 | tf_op jit(solution)/shard_map/reduce_scatter | solution.py:365
  673.0 33.9 %copy-start.8 = (f32[512,1024]{1,0:T(8,128)}, f32[512,1024]{1,0:T(8,128)S(1)}, u32[]{:S(2)}) copy-start(f32[512,1024]{1,0:T(8,128)S(1)} %fusion.12) | copy-start | bytes 6291460
  675.8 227.3 %reduce-scatter.30.cloned.1.call-start = ((), (), s32[]{:S(2)}) async-start(), calls=%async_computation.34 | async-start | bytes 2359296 | tf_op jit(solution)/shard_map/reduce_scatter | solution.py:365
  680.8 267.0 %reduce-scatter.34.cloned.1.call-start = ((), (), s32[]{:S(2)}) async-start(), calls=%async_computation.36 | async-start | bytes 2359296 | tf_op jit(solution)/shard_map/reduce_scatter | solution.py:365
  690.1 302.1 %reduce-scatter.38.cloned.1.call-start = ((), (), s32[]{:S(2)}) async-start(), calls=%async_computation.38 | async-start | bytes 2359296 | tf_op jit(solution)/shard_map/reduce_scatter | solution.py:365
  701.3 336.3 %reduce-scatter.42.cloned.1.call-start = ((), (), s32[]{:S(2)}) async-start(), calls=%async_computation.40 | async-start | bytes 2359296 | tf_op jit(solution)/shard_map/reduce_scatter | solution.py:365
  706.8 356.9 %reduce-scatter.24.cloned.1.call-start = ((), (), s32[]{:S(2)}) async-start(), calls=%async_computation.31 | async-start | bytes 983040 | tf_op jit(solution)/shard_map/reduce_scatter | solution.py:477
  824.7 263.2 %reduce-scatter.56.cloned.1.call-start = ((), (), s32[]{:S(2)}) async-start(), calls=%async_computation.47 | async-start | bytes 901120 | tf_op jit(solution)/shard_map/reduce_scatter | solution.py:366
  825.3 286.7 %reduce-scatter.48.cloned.1.call-start = ((), (), s32[]{:S(2)}) async-start(), calls=%async_computation.43 | async-start | bytes 901120 | tf_op jit(solution)/shard_map/reduce_scatter | solution.py:366
  826.1 310.1 %reduce-scatter.52.cloned.1.call-start = ((), (), s32[]{:S(2)}) async-start(), calls=%async_computation.45 | async-start | bytes 901120 | tf_op jit(solution)/shard_map/reduce_scatter | solution.py:366
  826.8 348.3 %reduce-scatter.22.cloned.1.call-start = ((), (), s32[]{:S(2)}) async-start(), calls=%async_computation.30 | async-start | bytes 1179648 | tf_op jit(solution)/shard_map/reduce_scatter | solution.py:461
  832.4 364.4 %reduce-scatter.28.cloned.1.call-start = ((), (), s32[]{:S(2)}) async-start(), calls=%async_computation.33 | async-start | bytes 327680 | tf_op jit(solution)/shard_map/reduce_scatter | solution.py:366
  858.7 358.4 %reduce-scatter.32.cloned.1.call-start = ((), (), s32[]{:S(2)}) async-start(), calls=%async_computation.35 | async-start | bytes 327680 | tf_op jit(solution)/shard_map/reduce_scatter | solution.py:366
  903.1 334.0 %reduce-scatter.36.cloned.1.call-start = ((), (), s32[]{:S(2)}) async-start(), calls=%async_computation.37 | async-start | bytes 327680 | tf_op jit(solution)/shard_map/reduce_scatter | solution.py:366
  947.9 309.5 %reduce-scatter.40.cloned.1.call-start = ((), (), s32[]{:S(2)}) async-start(), calls=%async_computation.39 | async-start | bytes 327680 | tf_op jit(solution)/shard_map/reduce_scatter | solution.py:366
  992.2 285.2 %reduce-scatter.44.cloned.1.call-start = ((), (), s32[]{:S(2)}) async-start(), calls=%async_computation.41 | async-start | bytes 327680 | tf_op jit(solution)/shard_map/reduce_scatter | solution.py:366
  1037.6 265.9 %all-gather.48.cloned.1.call-start = ((), (), s32[]{:S(2)}) async-start(), calls=%async_computation.50 | async-start | bytes 1769472 | tf_op jit(solution)/shard_map/all_gather | solution.py:478
  1063.8 266.7 %all-gather.54.cloned.1.call-start = ((), (), s32[]{:S(2)}) async-start(), calls=%async_computation.53 | async-start | bytes 1622016 | tf_op jit(solution)/shard_map/all_gather | solution.py:367
  1087.9 269.8 %all-gather.50.cloned.1.call-start = ((), (), s32[]{:S(2)}) async-start(), calls=%async_computation.51 | async-start | bytes 1622016 | tf_op jit(solution)/shard_map/all_gather | solution.py:367
  1112.1 272.9 %all-gather.52.cloned.1.call-start = ((), (), s32[]{:S(2)}) async-start(), calls=%async_computation.52 | async-start | bytes 1622016 | tf_op jit(solution)/shard_map/all_gather | solution.py:367
  1136.2 323.8 %reduce-scatter.20.cloned.1.call-start = ((), (), s32[]{:S(2)}) async-start(), calls=%async_computation.29 | async-start | bytes 9437184 | tf_op jit(solution)/shard_map/reduce_scatter | solution.py:473
  1460.0 44.5 %copy-start.16 = (bf16[512,1024]{1,0:T(8,128)(2,1)S(1)}, bf16[512,1024]{1,0:T(8,128)(2,1)}, u32[]{:S(2)}) copy-start(bf16[512,1024]{1,0:T(8,128)(2,1)} %reduce-scatter.20.cloned.1.call-done) | copy-start | bytes 3145732
  (34 other events, 114.2 us)
Sparse Core Ops, SparseCore 0:
  10.0 57.1 all-gather.43
  69.1 23.4 all-gather.45
  96.0 56.3 all-gather.29
  155.7 55.2 all-gather.33
  214.3 55.2 all-gather.27
  272.8 55.2 all-gather.31
  331.5 55.2 all-gather.35
  390.2 66.1 all-gather.37
  459.8 66.2 all-gather.39
  529.3 66.2 all-gather.41
  618.9 58.0 reduce-scatter.53
  680.7 70.1 reduce-scatter.45
  754.3 59.1 reduce-scatter.49
  817.5 41.1 reduce-scatter.25
  861.8 41.1 reduce-scatter.29
  906.6 41.2 reduce-scatter.33
  951.0 41.1 reduce-scatter.37
  996.3 41.2 reduce-scatter.41
  1040.4 23.3 reduce-scatter.23
  1065.9 21.9 reduce-scatter.55
  1090.2 21.7 reduce-scatter.47
  1114.4 21.7 reduce-scatter.51
  1140.0 35.0 reduce-scatter.21
  1177.2 19.5 reduce-scatter.27
  1199.2 17.9 reduce-scatter.31
  1219.3 17.8 reduce-scatter.35
  1239.4 17.9 reduce-scatter.39
  1259.6 17.8 reduce-scatter.43
  1279.5 23.9 all-gather.47
  1305.4 25.1 all-gather.53
  1332.6 25.1 all-gather.49
  1359.8 25.1 all-gather.51
  1388.7 71.2 reduce-scatter.19

commit v2 on v1

v2 whole, which is shorter than its diff:
```python
import functools
import math

import jax
import jax.numpy as jnp
from jax import lax
from jax.experimental import pallas as pl
from jax.experimental.pallas import tpu as pltpu
from jax.sharding import Mesh
from jax.sharding import PartitionSpec as P

BUCKETS = 32
DISTANCE = 128
PROMPT = 2048
CLEN = 256
BLK = 128
TILE = 256
NEG = -1e30
F32 = jnp.float32
BF = jnp.bfloat16
epsilon = 1e-06
gelu_scale = math.sqrt(2.0 / math.pi)
VMEM_LIMIT = 56 * 1024 * 1024


def bucket_starts():
    half=BUCKETS//2
    edges=[math.ceil(half*(DISTANCE/half)**(e/half)) for e in range(1,half)]
    return list(range(half+1))+edges

def nt(a,b):
    return lax.dot_general(a,b,(((1,),(1,)),((),())),preferred_element_type=F32)
def nn(a,b):
    return lax.dot_general(a,b,(((1,),(0,)),((),())),preferred_element_type=F32)

def head_mask(value,head,heads):
    if heads==1: return value
    size=value.shape[-1]//heads
    lane=lax.broadcasted_iota(jnp.int32,value.shape,1)
    return jnp.where((lane>=head*size)&(lane<(head+1)*size),value,jnp.zeros_like(value))

def build_bias(tab_ref,bias_ref,heads):
    starts=bucket_starts()
    key=lax.broadcasted_iota(jnp.int32,(BLK,BLK),0)
    query=lax.broadcasted_iota(jnp.int32,(BLK,BLK),1)
    for h in range(heads):
        last=tab_ref[(BUCKETS-1)*heads+h]
        for sub in (0,1):
            dist=query-key+BLK*sub
            val=jnp.full((BLK,BLK),tab_ref[h]-last,F32)
            for b in range(1,BUCKETS):
                val=jnp.where(dist>=starts[b],tab_ref[b*heads+h]-last,val)
            if sub==0:
                val=jnp.where(dist>=0,val,NEG)
                bias_ref[h,0:BLK,0:BLK]=val
                bias_ref[h,BLK:,BLK:]=val
            else:
                bias_ref[h,0:BLK,BLK:]=val
        bias_ref[h,BLK:,0:BLK]=jnp.full((BLK,BLK),NEG,F32)

def load_tile(src,slots,tile,lo,hi):
    a=src[slots[2*tile],:,lo:hi]
    b=src[slots[2*tile+1],:,lo:hi]
    return jnp.concatenate([a,b],axis=0)

def fwd_kernel(heads,prompt_tiles,slots,tab,qkv,o_ref,ot_ref,lse_ref,bias,kc,vt,qm,s_scr):
    tiles=kc.shape[0]//TILE
    width=kc.shape[1]
    size=width//heads
    build_bias(tab,bias,heads)
    def arrange(t,_):
        rows=pl.ds(pl.multiple_of(t*TILE,TILE),TILE)
        kc[rows,:]=load_tile(qkv,slots,t,width,2*width)
        vt[t]=jnp.transpose(load_tile(qkv,slots,t,2*width,3*width),(1,0))
        return 0
    lax.fori_loop(0,tiles,arrange,0)

    def scores(t_rows,h,kind,qh):
        s=nt(kc[t_rows,:],qh)
        if kind=="own":
            s=s+bias[h]
        elif kind=="prev":
            top=s[:BLK]
            low=jnp.concatenate([s[BLK:,:BLK]+bias[h,0:BLK,BLK:],s[BLK:,BLK:]],axis=1)
            s=jnp.concatenate([top,low],axis=0)
        return s

    def tile_body(t,n_far,own_static):
        q=load_tile(qkv,slots,t,0,width)
        outs=[]
        for h in range(heads):
            qh=head_mask(q,h,heads)
            m=None
            for j in range(n_far+1):
                if j<n_far:
                    rows=pl.ds(j*TILE,TILE); kind="prev" if j==n_far-1 else "far"
                else:
                    rows=pl.ds(pl.multiple_of(t*TILE,TILE),TILE) if not own_static else pl.ds(t*TILE,TILE); kind="own"
                s=scores(rows,h,kind,qh)
                s_scr[h,j]=s
                part=jnp.max(s.reshape(TILE//8,8,TILE),axis=0)
                m=part if m is None else jnp.maximum(m,part)
            m=jnp.max(m,axis=0,keepdims=True)
            l=None; acc=None
            for j in range(n_far+1):
                p=jnp.exp(s_scr[h,j]-m)
                part=jnp.sum(p.reshape(TILE//8,8,TILE),axis=0)
                l=part if l is None else l+part
                vrow=j if j<n_far else t
                a=nn(vt[vrow,h*size:(h+1)*size,:],p.astype(BF))
                acc=a if acc is None else acc+a
            l=jnp.sum(l,axis=0,keepdims=True)
            o=acc*(1.0/l)
            cols=pl.ds(t*TILE if own_static else pl.multiple_of(t*TILE,TILE),TILE)
            ot_ref[h*size:(h+1)*size,cols]=o
            lse_ref[h:h+1,cols]=m+jnp.log(l)
            outs.append(o)
        o=jnp.concatenate(outs,axis=0) if heads>1 else outs[0]
        o=jnp.transpose(o,(1,0)).astype(BF)
        o_ref[slots[2*t]]=o[:BLK]
        o_ref[slots[2*t+1]]=o[BLK:]
    for t in range(prompt_tiles):
        tile_body(t,t,True)
    def cont(c,_):
        tile_body(c,prompt_tiles,False)
        return 0
    lax.fori_loop(prompt_tiles,tiles,cont,0)

def sa_fwd(slots,tab,qkv,heads,prompt_tiles):
    nb,_,w3=qkv.shape; w=w3//3; n=nb*BLK; tiles=n//TILE
    return pl.pallas_call(
        functools.partial(fwd_kernel,heads,prompt_tiles),
        out_shape=(jax.ShapeDtypeStruct((nb,BLK,w),BF),jax.ShapeDtypeStruct((w,n),F32),jax.ShapeDtypeStruct((heads,n),F32)),
        in_specs=[pl.BlockSpec(memory_space=pltpu.SMEM),pl.BlockSpec(memory_space=pltpu.SMEM),pl.BlockSpec(memory_space=pltpu.VMEM)],
        out_specs=[pl.BlockSpec(memory_space=pltpu.VMEM)]*3,
        scratch_shapes=[pltpu.VMEM((heads,TILE,TILE),F32),pltpu.VMEM((n,w),BF),pltpu.VMEM((tiles,w,TILE),BF),pltpu.VMEM((8,128),F32),pltpu.VMEM((heads,prompt_tiles+1,TILE,TILE),F32)],
        compiler_params=pltpu.CompilerParams(vmem_limit_bytes=VMEM_LIMIT),
        cost_estimate=pl.CostEstimate(flops=32 * 10**9, bytes_accessed=8 * n * w3, transcendentals=0),
        name="self_attention_forward",
    )(slots,tab,qkv)

def bwd_kernel(heads,prompt_tiles,unroll,low,high,slots,tab,qkv,do_ref,ot_ref,lse_ref,*refs):
    if low:
        dq_in,dkv_in,near_in,far_in,dqkv_ref,dtab_ref,bias,kc,vc,kt,dqt,dkv,near,far=refs
    else:
        dq_out,dkv,near,far,bias,kc,vc,kt,dqt=refs
    tiles=kc.shape[0]//TILE
    width=kc.shape[1]
    size=width//heads
    build_bias(tab,bias,heads)
    for mine,start in ((near,near_in if low else None),(far,far_in if low else None),(dkv,dkv_in if low else None)):
        mine[...]=start[...] if low else jnp.zeros_like(mine)
    def arrange(t,_):
        rows=pl.ds(pl.multiple_of(t*TILE,TILE),TILE)
        k=load_tile(qkv,slots,t,width,2*width)
        kc[rows,:]=k
        kt[t]=jnp.transpose(k,(1,0))
        vc[rows,:]=load_tile(qkv,slots,t,2*width,3*width)
        return 0
    lax.fori_loop(0,tiles,arrange,0)

    def query_tile(t,_):
        cols=pl.ds(pl.multiple_of(t*TILE,TILE),TILE)
        q=load_tile(qkv,slots,t,0,width)
        do=load_tile(do_ref,slots,t,0,width)
        dot=jnp.transpose(do.astype(F32),(1,0))*ot_ref[:,cols]
        qh=[head_mask(q,h,heads) for h in range(heads)]
        doh=[head_mask(do,h,heads) for h in range(heads)]
        lse=[lse_ref[h:h+1,cols] for h in range(heads)]
        delta=[jnp.sum(dot[h*size:(h+1)*size],axis=0,keepdims=True) for h in range(heads)]
        dqt[...]=jnp.zeros_like(dqt)

        def piece(j,kind):
            rows=pl.ds(pl.multiple_of(j*TILE,TILE),TILE)
            k=kc[rows,:]; v=vc[rows,:]
            dv=None; dk=None
            for h in range(heads):
                s=nt(k,qh[h])
                if kind=="own":
                    s=s+bias[h]
                elif kind=="prev":
                    low=jnp.concatenate([s[BLK:,:BLK]+bias[h,0:BLK,BLK:],s[BLK:,BLK:]],axis=1)
                    s=jnp.concatenate([s[:BLK],low],axis=0)
                p=jnp.exp(s-lse[h])
                dp=nt(v,doh[h])
                ds=p*(dp-delta[h])
                if kind=="own":
                    near[h,0]+=ds[:BLK,:BLK]+ds[BLK:,BLK:]
                    near[h,1]+=ds[:BLK,BLK:]
                elif kind=="prev":
                    near[h,1]+=ds[BLK:,:BLK]
                    f=jnp.sum(ds[:BLK].reshape(BLK//8,8,TILE),axis=0)
                    f2=jnp.sum(ds[BLK:,BLK:].reshape(BLK//8,8,BLK),axis=0)
                    far[h]+=f
                    far[h,:,BLK:]+=f2
                else:
                    far[h]+=jnp.sum(ds.reshape(TILE//8,8,TILE),axis=0)
                pb=p.astype(BF); db=ds.astype(BF)
                a=nn(pb,doh[h]); dv=a if dv is None else dv+a
                b=nn(db,qh[h]); dk=b if dk is None else dk+b
                dqt[h*size:(h+1)*size,:]+=nn(kt[j,h*size:(h+1)*size,:],db)
            dkv[rows,0:width]+=dk
            dkv[rows,width:2*width]+=dv
        n_far=jnp.maximum(jnp.minimum(t,prompt_tiles)-1,0)
        def far_step(j,_):
            piece(j,"far"); return 0
        def far_many(j,_):
            for u in range(unroll): piece(j*unroll+u,"far")
            return 0
        if unroll>1:
            lax.fori_loop(0,n_far//unroll,far_many,0)
            lax.fori_loop((n_far//unroll)*unroll,n_far,far_step,0)
        else:
            lax.fori_loop(0,n_far,far_step,0)
        @pl.when(t>0)
        def _():
            piece(n_far,"prev")
        piece(t,"own")
        dq=jnp.transpose(dqt[...],(1,0)).astype(BF)
        if low:
            dqkv_ref[slots[2*t],:,0:width]=dq[:BLK]
            dqkv_ref[slots[2*t+1],:,0:width]=dq[BLK:]
        else:
            dq_out[cols,:]=dq
        return 0
    lax.fori_loop(low,high,query_tile,0)
    if not low:
        return
    def bring(t,_):
        dq=dq_in[pl.ds(pl.multiple_of(t*TILE,TILE),TILE),:]
        dqkv_ref[slots[2*t],:,0:width]=dq[:BLK]
        dqkv_ref[slots[2*t+1],:,0:width]=dq[BLK:]
        return 0
    lax.fori_loop(0,low,bring,0)
    def finish(t,_):
        g=dkv[pl.ds(pl.multiple_of(t*TILE,TILE),TILE),:].astype(BF)
        dqkv_ref[slots[2*t],:,width:3*width]=g[:BLK]
        dqkv_ref[slots[2*t+1],:,width:3*width]=g[BLK:]
        return 0
    lax.fori_loop(0,tiles,finish,0)
    starts=bucket_starts()
    key=lax.broadcasted_iota(jnp.int32,(BLK,BLK),0)
    query=lax.broadcasted_iota(jnp.int32,(BLK,BLK),1)
    for h in range(heads):
        for b in range(BUCKETS):
            total=jnp.zeros((8,BLK),F32)
            for sub in (0,1):
                dist=query-key+BLK*sub
                inside=dist>=starts[b]
                if b<BUCKETS-1: inside=inside&(dist<starts[b+1])
                total=total+jnp.sum(jnp.where(inside,near[h,sub],0.0).reshape(BLK//8,8,BLK),axis=0)
            if b==BUCKETS-1:
                total=total+far[h,:,0:BLK]+far[h,:,BLK:]
            row=jnp.sum(total,axis=0,keepdims=True)
            dtab_ref[h,b:b+1,:]=jnp.broadcast_to(jnp.sum(row,axis=1,keepdims=True),(1,BLK))

def sa_bwd(slots,tab,qkv,do,ot,lse,heads,prompt_tiles,low,high,held=(),unroll=2):
    nb,_,w3=qkv.shape; w=w3//3; n=nb*BLK; tiles=n//TILE
    shape=jax.ShapeDtypeStruct
    sums=[shape((n,2*w),F32),shape((heads,2,BLK,BLK),F32),shape((heads,8,TILE),F32)]
    if low:
        out=[shape((nb,BLK,w3),BF),shape((heads,BUCKETS,BLK),F32)]
    else:
        out=[shape((high*TILE,w),BF)]+sums
    scratch=[pltpu.VMEM((heads,TILE,TILE),F32),pltpu.VMEM((n,w),BF),pltpu.VMEM((n,w),BF),pltpu.VMEM((tiles,w,TILE),BF),pltpu.VMEM((w,TILE),F32)]
    if low:
        scratch+=[pltpu.VMEM(v.shape,F32) for v in sums]
    return pl.pallas_call(
        functools.partial(bwd_kernel,heads,prompt_tiles,unroll,low,high),
        out_shape=out,
        in_specs=[pl.BlockSpec(memory_space=pltpu.SMEM)]*2+[pl.BlockSpec(memory_space=pltpu.VMEM)]*(4+len(held)),
        out_specs=[pl.BlockSpec(memory_space=pltpu.VMEM)]*len(out),
        scratch_shapes=scratch,
        compiler_params=pltpu.CompilerParams(vmem_limit_bytes=VMEM_LIMIT),
        cost_estimate=pl.CostEstimate(flops=43 * 10**9, bytes_accessed=12 * n * w3, transcendentals=0),
        name="self_attention_backward",
    )(slots,tab,qkv,do,ot,lse,*held)


def line_tile(step, size=TILE):
    return pl.ds(pl.multiple_of(step * size, size), size)


def whole_weight(ref, scratch):
    parts, shards, _, rows, _ = ref.shape
    for z in range(shards):
        for c in range(parts):
            start = (z * parts + c) * rows
            scratch[start : start + rows, :] = ref[c, z, 0]


def store_rows(ref, layout, which, cols, value):
    parts, shards, matrices, rows = layout
    for z in range(shards):
        for c in range(parts):
            start = (z * parts + c) * rows
            place = (z * matrices + which) * rows
            ref[c, place : place + rows, cols] = value[start : start + rows]


def store_grad(ref, which, cols, value):
    parts, shards, _, rows, _ = ref.shape
    for z in range(shards):
        for c in range(parts):
            start = (z * parts + c) * rows
            ref[c, z, which, :, cols] = value[start : start + rows]


def inverse_rms(v):
    return lax.rsqrt(jnp.mean(v * v, axis=-1, keepdims=True) + epsilon)


def norm_back(v, gain, dn):
    r = inverse_rms(v)
    weighted = dn * gain
    dv = r * weighted - v * (r * r * r) * jnp.mean(weighted * v, axis=-1, keepdims=True)
    return dv, jnp.sum(dn * v * r, axis=0, keepdims=True)


def whole(shape, index=None):
    zeros = (0,) * len(shape)
    return pl.BlockSpec(shape, lambda *_: zeros if index is None else index)


def packed_spec(packed, which):
    parts, shards, _, rows, width = packed.shape
    return pl.BlockSpec((parts, shards, 1, rows, width), lambda *_: (0, 0, which, 0, 0))


def params():
    return pltpu.CompilerParams(vmem_limit_bytes=VMEM_LIMIT)


def cost(flops, size):
    return pl.CostEstimate(flops=flops, bytes_accessed=size, transcendentals=0)


def source_kernel(source_ref, w_ref, out_ref, weight):
    whole_weight(w_ref, weight)
    source = source_ref[...]
    for t in range(out_ref.shape[-1] // TILE):
        cols = slice(t * TILE, (t + 1) * TILE)
        out_ref[0, :, cols] = nn(source, weight[:, cols]).astype(BF)


def source_projection(source, packed):
    rows, width = source.shape
    parts, shards, _, own, _ = packed.shape
    return pl.pallas_call(
        source_kernel,
        grid=(2,),
        out_shape=jax.ShapeDtypeStruct((2, rows, width), BF),
        in_specs=[
            whole((rows, width)),
            pl.BlockSpec((parts, shards, 1, own, width), lambda i: (0, 0, 3 + i, 0, 0)),
        ],
        out_specs=pl.BlockSpec((1, rows, width), lambda i: (i, 0, 0)),
        scratch_shapes=[pltpu.VMEM((width, width), BF)],
        compiler_params=params(),
        cost_estimate=cost(4 * rows * width * width, 8 * width * width),
        name="source_projection",
    )(source, packed)


def middle_kernel(
    head_count, o_ref, states_ref, gain_two, gain_three, wo_ref, wq_ref, wc_ref, ckv_ref,
    ob_ref, x1_ref, cq_ref, cob_ref, cot_ref, lse_ref, x2_ref, n3_ref, weight, cvt,
):
    rows, width = states_ref.shape
    size = width // head_count
    pair = 2 * size
    for s in range(o_ref.shape[0]):
        inner = o_ref.shape[2]
        ob_ref[:, s * inner : (s + 1) * inner] = o_ref[s]
    whole_weight(wo_ref, weight)

    def add_out(t, _):
        cols = line_tile(t)
        x1_ref[:, cols] = states_ref[:, cols].astype(F32) + nn(ob_ref[...], weight[:, cols])
        return 0

    lax.fori_loop(0, width // TILE, add_out, 0)
    x1 = x1_ref[...]
    n3_ref[...] = (x1 * inverse_rms(x1) * gain_two[...]).astype(BF)
    whole_weight(wq_ref, weight)

    def make_query(t, _):
        cols = line_tile(t)
        cq_ref[:, cols] = nn(n3_ref[...], weight[:, cols]).astype(BF)
        return 0

    lax.fori_loop(0, width // TILE, make_query, 0)

    def attend(p, _):
        cols = line_tile(p, pair)
        keys = ckv_ref[0, :, cols]
        cvt[...] = jnp.transpose(ckv_ref[1, :, cols], (1, 0))
        count = keys.shape[0]
        for half in range(rows // TILE):
            span = slice(half * TILE, (half + 1) * TILE)
            q = cq_ref[span, cols]
            outs = []
            for h in range(2):
                s = nt(keys, head_mask(q, h, 2))
                m = jnp.max(jnp.max(s.reshape(count // 8, 8, TILE), axis=0), axis=0, keepdims=True)
                e = jnp.exp(s - m)
                total = jnp.sum(jnp.sum(e.reshape(count // 8, 8, TILE), axis=0), axis=0, keepdims=True)
                out = nn(cvt[h * size : (h + 1) * size, :], e.astype(BF)) * (1.0 / total)
                lse_ref[p, h : h + 1, span] = m + jnp.log(total)
                outs.append(out)
            both = jnp.concatenate(outs, axis=0)
            cot_ref[p, :, span] = both
            cob_ref[span, cols] = jnp.transpose(both, (1, 0)).astype(BF)
        return 0

    lax.fori_loop(0, width // pair, attend, 0)
    whole_weight(wc_ref, weight)

    def add_cross(t, _):
        cols = line_tile(t)
        x2_ref[:, cols] = x1_ref[:, cols] + nn(cob_ref[...], weight[:, cols])
        return 0

    lax.fori_loop(0, width // TILE, add_cross, 0)
    x2 = x2_ref[...]
    n3_ref[...] = (x2 * inverse_rms(x2) * gain_three[...]).astype(BF)


def middle_forward(o, states, gain_two, gain_three, packed, ckv, head_count):
    rows, width = states.shape
    size = width // head_count
    pairs = head_count // 2
    tokens = lambda dtype: jax.ShapeDtypeStruct((rows, width), dtype)
    shapes = [
        tokens(BF), tokens(F32), tokens(BF), tokens(BF),
        jax.ShapeDtypeStruct((pairs, 2 * size, rows), F32), jax.ShapeDtypeStruct((pairs, 8, rows), F32),
        tokens(F32), tokens(BF),
    ]
    return pl.pallas_call(
        functools.partial(middle_kernel, head_count),
        grid=(1,),
        out_shape=shapes,
        in_specs=[
            whole(o.shape), whole((rows, width)), whole((1, width)), whole((1, width)),
            packed_spec(packed, 0), packed_spec(packed, 1), packed_spec(packed, 2), whole(ckv.shape),
        ],
        out_specs=[whole(s.shape) for s in shapes],
        scratch_shapes=[pltpu.VMEM((width, width), BF), pltpu.VMEM((2 * size, ckv.shape[1]), BF)],
        compiler_params=params(),
        cost_estimate=cost(60 * rows * width * width, 24 * rows * width),
        name="middle_forward",
    )(o, states, gain_two, gain_three, packed, packed, packed, ckv)


def feed_kernel(
    n3_ref, cot_ref, x2_ref, gain_ref, w_ref, wd_ref,
    out_ref, dx2_ref, gain_out_ref, gw_ref, gd_ref, n3t, acc, dn, wg, wu,
):
    step = pl.program_id(0)

    @pl.when(step == 0)
    def _():
        n3t[...] = jnp.transpose(n3_ref[...], (1, 0))
        acc[...] = jnp.zeros_like(acc)
        dn[...] = jnp.zeros_like(dn)

    parts, shards, _, rows, _ = w_ref.shape
    for z in range(shards):
        for c in range(parts):
            start = (z * parts + c) * rows
            wg[start : start + rows, :] = w_ref[c, z, 0]
            wu[start : start + rows, :] = w_ref[c, z, 1]
    n3, cot, wd = n3_ref[...], cot_ref[...], wd_ref[...]
    gate, up = nn(n3, wg[...]), nn(n3, wu[...])
    dh = nt(cot, wd)
    t = jnp.tanh(gelu_scale * (gate + 0.044715 * gate * gate * gate))
    gelu = 0.5 * gate * (1.0 + t)
    slope = 0.5 * (1.0 + t) + 0.5 * gate * (1.0 - t * t) * (gelu_scale * (1.0 + 3 * 0.044715 * gate * gate))
    hidden = (gelu * up).astype(BF)
    dgate = (dh * up * slope).astype(BF)
    dup = (dh * gelu).astype(BF)
    acc[...] += nn(hidden, wd)
    gd_ref[...] = nn(jnp.transpose(hidden, (1, 0)), cot).astype(BF)
    everything = slice(None)
    store_grad(gw_ref, 0, everything, nn(n3t[...], dgate).astype(BF))
    store_grad(gw_ref, 1, everything, nn(n3t[...], dup).astype(BF))
    dn[...] += nt(dgate, wg[...]) + nt(dup, wu[...])

    @pl.when(step == pl.num_programs(0) - 1)
    def _():
        x2 = x2_ref[...]
        out_ref[...] = (x2 + acc[...]).astype(BF)
        dv, gain_out_ref[...] = norm_back(x2, gain_ref[...], dn[...])
        dx2_ref[...] = cot_ref[...].astype(F32) + dv


def feed_forward(n3, cot, x2, gain, wide, down):
    rows, width = n3.shape
    parts, shards, _, own, hidden = wide.shape
    tokens = lambda dtype: jax.ShapeDtypeStruct((rows, width), dtype)
    piece = pl.BlockSpec((parts, shards, 2, own, TILE), lambda i: (0, 0, 0, 0, i))
    return pl.pallas_call(
        feed_kernel,
        grid=(hidden // TILE,),
        out_shape=[
            tokens(BF), tokens(F32), jax.ShapeDtypeStruct((1, width), F32),
            jax.ShapeDtypeStruct(wide.shape, BF), jax.ShapeDtypeStruct(down.shape, BF),
        ],
        in_specs=[
            whole((rows, width)), whole((rows, width)), whole((rows, width)), whole((1, width)),
            piece, pl.BlockSpec((TILE, width), lambda i: (i, 0)),
        ],
        out_specs=[
            whole((rows, width)), whole((rows, width)), whole((1, width)),
            piece, pl.BlockSpec((TILE, width), lambda i: (i, 0)),
        ],
        scratch_shapes=[
            pltpu.VMEM((width, rows), BF), pltpu.VMEM((rows, width), F32), pltpu.VMEM((rows, width), F32),
            pltpu.VMEM((width, TILE), BF), pltpu.VMEM((width, TILE), BF),
        ],
        compiler_params=params(),
        cost_estimate=cost(28 * rows * width * hidden, 12 * width * hidden),
        name="feed_forward",
    )(n3, cot, x2, gain, wide, down)


def middle_back_kernel(
    head_count, dx2_ref, x1_ref, gain_ref, wo_ref, wq_ref, wc_ref, cq_ref, ckv_ref, cot_ref, lse_ref,
    dx1_ref, gain_out_ref, dcq_ref, dckv_ref, dso_ref, weight, dco, ckt, dn,
):
    rows, width = dx2_ref.shape
    size = width // head_count
    pair = 2 * size
    count = ckv_ref.shape[1]
    whole_weight(wc_ref, weight)

    def back_out(t, _):
        dco[:, line_tile(t)] = nt(dx2_ref[...].astype(BF), weight[line_tile(t), :]).astype(BF)
        return 0

    lax.fori_loop(0, width // TILE, back_out, 0)

    def attend(p, _):
        cols = line_tile(p, pair)
        q, do = cq_ref[:, cols], dco[:, cols]
        terms = jnp.transpose(do.astype(F32), (1, 0)) * cot_ref[p]
        ckt[...] = jnp.transpose(ckv_ref[0, :, cols], (1, 0))
        qh = [head_mask(q, h, 2) for h in range(2)]
        doh = [head_mask(do, h, 2) for h in range(2)]
        lse = [lse_ref[p, h : h + 1, :] for h in range(2)]
        delta = [jnp.sum(terms[h * size : (h + 1) * size], axis=0, keepdims=True) for h in range(2)]
        dqt = [None, None]
        for t in range(count // TILE):
            span = slice(t * TILE, (t + 1) * TILE)
            k, v = ckv_ref[0, span, cols], ckv_ref[1, span, cols]
            dk = dv = None
            for h in range(2):
                weights = jnp.exp(nt(k, qh[h]) - lse[h])
                ds = (weights * (nt(v, doh[h]) - delta[h])).astype(BF)
                a, b = nn(weights.astype(BF), doh[h]), nn(ds, qh[h])
                dv = a if dv is None else dv + a
                dk = b if dk is None else dk + b
                c = nn(ckt[h * size : (h + 1) * size, span], ds)
                dqt[h] = c if dqt[h] is None else dqt[h] + c
            dckv_ref[0, span, cols] = dk.astype(BF)
            dckv_ref[1, span, cols] = dv.astype(BF)
        dcq_ref[:, cols] = jnp.transpose(jnp.concatenate(dqt, axis=0), (1, 0)).astype(BF)
        return 0

    lax.fori_loop(0, width // pair, attend, 0)
    whole_weight(wq_ref, weight)

    def back_query(t, _):
        dn[:, line_tile(t)] = nt(dcq_ref[...], weight[line_tile(t), :])
        return 0

    lax.fori_loop(0, width // TILE, back_query, 0)
    dv, gain_out_ref[...] = norm_back(x1_ref[...], gain_ref[...], dn[...])
    dx1_ref[...] = dx2_ref[...] + dv
    whole_weight(wo_ref, weight)
    inner = dso_ref.shape[2]
    per = TILE // inner if inner < TILE else 1
    da = dx1_ref[...].astype(BF)
    for t in range(width // TILE):
        tile = nt(da, weight[t * TILE : (t + 1) * TILE, :]).astype(BF)
        for u in range(per):
            dso_ref[t * per + u] = tile[:, u * inner : (u + 1) * inner]


def middle_back(dx2, x1, gain, packed, cq, ckv, cot, lse, head_count, parts):
    rows, width = dx2.shape
    size = width // head_count
    count = ckv.shape[1]
    shapes = [
        jax.ShapeDtypeStruct((rows, width), F32), jax.ShapeDtypeStruct((1, width), F32),
        jax.ShapeDtypeStruct((rows, width), BF), jax.ShapeDtypeStruct(ckv.shape, BF),
        jax.ShapeDtypeStruct((parts, rows, width // parts), BF),
    ]
    return pl.pallas_call(
        functools.partial(middle_back_kernel, head_count),
        grid=(1,),
        out_shape=shapes,
        in_specs=[
            whole((rows, width)), whole((rows, width)), whole((1, width)),
            packed_spec(packed, 0), packed_spec(packed, 1), packed_spec(packed, 2),
            whole((rows, width)), whole(ckv.shape), whole(cot.shape), whole(lse.shape),
        ],
        out_specs=[whole(s.shape) for s in shapes],
        scratch_shapes=[
            pltpu.VMEM((width, width), BF), pltpu.VMEM((rows, width), BF),
            pltpu.VMEM((2 * size, count), BF), pltpu.VMEM((rows, width), F32),
        ],
        compiler_params=params(),
        cost_estimate=cost(60 * rows * width * width, 24 * rows * width),
        name="middle_back",
    )(dx2, x1, gain, packed, packed, packed, cq, ckv, cot, lse)


def middle_grad_kernel(
    dx2_ref, x1_ref, gain_ref, cob_ref, dcq_ref, dckv_ref, source_ref, ob_ref, dx1_ref, wk_ref, wv_ref,
    g_ref, wk, wv, left, left_source,
):
    width = x1_ref.shape[1]
    parts, shards, _, own, _ = wk_ref.shape
    layout = (parts, shards, 5, own)
    tail = shards * 5 * own
    piece = source_ref.shape[0] // parts
    whole_weight(wk_ref, wk)
    whole_weight(wv_ref, wv)
    for t in range(width // TILE):
        span = slice(t * TILE, (t + 1) * TILE)
        value = (nt(dckv_ref[0], wk[span, :]) + nt(dckv_ref[1], wv[span, :])).astype(BF)
        for c in range(parts):
            g_ref[c, tail : tail + piece, span] = value[c * piece : (c + 1) * piece]

    def product(which, lhs, right):
        def tile(t, _):
            cols = line_tile(t)
            store_rows(g_ref, layout, which, cols, nn(lhs[...], right(cols)).astype(BF))
            return 0

        lax.fori_loop(0, width // TILE, tile, 0)

    left[...] = jnp.transpose(ob_ref[...], (1, 0))
    product(0, left, lambda cols: dx1_ref[:, cols].astype(BF))
    x1 = x1_ref[...]
    left[...] = jnp.transpose((x1 * inverse_rms(x1) * gain_ref[...]).astype(BF), (1, 0))
    product(1, left, lambda cols: dcq_ref[:, cols])
    left[...] = jnp.transpose(cob_ref[...], (1, 0))
    product(2, left, lambda cols: dx2_ref[:, cols].astype(BF))
    left_source[...] = jnp.transpose(source_ref[...], (1, 0))
    product(3, left_source, lambda cols: dckv_ref[0, :, cols])
    product(4, left_source, lambda cols: dckv_ref[1, :, cols])


def middle_grads(dx2, x1, gain, cob, dcq, dckv, source, ob, dx1, packed):
    rows, width = dx2.shape
    count = source.shape[0]
    parts, shards, _, own, _ = packed.shape
    tokens = whole((rows, width))
    shape = (parts, shards * 5 * own + count // parts, width)
    return pl.pallas_call(
        middle_grad_kernel,
        grid=(1,),
        out_shape=jax.ShapeDtypeStruct(shape, BF),
        in_specs=[
            tokens, tokens, whole((1, width)), tokens, tokens, whole(dckv.shape), whole((count, width)), tokens, tokens,
            packed_spec(packed, 3), packed_spec(packed, 4),
        ],
        out_specs=whole(shape),
        scratch_shapes=[
            pltpu.VMEM((width, width), BF), pltpu.VMEM((width, width), BF),
            pltpu.VMEM((width, rows), BF), pltpu.VMEM((width, count), BF),
        ],
        compiler_params=params(),
        cost_estimate=cost(46 * rows * width * width, 24 * rows * width),
        name="middle_grads",
    )(dx2, x1, gain, cob, dcq, dckv, source, ob, dx1, packed, packed)


def final_kernel(d_ref, w_ref, states_ref, gain_ref, dx1_ref, out_ref):
    dn = None
    for s in range(d_ref.shape[0]):
        part = nt(d_ref[s], w_ref[s])
        dn = part if dn is None else dn + part
    dv, _ = norm_back(states_ref[...].astype(F32), gain_ref[...], dn)
    out_ref[...] = dx1_ref[...] + dv


def final_back(dqkv, weights, states, gain, dx1, tile=128):
    parts, rows, inner = dqkv.shape
    width = states.shape[1]
    return pl.pallas_call(
        final_kernel,
        grid=(rows // tile,),
        out_shape=jax.ShapeDtypeStruct((rows, width), F32),
        in_specs=[
            pl.BlockSpec((parts, tile, inner), lambda i: (0, i, 0)),
            whole(weights.shape),
            pl.BlockSpec((tile, width), lambda i: (i, 0)),
            whole((1, width)),
            pl.BlockSpec((tile, width), lambda i: (i, 0)),
        ],
        out_specs=pl.BlockSpec((tile, width), lambda i: (i, 0)),
        compiler_params=params(),
        cost_estimate=cost(6 * rows * width * width, 12 * rows * width),
        name="final_back",
    )(dqkv, weights, states, gain, dx1)


def first_kernel(states_ref, gain_ref, w_ref, out_ref):
    x = states_ref[0].astype(F32)
    n = (x * inverse_rms(x) * gain_ref[...]).astype(BF)
    out_ref[...] = nn(n, w_ref[...]).astype(BF)


def first_projection(gathered, gain, weight, rows):
    parts, _, width = gathered.shape
    cols = weight.shape[1]
    return pl.pallas_call(
        first_kernel,
        grid=(parts,),
        out_shape=jax.ShapeDtypeStruct((parts * rows, cols), BF),
        in_specs=[
            pl.BlockSpec((1, rows, width), lambda i: (i, 0, 0)), whole((1, width)), whole((width, cols)),
        ],
        out_specs=pl.BlockSpec((rows, cols), lambda i: (i, 0)),
        compiler_params=params(),
        cost_estimate=cost(2 * parts * rows * width * cols, 2 * parts * rows * (width + cols)),
        name="first_projection",
    )(gathered, gain, weight)


def last_kernel(states_ref, gain_ref, w_ref, d_ref, gw_ref, gain_out_ref, acc_ref):
    step = pl.program_id(0)
    x = states_ref[0].astype(F32)
    n = (x * inverse_rms(x) * gain_ref[...]).astype(BF)
    g = lax.dot_general(n, d_ref[...], (((0,), (0,)), ((), ())), preferred_element_type=F32)

    @pl.when(step == 0)
    def _():
        acc_ref[...] = g

    @pl.when(step > 0)
    def _():
        acc_ref[...] += g

    @pl.when(step == pl.num_programs(0) - 1)
    def _():
        total = acc_ref[...]
        gw_ref[...] = total.astype(BF)
        gain_out_ref[...] = jnp.sum(total * w_ref[...].astype(F32), axis=1, keepdims=True)


def last_projection(gathered, gain, weight, grads, rows):
    parts, _, width = gathered.shape
    cols = weight.shape[1]
    return pl.pallas_call(
        last_kernel,
        grid=(parts,),
        out_shape=(jax.ShapeDtypeStruct((width, cols), BF), jax.ShapeDtypeStruct((width, 1), F32)),
        in_specs=[
            pl.BlockSpec((1, rows, width), lambda i: (i, 0, 0)), whole((1, width)), whole((width, cols)),
            pl.BlockSpec((rows, cols), lambda i: (i, 0)),
        ],
        out_specs=[whole((width, cols)), whole((width, 1))],
        scratch_shapes=[pltpu.VMEM((width, cols), F32)],
        compiler_params=params(),
        cost_estimate=cost(2 * parts * rows * width * cols, 2 * parts * rows * (width + cols)),
        name="last_projection",
    )(gathered, gain, weight, grads)


CTX = ("plane", "core")


def spread(piece):
    count = lax.axis_size("fsdp")
    return lax.all_to_all(jnp.broadcast_to(piece[None], (count,) + piece.shape), "fsdp", 0, 0, tiled=True)


def collect(parts):
    return jnp.sum(lax.all_to_all(parts, "fsdp", 0, 0, tiled=True).astype(F32), axis=0)


def collect_far(parts):
    count, mine = lax.axis_size("fsdp"), lax.axis_index("fsdp")
    if count > 4:
        return collect(parts)
    total = take(parts, mine, 0).astype(F32)
    for step in range(1, count):
        for sign in (1, -1):
            message = take(parts, jnp.clip(mine + sign * step, 0, count - 1), 0)
            pairs = [(i, i + sign * step) for i in range(count) if 0 <= i + sign * step < count]
            total = total + lax.ppermute(message, "fsdp", pairs).astype(F32)
    return total


def after(value, earlier):
    return lax.optimization_barrier((value, earlier))[0]


def own_rows(shard):
    rows = shard.shape[0] // lax.axis_size(CTX)
    return lax.dynamic_slice_in_dim(shard, lax.axis_index(CTX) * rows, rows, 0)


def swap(value, axis):
    return lax.ppermute(value, axis, [(0, 1), (1, 0)])


def take(value, index, axis):
    return lax.dynamic_index_in_dim(value, index, axis, keepdims=False)


def gather_down(shard):
    core = lax.axis_index("core")
    rows, width = shard.shape
    mine = spread(lax.dynamic_slice_in_dim(shard, core * (rows // 2), rows // 2, 0))
    other = swap(mine, "core")
    first = jnp.where(core == 0, mine, other)
    second = jnp.where(core == 0, other, mine)
    return jnp.stack([first, second], axis=1).reshape(-1, width)


def share_down(grad):
    shards, core = lax.axis_size("fsdp"), lax.axis_index("core")
    halves = grad.reshape(shards, 2, -1, grad.shape[1])
    other = swap(take(halves, 1 - core, 1), "core")
    return (take(halves, core, 1).astype(F32) + other.astype(F32)).astype(BF)


def reduce_planes(half):
    planes, width = lax.axis_size("plane"), half.shape[1]
    if planes != 4:
        return lax.psum_scatter(half, "plane", scatter_dimension=0, tiled=True)
    plane = lax.axis_index("plane")
    for bit, size in ((1, 2), (2, 1)):
        side = (plane // bit) % 2
        split = half.reshape(size, 2, -1, width)
        got = lax.ppermute(take(split, 1 - side, 1), "plane", [(i, i ^ bit) for i in range(4)])
        half = (take(split, side, 1).astype(F32) + got.astype(F32)).astype(BF)
    return half.reshape(-1, width)


def on_device(
    states, positions, segments, encoded, cotangent,
    self_gain, self_query, self_key, self_value, self_output, bias_table,
    cross_gain, cross_query, cross_key, cross_value, cross_output,
    feed_gain, gate_weight, up_weight, down_weight,
):
    parts, shards = lax.axis_size(CTX), lax.axis_size("fsdp")
    place = lax.axis_index(CTX)
    local, width = states.shape[1:]
    head_count = bias_table.shape[1]
    size = width // head_count
    heads = head_count // parts
    inner = heads * size
    blocks = local // BLK
    shard_width = self_gain.shape[0]
    hidden_width = gate_weight.shape[1]
    own = shard_width // parts
    aligned = own % 16 == 0

    def arranged(pieces):
        if aligned:
            return pieces
        matrices, columns = pieces.shape[2], pieces.shape[4]
        return pieces.transpose(2, 1, 0, 3, 4).reshape(1, 1, matrices, width, columns)

    def scattered(grads):
        if aligned:
            return grads
        matrices, columns = grads.shape[2], grads.shape[4]
        return grads.reshape(matrices, shards, parts, own, columns).transpose(2, 1, 0, 3, 4)

    gathered = lax.all_gather(jnp.concatenate([states[0], encoded[0]], axis=0), CTX, axis=0, tiled=False)
    encoded_all = gathered[:, local:].reshape(-1, width)
    columns = lax.dynamic_slice_in_dim(
        jnp.stack([self_query, self_key, self_value], axis=1), place * inner, inner, 2
    ).reshape(shard_width, 3 * inner)
    small = jnp.concatenate([self_gain, cross_gain, feed_gain, bias_table.reshape(-1)])
    small_width = small.shape[0]
    small = jnp.pad(small, (0, 16 * 3 * inner - small_width)).reshape(16, 3 * inner)
    line = spread(jnp.concatenate([columns, small], axis=0))
    qkv_weight = line[:, :shard_width].reshape(width, 3 * inner)
    small = line[:, shard_width:].reshape(shards, -1)[:, :small_width].astype(F32)
    gains = [small[:, i * shard_width : (i + 1) * shard_width].reshape(1, width) for i in range(3)]
    table = small[:, 3 * shard_width :].reshape(BUCKETS, head_count)
    own_table = lax.dynamic_slice_in_dim(table, place * heads, heads, 1).reshape(-1)
    first_pos, first_seg = positions[0, ::BLK], segments[0, ::BLK]
    canon = jnp.where(
        first_seg == 0,
        first_pos // BLK,
        PROMPT // BLK + (first_seg - 1) * (CLEN // BLK) + (first_pos - PROMPT) // BLK,
    )
    canon_all = lax.all_gather(canon, CTX, axis=0, tiled=True)
    slots = jnp.argmax(canon_all[None, :] == jnp.arange(blocks * parts)[:, None], axis=1).astype(jnp.int32)

    squares = jnp.stack([own_rows(w) for w in (self_output, cross_query, cross_output, cross_key, cross_value)], axis=0)
    squares = spread(after(squares, line))
    wide = spread(after(jnp.stack([own_rows(gate_weight), own_rows(up_weight)], axis=0), squares))
    squares = lax.all_gather(after(squares, gathered), CTX, axis=0, tiled=False)

    prompt_tiles = PROMPT // TILE
    qkv = first_projection(gathered, gains[0], qkv_weight, local).reshape(parts * blocks, BLK, 3 * inner)
    o, ot, lse = sa_fwd(slots, own_table, qkv, heads, prompt_tiles)
    o = lax.all_to_all(o.reshape(parts, local, inner), CTX, 0, 0, tiled=True)

    wide = lax.all_gather(after(wide, (squares, lse)), CTX, axis=0, tiled=False)
    qkv_all = lax.all_gather(after(qkv_weight, wide), CTX, axis=0, tiled=False)
    squares, wide = arranged(squares), arranged(wide)
    down = gather_down(after(down_weight, o))
    ckv = source_projection(encoded_all, squares)
    ob, x1, cq, cob, cot, cross_lse, x2, n3 = middle_forward(
        o, states[0], gains[1], gains[2], squares, ckv, head_count
    )
    layer_out, dx2, feed_gain_part, g_wide, g_down = feed_forward(n3, cotangent[0], x2, gains[2], wide, down)
    g_wide = lax.psum_scatter(scattered(g_wide), CTX, scatter_dimension=0, tiled=False)
    g_down = share_down(g_down)
    dx1, cross_gain_part, dcq, dckv, dso = middle_back(
        after(dx2, qkv_all), x1, gains[1], squares, cq, ckv, cot, cross_lse, head_count, parts
    )
    dso = lax.all_to_all(dso, CTX, 0, 0, tiled=True).reshape(parts * blocks, BLK, inner)
    g_squares = middle_grads(dx2, x1, gains[1], cob, dcq, dckv, encoded_all, ob, dx1, squares)
    if not aligned:
        encoded_part = g_squares[0, 5 * width :].reshape(parts, -1, width)
        g_squares = scattered(g_squares[0, : 5 * width].reshape(1, 1, 5, width, width)).reshape(parts, -1, width)
        g_squares = jnp.concatenate([g_squares, encoded_part], axis=1)
    g_squares = lax.psum_scatter(g_squares, CTX, scatter_dimension=0, tiled=False)
    encoded_grad = g_squares[shards * 5 * own :].astype(F32)
    g_squares = collect(g_squares[: shards * 5 * own].reshape(shards, 5 * own, width)).astype(BF)

    middle = prompt_tiles + (blocks * parts * BLK // TILE - prompt_tiles) // 4
    g_down = collect(after(g_down, dso)).astype(BF)
    held = sa_bwd(slots, own_table, qkv, dso, ot, lse, heads, prompt_tiles, 0, middle)
    second = after(dso, g_wide)
    g_wide = collect_far(g_wide).astype(BF)
    dqkv, dtable = sa_bwd(
        slots, own_table, qkv, second, ot, lse, heads, prompt_tiles, middle, blocks * parts * BLK // TILE, held
    )
    grads = after(dqkv, (g_down, g_wide)).reshape(parts * local, 3 * inner)
    g_qkv, self_gain_part = last_projection(gathered, gains[0], qkv_weight, grads, local)
    g_down = reduce_planes(g_down)
    dqkv = lax.all_to_all(dqkv.reshape(parts, local, 3 * inner), CTX, 0, 0, tiled=True)
    states_grad = final_back(dqkv, qkv_all, states[0], gains[0], dx1)

    table_part = jnp.zeros((BUCKETS, head_count), F32)
    table_part = lax.dynamic_update_slice_in_dim(table_part, dtable[:, :, 0].T, place * heads, 1)
    sums = [self_gain_part[:, 0] / gains[0][0], cross_gain_part[0], feed_gain_part[0]]
    sums = jnp.concatenate([v.reshape(shards, shard_width) for v in sums] + [table_part.reshape(shards, -1)], axis=1)
    sums = jnp.pad(sums, ((0, 0), (0, 16 * 3 * inner - small_width))).reshape(shards, 16, 3 * inner).astype(BF)
    last = jnp.concatenate([g_qkv.reshape(shards, shard_width, 3 * inner), sums], axis=1)
    last = lax.all_gather(collect(last).astype(BF), CTX, axis=0, tiled=False)
    sums = jnp.sum(last[:, shard_width:].reshape(parts, -1)[:, :small_width].astype(F32), axis=0)
    g_qkv = last[:, :shard_width].astype(F32).reshape(parts, shard_width, 3, inner).transpose(2, 1, 0, 3)
    g_qkv = g_qkv.reshape(3, shard_width, width)
    gain_grads = [sums[i * shard_width : (i + 1) * shard_width] for i in range(3)]
    table_grad = sums[3 * shard_width :].reshape(-1, head_count)
    g_wide = lax.all_gather(g_wide, CTX, axis=0, tiled=False).astype(F32)
    g_wide = g_wide.transpose(1, 0, 2, 3).reshape(2, shard_width, hidden_width)
    rest = lax.all_gather(jnp.concatenate([g_squares, g_down], axis=0), CTX, axis=0, tiled=False).astype(F32)
    g_squares = rest[:, : 5 * own].reshape(parts, 5, own, width).transpose(1, 0, 2, 3).reshape(5, shard_width, width)
    g_down = rest[:, 5 * own :].reshape(parts // 2, 2, -1, width).transpose(1, 0, 2, 3).reshape(-1, width)
    return (
        layer_out[None], states_grad[None], encoded_grad[None],
        gain_grads[0], g_qkv[0], g_qkv[1], g_qkv[2], g_squares[0], table_grad,
        gain_grads[1], g_squares[1], g_squares[3], g_squares[4], g_squares[2],
        gain_grads[2], g_wide[0], g_wide[1], g_down,
    )


def solution(mesh):
    ctx, fsdp = mesh.devices.shape
    split = Mesh(mesh.devices.reshape(ctx // 2, 2, fsdp), ("plane", "core", "fsdp"))
    tokens, matrix, vector = P("fsdp", CTX, None), P("fsdp", None), P("fsdp")
    place = P("fsdp", CTX)
    return jax.shard_map(
        on_device,
        mesh=split,
        in_specs=(tokens, place, place, tokens, tokens)
        + (vector, matrix, matrix, matrix, matrix, matrix)
        + (vector, matrix, matrix, matrix, matrix)
        + (vector, matrix, matrix, matrix),
        out_specs=(tokens, tokens, tokens)
        + (vector, matrix, matrix, matrix, matrix, matrix)
        + (vector, matrix, matrix, matrix, matrix)
        + (vector, matrix, matrix, matrix),
        check_vma=False,
    )
```

time: 1530 us -> 712 us (0.47)
  waiting for transfers between devices: 947 us -> 145 us
  matrix products: 144 us -> 0 us
  Pallas kernels: 130 us -> 269 us
  starting transfers between devices: 15.7 us -> 49.4 us
  local copies, waits for them, and re-layouts: 71.7 us -> 52.9 us
    reduce_scatter x19 -> x2, waiting for transfers between devices: 464 us -> 11 us  [the longest x1 11 us: on_device(): lax.psum_scatter(scattered(g_wide), CTX, scatter_dimension=0, tiled=False)]
    all_gather x14 -> x7, waiting for transfers between devices: 479 us -> 48.5 us  [the longest x1 43.8 us: on_device(): wide = lax.all_gather(after(wide, (squares, lse)), CTX, axis=0, tiled=False)]
    pallas_call x3 -> x10, Pallas kernels: 102 us -> 240 us  [the longest x2 80.2 us: sa_bwd(): pl.pallas_call(functools.partial(bwd_kernel, heads, prompt_tiles, unroll,...]
    dot_general x29 -> x0, matrix products: 135 us -> none  [the longest x8 44.5 us: project(): return jnp.einsum('td,de->te', left, right, preferred_element_type=F32)]
    all_to_all x1 -> x3, blocking collectives: 23.8 us -> 135 us  [the longest x1 58 us: on_device(): lax.all_to_all(dqkv.reshape(parts, local, 3 * inner), CTX, 0, 0, tiled=True)]
    all_gather x7 -> x0, blocking collectives: 85.1 us -> none  [the longest x5 50.6 us: reduce_all(): return lax.all_gather(g[0], CTX, axis=0, tiled=True).astype(F32)]
    all_to_all x0 -> x6, waiting for transfers between devices: none -> 45.2 us  [the longest x3 34.3 us: spread(): lax.all_to_all(jnp.broadcast_to(piece[None], (count,) + piece.shape), 'fs...]
    psum x1 -> x0, blocking collectives: 39.5 us -> none  [on_device(): sums = lax.psum(sums, CTX + ('fsdp',))]
  transfers between devices with their start and end apart: 34 -> 26, of which waited for: 28 -> 13; matrix products, arithmetic and copies ran while one was open for 13% -> 10% of each run, Pallas kernels for 9% -> 38%
where the time goes in v2:
time: 712 us; the launch traced here: 707 us
  Pallas kernels  269 us (38%)
  waiting for transfers between devices  145 us (20%)
  blocking collectives  143 us (20%)
  local copies, waits for them, and re-layouts  52.9 us (7%)
  starting transfers between devices  49.4 us (7%)
  other arithmetic  32.4 us (5%)
  between operations  15.5 us (2%)
    pallas_call x2, Pallas kernels, sa_bwd(): pl.pallas_call(functools.partial(bwd_kernel, heads, prompt_tiles, unroll,...  80.2 us
    all_to_all x1, blocking collectives, on_device(): lax.all_to_all(dqkv.reshape(parts, local, 3 * inner), CTX, 0, 0, tiled=True)  58 us
    all_gather x1, waiting for transfers between devices, on_device(): wide = lax.all_gather(after(wide, (squares, lse)), CTX, axis=0, tiled=False)  43.8 us
    all_to_all x1, blocking collectives, collect(): lax.all_to_all(parts, 'fsdp', 0, 0, tiled=True).astype(F32)  42.7 us
    pallas_call x1, Pallas kernels, feed_forward(): pl.pallas_call(feed_kernel, grid=(hidden // TILE,), out_shape=[tokens(BF)...  38.7 us
    all_to_all x3, waiting for transfers between devices, spread(): lax.all_to_all(jnp.broadcast_to(piece[None], (count,) + piece.shape), 'fs...  34.3 us
    all_to_all x1, blocking collectives, spread(): lax.all_to_all(jnp.broadcast_to(piece[None], (count,) + piece.shape), 'fs...  34 us
    pallas_call x1, Pallas kernels, middle_forward(): pl.pallas_call(functools.partial(middle_kernel, head_count), grid=(1,), o...  29.4 us
  transfers between devices with their start and end apart: 26, of which 13 were waited for; matrix products, arithmetic and copies ran while one was open for 10% of the time, Pallas kernels for 38%

profile of v2, /device:TPU:0, one launch (start us, length us, event | category | flops | bytes accessed | tf_op | source)
XLA Modules:
  0.0 707.1 jit_solution(15471631760592046313)
XLA Ops:
  7.3 2.5 pad_maximum_fusion.1
  12.1 6.3 all-to-all-start
  22.7 16.9 %all-to-all-done = bf16[4,272,384]{2,1,0:T(8,128)(2,1)S(1)} async-done(((bf16[4,272,384]{2,1,0:T(8,128)(2,1)}), bf16[4,272,384]{2,1,0:T(8,128)(2,1)S(1)}, u32[]{:S(2)}, u32[]{:S(2)}) %all-to-all-start) | async-done | bytes 835616 | tf_op jit(solution)/shard_map/all_to_all | solution.py:779
  39.7 34.0 %all_to_all.50 = bf16[4,5,32,1024]{3,2,1,0:T(8,128)(2,1)} all-to-all(bf16[4,5,32,1024]{3,2,1,0:T(8,128)(2,1)S(1)} %broadcast_in_dim.15), channel_id=1, replica_groups=mesh['plane'=4,'core'=2,'fsdp'=4] {'fsdp'}, dimensions={0} | all-to-all | bytes 2621440 | tf_op jit(solution)/shard_map/all_to_all | solution.py:779
  76.7 8.0 %all-reduce.2 = s32[32]{0:T(128)S(1)} all-reduce(s32[32]{0:T(128)S(1)} %fusion.25), channel_id=1, replica_groups=mesh['plane'=4,'core'=2,'fsdp'=4] {'plane','core'}, use_global_device_ids=true, to_apply=%add.2 | all-reduce | flops 32 | bytes 256
  90.6 3.6 all-to-all-start.3
  94.5 11.0 %first_projection.1 = bf16[4096,384]{1,0:T(8,128)(2,1)} custom-call(bf16[8,576,1024]{2,1,0:T(8,128)(2,1)} %bitcast.148, f32[1,1024]{1,0:T(1,128)} %bitcast.211, bf16[1024,384]{1,0:T(8,128)(2,1)} %bitcast.154), custom_call_target="tpu_custom_call" | custom-call | flops 3221225472 | bytes 11534336 | tf_op jit(solution)/shard_map/first_projection/pallas_call | solution.py:720
  105.5 28.6 %self_attention_forward.1 = (bf16[32,128,128]{2,1,0:T(8,128)(2,1)}, f32[128,4096]{1,0:T(8,128)}, f32[2,4096]{1,0:T(2,128)}) custom-call(s32[32]{0:T(128)} %get-tuple-element.57.slots, f32[64]{0:T(128)} %reshape.208.tab, bf16[32,128,384]{2,1,0:T(8,128)(2,1)} %bitcast.182), custom_call_target="tpu_custom_call" | custom-call | flops 32000000000 | bytes 12582912 | tf_op jit(solution)/shard_map/self_attention_forward/pallas_call | solution.py:131
  134.2 3.1 all-gather.17.cloned.1.call-done
  137.3 3.6 all-to-all-start.1
  140.9 20.3 %all-to-all-done.1.o_ref = bf16[8,512,128]{2,1,0:T(8,128)(2,1)S(1)} async-done(((bf16[8,512,128]{2,1,0:T(8,128)(2,1)}), bf16[8,512,128]{2,1,0:T(8,128)(2,1)S(1)}, u32[]{:S(2)}, u32[]{:S(2)}) %all-to-all-start.1) | async-done | bytes 1048608 | tf_op jit(solution)/shard_map/all_to_all | solution.py:908
  163.1 4.6 all-to-all-start.4
  167.8 43.8 %all-gather.19.cloned.1.call-done = bf16[32,2,32,2816]{3,2,1,0:T(8,128)(2,1)} async-done(((bf16[4,2,32,2816]{3,2,1,0:T(8,128)(2,1)}), bf16[32,2,32,2816]{3,2,1,0:T(8,128)(2,1)}) %all-gather.19.cloned.1.call-update) | async-done | bytes 11534352 | tf_op jit(solution)/shard_map/all_gather | solution.py:910
  212.2 17.4 %all-to-all-done.4 = bf16[4,352,1024]{2,1,0:T(8,128)(2,1)} async-done(((bf16[4,352,1024]{2,1,0:T(8,128)(2,1)}), bf16[4,352,1024]{2,1,0:T(8,128)(2,1)}, u32[]{:S(2)}, u32[]{:S(2)}) %all-to-all-start.4) | async-done | bytes 2883616 | tf_op jit(solution)/shard_map/all_to_all | solution.py:779
  235.2 3.1 select_bitcast_fusion.1
  238.3 3.0 pad_maximum_fusion
  241.2 5.4 source_projection.1.ckv_ref
  246.6 29.4 %middle_forward.1 = (bf16[512,1024]{1,0:T(8,128)(2,1)}, f32[512,1024]{1,0:T(8,128)}, bf16[512,1024]{1,0:T(8,128)(2,1)}, bf16[512,1024]{1,0:T(8,128)(2,1)}, f32[8...) custom-call(bf16[8,512,128]{2,1,0:T(8,128)(2,1)} %copy-done.5, ...), custom_call_target="tpu_custom_call" | custom-call | flops 32212254720 | bytes 12582912 | tf_op jit(solution)/shard_map/middle_forward/pallas_call | solution.py:439
  276.0 38.7 %feed_forward.1 = (bf16[512,1024]{1,0:T(8,128)(2,1)}, f32[512,1024]{1,0:T(8,128)}, f32[1,1024]{1,0:T(1,128)}, bf16[8,4,2,32,2816]{4,3,2,1,0:T(8,128)(2,1)}, bf16[2816,1024]{1,0:T(8,128)(2,1)}) custom-call(bf16[512,1024]{1,0:T(8,128)(2,1)} %get-tuple-element.61.n3_ref, bf16[512,1024]{1,0:T(8,128)(2,1)} %bitcast.222, f32[512,1024]{1,0:T(8,128)} %get-tuple-element.62.x2_ref, ...), custom_call_target="tpu_custom_call" | custom-call | flops 41339060224 | bytes 34603008 | tf_op jit(solution)/shard_map/feed_forward/pallas_call | solution.py:502
  315.0 27.8 %middle_back.1 = (f32[512,1024]{1,0:T(8,128)}, f32[1,1024]{1,0:T(1,128)}, bf16[512,1024]{1,0:T(8,128)(2,1)}, bf16[2,512,1024]{2,1,0:T(8,128)(2,1)}, bf16[8,512,128]{2,1,0:T(8,128)(2,1)}) custom-call(f32[512,1024]{1,0:T(8,128)} %get-tuple-element.70.dx2_ref, f32[512,1024]{1,0:T(8,128)} %get-tuple-element.71.x1_ref, f32[1,1024]{1,0:T(1,128)} %bitcast.216, ...), custom_call_target="tpu_custom_call" | custom-call | flops 32212254720 | bytes 12582912 | tf_op jit(solution)/shard_map/middle_back/pallas_call | solution.py:599
  342.7 22.5 %middle_grads.1 = bf16[8,704,1024]{2,1,0:T(8,128)(2,1)} custom-call(f32[512,1024]{1,0:T(8,128)} %get-tuple-element.70.dx2_ref, f32[512,1024]{1,0:T(8,128)} %get-tuple-element.71.x1_ref, f32[1,1024]{1,0:T(1,128)} %bitcast.217, bf16[512,1024]{1,0:T(8,128)(2,1)} %get-tuple-element.83.cob_ref, bf16[512,1024]{1,0:T(8,128)(2,1)} %get-tuple-element.84.dcq_ref, ...), custom_call_target="tpu_custom_call" | custom-call | flops 24696061952 | bytes 12582912 | tf_op jit(solution)/shard_map/middle_grads/pallas_call | solution.py:662
  365.3 3.7 dynamic-slice_bitcast_fusion
  369.2 3.6 all-to-all-start.5
  374.6 5.8 fusion
  380.4 8.3 %all-to-all-done.5 = bf16[8,512,128]{2,1,0:T(8,128)(2,1)S(1)} async-done(((bf16[8,512,128]{2,1,0:T(8,128)(2,1)}), bf16[8,512,128]{2,1,0:T(8,128)(2,1)S(1)}, u32[]{:S(2)}, u32[]{:S(2)}) %all-to-all-start.5) | async-done | bytes 1048608 | tf_op jit(solution)/shard_map/all_to_all | solution.py:924
  389.7 4.6 all-to-all-start.7
  394.3 11.0 %reduce-scatter.5.cloned.1.call-done = bf16[1,4,2,32,2816]{4,3,2,1,0:T(8,128)(2,1)} async-done(((bf16[8,4,2,32,2816]{4,3,2,1,0:T(8,128)(2,1)}), bf16[1,4,2,32,2816]{4,3,2,1,0:T(8,128)(2,1)}) %reduce-scatter.5.cloned.1.call-update) | async-done | bytes 1441808 | tf_op jit(solution)/shard_map/reduce_scatter | solution.py:919
  405.3 2.7 dynamic-slice_bitcast_fusion.7
  408.0 2.6 collective-permute-start.2
  410.6 40.3 %self_attention_backward.2 = (bf16[2560,128]{1,0:T(8,128)(2,1)}, f32[4096,256]{1,0:T(8,128)}, f32[2,2,128,128]{3,2,1,0:T(8,128)}, f32[2,8,256]{2,1,0:T(8,128)}) custom-call(s32[32]{0:T(128)} %get-tuple-element.57.slots, f32[64]{0:T(128)} %reshape.208.tab, bf16[32,128,384]{2,1,0:T(8,128)(2,1)} %bitcast.183, bf16[32,128,128]{2,1,0:T(8,128)(2,1)} %bitcast.202, ...), custom_call_target="tpu_custom_call" | custom-call | flops 43000000512 | bytes 18874368 | tf_op jit(solution)/shard_map/self_attention_backward/pallas_call | solution.py:268
  452.1 5.1 collective-permute-start.4
  458.6 6.4 collective-permute-start.6
  466.3 39.9 %self_attention_backward.3 = (bf16[32,128,384]{2,1,0:T(8,128)(2,1)}, f32[2,32,128]{2,1,0:T(8,128)}) custom-call(s32[32]{0:T(128)} %get-tuple-element.57.slots, f32[64]{0:T(128)} %reshape.208.tab, bf16[32,128,384]{2,1,0:T(8,128)(2,1)} %bitcast.184, bf16[32,128,128]{2,1,0:T(8,128)(2,1)} %bitcast.203, f32[128,4096]{1,0:T(8,128)} %get-tuple-element.76.ot_ref, ...), custom_call_target="tpu_custom_call" | custom-call | flops 43000000512 | bytes 18874368 | tf_op jit(solution)/shard_map/self_attention_backward/pallas_call | solution.py:268
  507.4 2.4 reduce_sum.45
  511.9 12.4 %last_projection.1 = (bf16[1024,384]{1,0:T(8,128)(2,1)}, f32[1024,1]{1,0:T(8,128)}) custom-call(bf16[8,576,1024]{2,1,0:T(8,128)(2,1)} %bitcast.150, f32[1,1024]{1,0:T(1,128)} %bitcast.212, bf16[1024,384]{1,0:T(8,128)(2,1)} %bitcast.156, bf16[4096,384]{1,0:T(8,128)(2,1)} %bitcast.158), custom_call_target="tpu_custom_call" | custom-call | flops 3221225472 | bytes 11534336 | tf_op jit(solution)/shard_map/last_projection/pallas_call | solution.py:758
  527.5 42.7 %all_to_all.51 = bf16[4,272,384]{2,1,0:T(8,128)(2,1)S(1)} all-to-all(bf16[4,272,384]{2,1,0:T(8,128)(2,1)S(1)} %pad_maximum_fusion.2), channel_id=1, replica_groups=mesh['plane'=4,'core'=2,'fsdp'=4] {'fsdp'}, dimensions={0} | all-to-all | bytes 1671168 | tf_op jit(solution)/shard_map/all_to_all | solution.py:783
  571.8 2.5 slice.163
  574.3 3.6 all-to-all-start.9
  578.1 7.4 %collective-permute-done.8 = bf16[2,88,1024]{2,1,0:T(8,128)(2,1)S(1)} collective-permute-done((bf16[2,88,1024]{2,1,0:T(8,128)(2,1)S(1)}, bf16[2,88,1024]{2,1,0:T(8,128)(2,1)S(1)}, u32[]{:S(2)}, u32[]{:S(2)}) %collective-permute-start.8) | collective-permute-done | bytes 360480 | tf_op jit(solution)/shard_map/ppermute | solution.py:841
  585.7 8.2 %collective-permute-done.9 = bf16[1,88,1024]{2,1,0:T(8,128)(2,1)S(1)} collective-permute-done((bf16[1,88,1024]{2,1,0:T(8,128)(2,1)S(1)}, bf16[1,88,1024]{2,1,0:T(8,128)(2,1)S(1)}, u32[]{:S(2)}, u32[]{:S(2)}) %collective-permute-start.9) | collective-permute-done | bytes 180256 | tf_op jit(solution)/shard_map/ppermute | solution.py:841
  593.9 2.6 all-to-all-done.9
  597.6 58.0 %all_to_all.52.d_ref = bf16[8,512,384]{2,1,0:T(8,128)(2,1)} all-to-all(bf16[8,512,384]{2,1,0:T(8,128)(2,1)} %bitcast.159), channel_id=1, replica_groups=mesh['plane'=4,'core'=2,'fsdp'=4] {'plane','core'}, dimensions={0} | all-to-all | bytes 6291456 | tf_op jit(solution)/shard_map/all_to_all | solution.py:945
  655.6 13.0 %final_back.1 = f32[512,1024]{1,0:T(8,128)} custom-call(bf16[8,512,384]{2,1,0:T(8,128)(2,1)} %all_to_all.52.d_ref, bf16[8,1024,384]{2,1,0:T(8,128)(2,1)} %bitcast.170, bf16[512,1024]{1,0:T(8,128)(2,1)} %bitcast.179, f32[1,1024]{1,0:T(1,128)} %bitcast.213, f32[512,1024]{1,0:T(8,128)} %get-tuple-element.82.dx1_ref), custom_call_target="tpu_custom_call" | custom-call | flops 3221225472 | bytes 6291456 | tf_op jit(solution)/shard_map/final_back/pallas_call | solution.py:693
  668.6 3.3 slice_convert_fusion
  671.9 3.6 copy.80
  686.3 3.1 fusion.27
  692.6 2.5 slice.164
  695.9 2.5 fusion.28
  (153 shorter events, 56.6 us)
Async XLA Ops:
  7.2 154.0 %copy-start = (bf16[704,1024]{1,0:T(8,128)(2,1)S(1)}, bf16[704,1024]{1,0:T(8,128)(2,1)}, u32[]{:S(2)}) copy-start(bf16[704,1024]{1,0:T(8,128)(2,1)} %param.39) | copy-start | bytes 4325380
  7.2 2.7 copy-start.6
  7.2 2.9 copy-start.7
  7.2 3.1 copy-start.8
  7.2 66.5 %all-gather.15.cloned.1.call-start = ((), (), s32[]{:S(2)}) async-start(), calls=%async_computation.14 | async-start | bytes 10616832 | tf_op jit(solution)/shard_map/all_gather | solution.py:877
  7.3 3.3 copy-start.12
  7.3 3.4 copy-start.13
  7.3 3.3 copy-start.14
  7.3 3.3 copy-start.15
  12.1 27.5 %all-to-all-start = ((bf16[4,272,384]{2,1,0:T(8,128)(2,1)}), bf16[4,272,384]{2,1,0:T(8,128)(2,1)S(1)}, u32[]{:S(2)}, u32[]{:S(2)}) async-start(bf16[4,272,384]{2,1,0:T(8,128)(2,1)} %broadcast_in_dim.14), calls=%async_computation | async-start | bytes 1671168 | tf_op jit(solution)/shard_map/all_to_all | solution.py:779
  18.4 118.9 %all-gather.17.cloned.1.call-start = ((), (), s32[]{:S(2)}) async-start(), calls=%async_computation.15 | async-start | bytes 11796480 | tf_op jit(solution)/shard_map/all_gather | solution.py:903
  21.8 53.5 %copy-start.16 = (u32[32]{0:T(128)S(1)}, u32[32]{0:T(128)}, u32[]{:S(2)}) copy-start(u32[32]{0:T(128)} %constant.175) | copy-start | bytes 388
  86.5 0.6 copy-start.9
  90.6 43.6 %all-to-all-start.3 = ((bf16[4,2,32,2816]{3,2,1,0:T(8,128)(2,1)}), bf16[4,2,32,2816]{3,2,1,0:T(8,128)(2,1)S(1)}, u32[]{:S(2)}, u32[]{:S(2)}) async-start(bf16[4,2,32,2816]{3,2,1,0:T(8,128)(2,1)} %broadcast_in_dim.16), calls=%async_computation.3 | async-start | bytes 2883584 | tf_op jit(solution)/shard_map/all_to_all | solution.py:779
  94.2 117.4 %all-gather.19.cloned.1.call-start = ((), (), s32[]{:S(2)}) async-start(), calls=%async_computation.16 | async-start | bytes 12976128 | tf_op jit(solution)/shard_map/all_gather | solution.py:910
  134.2 3.1 copy-start.3
  137.3 23.8 %all-to-all-start.1 = ((bf16[8,512,128]{2,1,0:T(8,128)(2,1)}), bf16[8,512,128]{2,1,0:T(8,128)(2,1)S(1)}, u32[]{:S(2)}, u32[]{:S(2)}) async-start(bf16[8,512,128]{2,1,0:T(8,128)(2,1)} %bitcast.204), calls=%async_computation.1 | async-start | bytes 2097152 | tf_op jit(solution)/shard_map/all_to_all | solution.py:908
  161.1 2.0 copy-start.5
  163.1 66.4 %all-to-all-start.4 = ((bf16[4,352,1024]{2,1,0:T(8,128)(2,1)}), bf16[4,352,1024]{2,1,0:T(8,128)(2,1)}, u32[]{:S(2)}, u32[]{:S(2)}) async-start(bf16[4,352,1024]{2,1,0:T(8,128)(2,1)} %broadcast_in_dim.17), calls=%async_computation.4 | async-start | bytes 5767168 | tf_op jit(solution)/shard_map/all_to_all | solution.py:779
  167.8 147.2 %all-gather.21.cloned.1.call-start = ((), (), s32[]{:S(2)}) async-start(), calls=%async_computation.17 | async-start | bytes 7077888 | tf_op jit(solution)/shard_map/all_gather | solution.py:911
  211.6 193.7 %reduce-scatter.5.cloned.1.call-start = ((), (), s32[]{:S(2)}) async-start(), calls=%async_computation.13 | async-start | bytes 12976128 | tf_op jit(solution)/shard_map/reduce_scatter | solution.py:919
  229.6 5.6 collective-permute-start
  314.7 257.1 %reduce-scatter.3.cloned.1.call-start = ((), (), s32[]{:S(2)}) async-start(), calls=%async_computation.12 | async-start | bytes 12976128 | tf_op jit(solution)/shard_map/reduce_scatter | solution.py:930
  365.3 7.5 %copy-start.10 = (f32[1,1024]{1,0:T(1,128)S(1)}, f32[1,1024]{1,0:T(1,128)}, u32[]{:S(2)}) copy-start(f32[1,1024]{1,0:T(1,128)} %get-tuple-element.94) | copy-start | bytes 12292
  368.9 5.6 collective-permute-start.1
  369.2 19.5 %all-to-all-start.5 = ((bf16[8,512,128]{2,1,0:T(8,128)(2,1)}), bf16[8,512,128]{2,1,0:T(8,128)(2,1)S(1)}, u32[]{:S(2)}, u32[]{:S(2)}) async-start(bf16[8,512,128]{2,1,0:T(8,128)(2,1)} %get-tuple-element.75), calls=%async_computation.5 | async-start | bytes 2097152 | tf_op jit(solution)/shard_map/all_to_all | solution.py:924
  372.8 7.6 %copy-start.11 = (f32[1,1024]{1,0:T(1,128)S(1)}, f32[1,1024]{1,0:T(1,128)}, u32[]{:S(2)}) copy-start(f32[1,1024]{1,0:T(1,128)} %get-tuple-element.93) | copy-start | bytes 12292
  388.7 1.0 copy-start.4
  389.7 117.7 %all-to-all-start.7 = ((bf16[4,352,1024]{2,1,0:T(8,128)(2,1)}), bf16[4,352,1024]{2,1,0:T(8,128)(2,1)}, u32[]{:S(2)}, u32[]{:S(2)}) async-start(bf16[4,352,1024]{2,1,0:T(8,128)(2,1)} %fusion), calls=%async_computation.8 | async-start | bytes 5767168 | tf_op jit(solution)/shard_map/all_to_all | solution.py:783
  394.3 274.4 %all-gather.23.cloned.1.call-start = ((), (), s32[]{:S(2)}) async-start(), calls=%async_computation.18 | async-start | bytes 1880064 | tf_op jit(solution)/shard_map/all_gather | solution.py:954
  408.0 57.0 %collective-permute-start.2 = (bf16[2,32,2816]{2,1,0:T(8,128)(2,1)S(1)}, bf16[2,32,2816]{2,1,0:T(8,128)(2,1)S(1)}, u32[]{:S(2)}, u32[]{:S(2)}) collective-permute-start(bf16[2,32,2816]{2,1,0:T(8,128)(2,1)S(1)} %get-tuple-element.180), channel_id=1, source_target_pairs={{0,1},{1,2},{2,3},{4,5},{5,6},{6,7},{8,9},{9,10},{10,11},{12,13},{... | collective-permute-start | bytes 1081352 | tf_op jit(solution)/shard_map/ppermute | solution.py:795
  450.9 59.0 %collective-permute-start.3 = (bf16[2,32,2816]{2,1,0:T(8,128)(2,1)}, bf16[2,32,2816]{2,1,0:T(8,128)(2,1)S(1)}, u32[]{:S(2)}, u32[]{:S(2)}) collective-permute-start(bf16[2,32,2816]{2,1,0:T(8,128)(2,1)} %get-tuple-element.185), channel_id=1, source_target_pairs={{1,0},{2,1},{3,2},{5,4},{6,5},{7,6},{9,8},{10,9},{11,10},{13,12},{... | collective-permute-start | bytes 1081352 | tf_op jit(solution)/shard_map/ppermute | solution.py:795
  452.1 57.7 %collective-permute-start.4 = (bf16[2,32,2816]{2,1,0:T(8,128)(2,1)}, bf16[2,32,2816]{2,1,0:T(8,128)(2,1)S(1)}, u32[]{:S(2)}, u32[]{:S(2)}) collective-permute-start(bf16[2,32,2816]{2,1,0:T(8,128)(2,1)} %get-tuple-element.184), channel_id=1, source_target_pairs={{0,2},{1,3},{4,6},{5,7},{8,10},{9,11},{12,14},{13,15},{16,18},{17,... | collective-permute-start | bytes 1081352 | tf_op jit(solution)/shard_map/ppermute | solution.py:795
  457.3 52.6 %collective-permute-start.5 = (bf16[2,32,2816]{2,1,0:T(8,128)(2,1)}, bf16[2,32,2816]{2,1,0:T(8,128)(2,1)S(1)}, u32[]{:S(2)}, u32[]{:S(2)}) collective-permute-start(bf16[2,32,2816]{2,1,0:T(8,128)(2,1)} %get-tuple-element.183), channel_id=1, source_target_pairs={{2,0},{3,1},{6,4},{7,5},{10,8},{11,9},{14,12},{15,13},{18,16},{19,... | collective-permute-start | bytes 1081352 | tf_op jit(solution)/shard_map/ppermute | solution.py:795
  458.6 51.3 %collective-permute-start.6 = (bf16[2,32,2816]{2,1,0:T(8,128)(2,1)}, bf16[2,32,2816]{2,1,0:T(8,128)(2,1)S(1)}, u32[]{:S(2)}, u32[]{:S(2)}) collective-permute-start(bf16[2,32,2816]{2,1,0:T(8,128)(2,1)} %get-tuple-element.182), channel_id=1, source_target_pairs={{0,3},{4,7},{8,11},{12,15},{16,19},{20,23},{24,27},{28,31}} | collective-permute-start | bytes 1081352 | tf_op jit(solution)/shard_map/ppermute | solution.py:795
  465.0 44.9 %collective-permute-start.7 = (bf16[2,32,2816]{2,1,0:T(8,128)(2,1)S(1)}, bf16[2,32,2816]{2,1,0:T(8,128)(2,1)S(1)}, u32[]{:S(2)}, u32[]{:S(2)}) collective-permute-start(bf16[2,32,2816]{2,1,0:T(8,128)(2,1)S(1)} %get-tuple-element.181), channel_id=1, source_target_pairs={{3,0},{7,4},{11,8},{15,12},{19,16},{23,20},{27,24},{31,28}} | collective-permute-start | bytes 1081352 | tf_op jit(solution)/shard_map/ppermute | solution.py:795
  571.0 112.8 %all-gather.27.cloned.1.call-start = ((), (), s32[]{:S(2)}) async-start(), calls=%async_computation.20 | async-start | bytes 3244032 | tf_op jit(solution)/shard_map/all_gather | solution.py:960
  574.3 22.3 %all-to-all-start.9 = ((bf16[4,160,1024]{2,1,0:T(8,128)(2,1)}), bf16[4,160,1024]{2,1,0:T(8,128)(2,1)S(1)}, u32[]{:S(2)}, u32[]{:S(2)}) async-start(bf16[4,160,1024]{2,1,0:T(8,128)(2,1)} %bitcast.54), calls=%async_computation.11 | async-start | bytes 2621440 | tf_op jit(solution)/shard_map/all_to_all | solution.py:783
  577.8 114.7 %all-gather.25.cloned.1.call-start = ((), (), s32[]{:S(2)}) async-start(), calls=%async_computation.19 | async-start | bytes 4571136 | tf_op jit(solution)/shard_map/all_gather | solution.py:962
  578.0 7.5 %collective-permute-start.8 = (bf16[2,88,1024]{2,1,0:T(8,128)(2,1)S(1)}, bf16[2,88,1024]{2,1,0:T(8,128)(2,1)S(1)}, u32[]{:S(2)}, u32[]{:S(2)}) collective-permute-start(bf16[2,88,1024]{2,1,0:T(8,128)(2,1)S(1)} %dynamic-slice_bitcast_fusion.1), channel_id=1, source_target_pairs={{0,8},{8,0},{16,24},{24,16},{1,9},{9,1},{17,25},{25,17},{2,10},{10... | collective-permute-start | bytes 1081352 | tf_op jit(solution)/shard_map/ppermute | solution.py:841
  585.6 8.3 %collective-permute-start.9 = (bf16[1,88,1024]{2,1,0:T(8,128)(2,1)S(1)}, bf16[1,88,1024]{2,1,0:T(8,128)(2,1)S(1)}, u32[]{:S(2)}, u32[]{:S(2)}) collective-permute-start(bf16[1,88,1024]{2,1,0:T(8,128)(2,1)S(1)} %constant_dynamic-slice_fusion), channel_id=1, source_target_pairs={{0,16},{8,24},{16,0},{24,8},{1,17},{9,25},{17,1},{25,9},{2,18},{10... | collective-permute-start | bytes 540680 | tf_op jit(solution)/shard_map/ppermute | solution.py:841
  692.6 2.9 copy-start.2
  698.4 1.9 copy-start.1
Sparse Core Ops, SparseCore 0:
  10.5 61.5 all-gather.14
  74.0 63.2 all-gather.16
  139.7 71.7 all-gather.18
  213.9 45.5 all-gather.20
  314.8 90.4 reduce-scatter.4
  408.7 85.6 reduce-scatter.2
  571.1 26.0 all-gather.22
  599.7 54.1 all-gather.26
  656.3 36.2 all-gather.24

commit v3 on v2

--- a/solution.py
+++ b/solution.py
@@ -453,9 +453,14 @@
 
 
 def feed_kernel(
-    n3_ref, cot_ref, x2_ref, gain_ref, w_ref, wd_ref,
-    out_ref, dx2_ref, gain_out_ref, gw_ref, gd_ref, n3t, acc, dn, wg, wu,
+    core_ref, n3_ref, cot_ref, x2_ref, gain_ref, w_ref, mine_ref, other_ref,
+    out_ref, dx2_ref, gain_out_ref, gw_ref, keep_ref, give_ref, n3t, acc, dn, wg, wu, down,
 ):
+    half = mine_ref.shape[1]
+    own_half = pl.ds(pl.multiple_of(core_ref[0] * half, half), half)
+    other_half = pl.ds(pl.multiple_of((1 - core_ref[0]) * half, half), half)
+    down[:, own_half] = mine_ref[...]
+    down[:, other_half] = other_ref[...]
     step = pl.program_id(0)
 
     @pl.when(step == 0)
@@ -470,7 +475,7 @@
             start = (z * parts + c) * rows
             wg[start : start + rows, :] = w_ref[c, z, 0]
             wu[start : start + rows, :] = w_ref[c, z, 1]
-    n3, cot, wd = n3_ref[...], cot_ref[...], wd_ref[...]
+    n3, cot, wd = n3_ref[...], cot_ref[...], down[...]
     gate, up = nn(n3, wg[...]), nn(n3, wu[...])
     dh = nt(cot, wd)
     t = jnp.tanh(gelu_scale * (gate + 0.044715 * gate * gate * gate))
@@ -480,7 +485,9 @@
     dgate = (dh * up * slope).astype(BF)
     dup = (dh * gelu).astype(BF)
     acc[...] += nn(hidden, wd)
-    gd_ref[...] = nn(jnp.transpose(hidden, (1, 0)), cot).astype(BF)
+    down[...] = nn(jnp.transpose(hidden, (1, 0)), cot).astype(BF)
+    keep_ref[...] = down[:, own_half]
+    give_ref[...] = down[:, other_half]
     everything = slice(None)
     store_grad(gw_ref, 0, everything, nn(n3t[...], dgate).astype(BF))
     store_grad(gw_ref, 1, everything, nn(n3t[...], dup).astype(BF))
@@ -494,34 +501,35 @@
         dx2_ref[...] = cot_ref[...].astype(F32) + dv
 
 
-def feed_forward(n3, cot, x2, gain, wide, down):
+def feed_forward(core, n3, cot, x2, gain, wide, mine, other):
     rows, width = n3.shape
     parts, shards, _, own, hidden = wide.shape
     tokens = lambda dtype: jax.ShapeDtypeStruct((rows, width), dtype)
+    part = pl.BlockSpec((TILE, width // 2), lambda i: (i, 0))
     piece = pl.BlockSpec((parts, shards, 2, own, TILE), lambda i: (0, 0, 0, 0, i))
     return pl.pallas_call(
         feed_kernel,
         grid=(hidden // TILE,),
         out_shape=[
             tokens(BF), tokens(F32), jax.ShapeDtypeStruct((1, width), F32),
-            jax.ShapeDtypeStruct(wide.shape, BF), jax.ShapeDtypeStruct(down.shape, BF),
+            jax.ShapeDtypeStruct(wide.shape, BF), jax.ShapeDtypeStruct(mine.shape, BF), jax.ShapeDtypeStruct(mine.shape, BF),
         ],
         in_specs=[
-            whole((rows, width)), whole((rows, width)), whole((rows, width)), whole((1, width)),
-            piece, pl.BlockSpec((TILE, width), lambda i: (i, 0)),
+            pl.BlockSpec(memory_space=pltpu.SMEM),
+            whole((rows, width)), whole((rows, width)), whole((rows, width)), whole((1, width)), piece, part, part,
         ],
         out_specs=[
             whole((rows, width)), whole((rows, width)), whole((1, width)),
-            piece, pl.BlockSpec((TILE, width), lambda i: (i, 0)),
+            piece, part, part,
         ],
         scratch_shapes=[
             pltpu.VMEM((width, rows), BF), pltpu.VMEM((rows, width), F32), pltpu.VMEM((rows, width), F32),
-            pltpu.VMEM((width, TILE), BF), pltpu.VMEM((width, TILE), BF),
+            pltpu.VMEM((width, TILE), BF), pltpu.VMEM((width, TILE), BF), pltpu.VMEM((TILE, width), BF),
         ],
         compiler_params=params(),
         cost_estimate=cost(28 * rows * width * hidden, 12 * width * hidden),
         name="feed_forward",
-    )(n3, cot, x2, gain, wide, down)
+    )(core, n3, cot, x2, gain, wide, mine, other)
 
 
 def middle_back_kernel(
@@ -771,6 +779,38 @@
     )(gathered, gain, weight, grads)
 
 
+def unpack_kernel(own, rest_ref, last_ref, *outs):
+    parts = rest_ref.shape[0]
+    down = outs[5].shape[0] // parts
+    rows, inner = outs[0].shape[0], last_ref.shape[2] // 3
+    for c in range(parts):
+        for i in range(5):
+            outs[i][c * own : (c + 1) * own, :] = rest_ref[c, i * own : (i + 1) * own, :].astype(F32)
+        half = rest_ref.shape[2] // 2
+        for i in range(2):
+            start = ((c // 2) * 2 + i) * down
+            value = rest_ref[c, 5 * own : 5 * own + down, i * half : (i + 1) * half]
+            outs[5][start : start + down, (c % 2) * half : (c % 2 + 1) * half] = value.astype(F32)
+        for i in range(3):
+            outs[6 + i][:, c * inner : (c + 1) * inner] = last_ref[c, 0:rows, i * inner : (i + 1) * inner].astype(F32)
+
+
+def unpack(rest, last, own, down_rows):
+    parts, _, width = rest.shape
+    square = jax.ShapeDtypeStruct((own * parts, width), F32)
+    shapes = [square] * 5 + [jax.ShapeDtypeStruct((down_rows, width), F32)] + [square] * 3
+    return pl.pallas_call(
+        functools.partial(unpack_kernel, own),
+        grid=(1,),
+        out_shape=shapes,
+        in_specs=[whole(rest.shape), whole(last.shape)],
+        out_specs=[whole(v.shape) for v in shapes],
+        compiler_params=params(),
+        cost_estimate=cost(0, 6 * rest.size),
+        name="unpack",
+    )(rest, last)
+
+
 CTX = ("plane", "core")
 
 
@@ -779,14 +819,17 @@
     return lax.all_to_all(jnp.broadcast_to(piece[None], (count,) + piece.shape), "fsdp", 0, 0, tiled=True)
 
 
-def collect(parts):
-    return jnp.sum(lax.all_to_all(parts, "fsdp", 0, 0, tiled=True).astype(F32), axis=0)
+def collect(parts, *earlier):
+    parts = lax.all_to_all(parts, "fsdp", 0, 0, tiled=True)
+    if earlier:
+        parts = after(parts, *earlier)
+    return jnp.sum(parts.astype(F32), axis=0).astype(BF)
 
 
 def collect_far(parts):
     count, mine = lax.axis_size("fsdp"), lax.axis_index("fsdp")
     if count > 4:
-        return collect(parts)
+        return collect(parts).astype(F32)
     total = take(parts, mine, 0).astype(F32)
     for step in range(1, count):
         for sign in (1, -1):
@@ -796,8 +839,19 @@
     return total
 
 
-def after(value, earlier):
-    return lax.optimization_barrier((value, earlier))[0]
+def nothing(*refs):
+    pass
+
+
+def after(value, *earlier):
+    return pl.pallas_call(
+        nothing,
+        out_shape=jax.ShapeDtypeStruct(value.shape, value.dtype),
+        in_specs=[pl.BlockSpec(memory_space=pl.ANY)] * (1 + len(earlier)),
+        out_specs=pl.BlockSpec(memory_space=pl.ANY),
+        input_output_aliases={0: 0},
+        name="after",
+    )(value, *earlier)
 
 
 def own_rows(shard):
@@ -814,20 +868,10 @@
 
 
 def gather_down(shard):
-    core = lax.axis_index("core")
     rows, width = shard.shape
-    mine = spread(lax.dynamic_slice_in_dim(shard, core * (rows // 2), rows // 2, 0))
-    other = swap(mine, "core")
-    first = jnp.where(core == 0, mine, other)
-    second = jnp.where(core == 0, other, mine)
-    return jnp.stack([first, second], axis=1).reshape(-1, width)
-
-
-def share_down(grad):
-    shards, core = lax.axis_size("fsdp"), lax.axis_index("core")
-    halves = grad.reshape(shards, 2, -1, grad.shape[1])
-    other = swap(take(halves, 1 - core, 1), "core")
-    return (take(halves, core, 1).astype(F32) + other.astype(F32)).astype(BF)
+    start = lax.axis_index("core") * (width // 2)
+    mine = spread(lax.dynamic_slice_in_dim(shard, start, width // 2, 1)).reshape(-1, width // 2)
+    return mine, swap(mine, "core")
 
 
 def reduce_planes(half):
@@ -898,26 +942,28 @@
     slots = jnp.argmax(canon_all[None, :] == jnp.arange(blocks * parts)[:, None], axis=1).astype(jnp.int32)
 
     squares = jnp.stack([own_rows(w) for w in (self_output, cross_query, cross_output, cross_key, cross_value)], axis=0)
-    squares = spread(after(squares, line))
+    squares = spread(after(squares, line, slots))
     wide = spread(after(jnp.stack([own_rows(gate_weight), own_rows(up_weight)], axis=0), squares))
-    squares = lax.all_gather(after(squares, gathered), CTX, axis=0, tiled=False)
+    squares = lax.all_gather(squares, CTX, axis=0, tiled=False)
 
     prompt_tiles = PROMPT // TILE
     qkv = first_projection(gathered, gains[0], qkv_weight, local).reshape(parts * blocks, BLK, 3 * inner)
     o, ot, lse = sa_fwd(slots, own_table, qkv, heads, prompt_tiles)
     o = lax.all_to_all(o.reshape(parts, local, inner), CTX, 0, 0, tiled=True)
 
-    wide = lax.all_gather(after(wide, (squares, lse)), CTX, axis=0, tiled=False)
-    qkv_all = lax.all_gather(after(qkv_weight, wide), CTX, axis=0, tiled=False)
+    wide = lax.all_gather(after(wide, o), CTX, axis=0, tiled=False)
     squares, wide = arranged(squares), arranged(wide)
-    down = gather_down(after(down_weight, o))
+    down, other_down = gather_down(after(down_weight, o))
     ckv = source_projection(encoded_all, squares)
     ob, x1, cq, cob, cot, cross_lse, x2, n3 = middle_forward(
         o, states[0], gains[1], gains[2], squares, ckv, head_count
     )
-    layer_out, dx2, feed_gain_part, g_wide, g_down = feed_forward(n3, cotangent[0], x2, gains[2], wide, down)
+    qkv_all = lax.all_gather(after(qkv_weight, x2), CTX, axis=0, tiled=False)
+    layer_out, dx2, feed_gain_part, g_wide, g_down, g_other = feed_forward(
+        lax.axis_index("core").astype(jnp.int32).reshape(1), n3, cotangent[0], x2, gains[2], wide, down, other_down
+    )
     g_wide = lax.psum_scatter(scattered(g_wide), CTX, scatter_dimension=0, tiled=False)
-    g_down = share_down(g_down)
+    g_down = (g_down.astype(F32) + swap(g_other, "core").astype(F32)).astype(BF).reshape(shards, -1, width // 2)
     dx1, cross_gain_part, dcq, dckv, dso = middle_back(
         after(dx2, qkv_all), x1, gains[1], squares, cq, ckv, cot, cross_lse, head_count, parts
     )
@@ -927,44 +973,50 @@
         encoded_part = g_squares[0, 5 * width :].reshape(parts, -1, width)
         g_squares = scattered(g_squares[0, : 5 * width].reshape(1, 1, 5, width, width)).reshape(parts, -1, width)
         g_squares = jnp.concatenate([g_squares, encoded_part], axis=1)
+    middle = prompt_tiles + (blocks * parts * BLK // TILE - prompt_tiles) // 4
+    held = sa_bwd(slots, own_table, qkv, after(dso, g_down, g_squares), ot, lse, heads, prompt_tiles, 0, middle)
     g_squares = lax.psum_scatter(g_squares, CTX, scatter_dimension=0, tiled=False)
-    encoded_grad = g_squares[shards * 5 * own :].astype(F32)
-    g_squares = collect(g_squares[: shards * 5 * own].reshape(shards, 5 * own, width)).astype(BF)
-
-    middle = prompt_tiles + (blocks * parts * BLK // TILE - prompt_tiles) // 4
-    g_down = collect(after(g_down, dso)).astype(BF)
-    held = sa_bwd(slots, own_table, qkv, dso, ot, lse, heads, prompt_tiles, 0, middle)
-    second = after(dso, g_wide)
-    g_wide = collect_far(g_wide).astype(BF)
+    g_down = collect(after(g_down, dso), held[0])
     dqkv, dtable = sa_bwd(
-        slots, own_table, qkv, second, ot, lse, heads, prompt_tiles, middle, blocks * parts * BLK // TILE, held
+        slots, own_table, qkv, after(dso, g_wide), ot, lse, heads, prompt_tiles, middle,
+        blocks * parts * BLK // TILE, held,
     )
-    grads = after(dqkv, (g_down, g_wide)).reshape(parts * local, 3 * inner)
+    g_wide = collect(after(g_wide, g_down), dqkv)
+    g_squares = after(g_squares, g_wide)
+    g_squares_sum = collect(g_squares[: shards * 5 * own].reshape(shards, 5 * own, width))
+    dqkv_local = lax.all_to_all(after(dqkv, g_squares_sum).reshape(parts, local, 3 * inner), CTX, 0, 0, tiled=True)
+    states_grad = final_back(dqkv_local, qkv_all, states[0], gains[0], dx1)
+    g_wide = lax.all_gather(g_wide, CTX, axis=0, tiled=False)
+    grads = dqkv.reshape(parts * local, 3 * inner)
     g_qkv, self_gain_part = last_projection(gathered, gains[0], qkv_weight, grads, local)
     g_down = reduce_planes(g_down)
-    dqkv = lax.all_to_all(dqkv.reshape(parts, local, 3 * inner), CTX, 0, 0, tiled=True)
-    states_grad = final_back(dqkv, qkv_all, states[0], gains[0], dx1)
-
+    encoded_grad = g_squares[shards * 5 * own :].astype(F32)
     table_part = jnp.zeros((BUCKETS, head_count), F32)
     table_part = lax.dynamic_update_slice_in_dim(table_part, dtable[:, :, 0].T, place * heads, 1)
     sums = [self_gain_part[:, 0] / gains[0][0], cross_gain_part[0], feed_gain_part[0]]
     sums = jnp.concatenate([v.reshape(shards, shard_width) for v in sums] + [table_part.reshape(shards, -1)], axis=1)
     sums = jnp.pad(sums, ((0, 0), (0, 16 * 3 * inner - small_width))).reshape(shards, 16, 3 * inner).astype(BF)
     last = jnp.concatenate([g_qkv.reshape(shards, shard_width, 3 * inner), sums], axis=1)
-    last = lax.all_gather(collect(last).astype(BF), CTX, axis=0, tiled=False)
+    last = collect_far(last).astype(BF)
+    g_down = jnp.concatenate([g_down[: g_down.shape[0] // 2], g_down[g_down.shape[0] // 2 :]], axis=1)
+    rest = jnp.concatenate([g_squares_sum, g_down], axis=0)
+    rest = lax.all_gather(after(rest, g_wide), CTX, axis=0, tiled=False)
+    last = lax.all_gather(after(last, rest, dqkv_local), CTX, axis=0, tiled=False)
     sums = jnp.sum(last[:, shard_width:].reshape(parts, -1)[:, :small_width].astype(F32), axis=0)
-    g_qkv = last[:, :shard_width].astype(F32).reshape(parts, shard_width, 3, inner).transpose(2, 1, 0, 3)
-    g_qkv = g_qkv.reshape(3, shard_width, width)
     gain_grads = [sums[i * shard_width : (i + 1) * shard_width] for i in range(3)]
     table_grad = sums[3 * shard_width :].reshape(-1, head_count)
-    g_wide = lax.all_gather(g_wide, CTX, axis=0, tiled=False).astype(F32)
-    g_wide = g_wide.transpose(1, 0, 2, 3).reshape(2, shard_width, hidden_width)
-    rest = lax.all_gather(jnp.concatenate([g_squares, g_down], axis=0), CTX, axis=0, tiled=False).astype(F32)
-    g_squares = rest[:, : 5 * own].reshape(parts, 5, own, width).transpose(1, 0, 2, 3).reshape(5, shard_width, width)
-    g_down = rest[:, 5 * own :].reshape(parts // 2, 2, -1, width).transpose(1, 0, 2, 3).reshape(-1, width)
+    g_wide = g_wide.astype(F32).transpose(1, 0, 2, 3).reshape(2, shard_width, hidden_width)
+    if aligned:
+        *g_squares, g_down, g_query, g_key, g_value = unpack(rest, last, own, down_weight.shape[0])
+    else:
+        rest = rest.astype(F32)
+        g_squares = rest[:, : 5 * own].reshape(parts, 5, own, width).transpose(1, 0, 2, 3).reshape(5, shard_width, width)
+        g_down = rest[:, 5 * own :].reshape(parts // 2, 2, -1, 2, width // 2).transpose(0, 3, 2, 1, 4).reshape(-1, width)
+        g_qkv = last[:, :shard_width].astype(F32).reshape(parts, shard_width, 3, inner).transpose(2, 1, 0, 3)
+        g_query, g_key, g_value = g_qkv.reshape(3, shard_width, width)
     return (
         layer_out[None], states_grad[None], encoded_grad[None],
-        gain_grads[0], g_qkv[0], g_qkv[1], g_qkv[2], g_squares[0], table_grad,
+        gain_grads[0], g_query, g_key, g_value, g_squares[0], table_grad,
         gain_grads[1], g_squares[1], g_squares[3], g_squares[4], g_squares[2],
         gain_grads[2], g_wide[0], g_wide[1], g_down,
     )

time: 712 us -> 618 us (0.87)
  blocking collectives: 143 us -> 64.8 us
  waiting for transfers between devices: 145 us -> 117 us
  starting transfers between devices: 49.4 us -> 61.3 us
  other arithmetic: 32.4 us -> 22 us
  Pallas kernels: 269 us -> 279 us
    all_to_all x2 -> x1, blocking collectives: 101 us -> 22.5 us  [on_device(): o = lax.all_to_all(o.reshape(parts, local, inner), CTX, 0, 0, tiled=True)]
    all_gather x6, waiting for transfers between devices: 48.5 us -> 7.74 us  [the longest x1 7.72 us: on_device(): lax.all_gather(after(last, rest, dqkv_local), CTX, axis=0, tiled=False)]
    unnamed x55 -> x86, local copies, waits for them, and re-layouts: 13.3 us -> 31 us
    reduce_scatter x1, waiting for transfers between devices: 11 us -> 0.01 us  [on_device(): lax.psum_scatter(scattered(g_wide), CTX, scatter_dimension=0, tiled=False)]
    all_to_all x3 -> x4, waiting for transfers between devices: 22.9 us -> 33.7 us  [the longest x3 29.1 us: collect(): parts = lax.all_to_all(parts, 'fsdp', 0, 0, tiled=True)]
    ppermute x6, waiting for transfers between devices: 0.02 us -> 8.73 us  [collect_far(): total = total + lax.ppermute(message, 'fsdp', pairs).astype(F32)]
    slice x4 -> x1, local copies, waits for them, and re-layouts: 7.5 us -> 0.01 us  [on_device(): g_down[:g_down.shape[0] // 2]]
    pallas_call x0 -> x17, Pallas kernels: none -> 7.27 us  [the longest x1 7.26 us: unpack(): pl.pallas_call(functools.partial(unpack_kernel, own), grid=(1,), out_shap...]
  transfers between devices with their start and end apart: 26 -> 27, of which waited for: 13 -> 13; matrix products, arithmetic and copies ran while one was open for 10% -> 9% of each run, Pallas kernels for 38% -> 44%
where the time goes in v3:
time: 618 us; the launch traced here: 613 us
  Pallas kernels  279 us (45%)
  waiting for transfers between devices  117 us (19%)
  blocking collectives  64.8 us (10%)
  starting transfers between devices  61.3 us (10%)
  local copies, waits for them, and re-layouts  53.6 us (9%)
  other arithmetic  22 us (4%)
  between operations  15.3 us (2%)
    pallas_call x2, Pallas kernels, sa_bwd(): pl.pallas_call(functools.partial(bwd_kernel, heads, prompt_tiles, unroll,...  79.7 us
    pallas_call x1, Pallas kernels, feed_forward(): pl.pallas_call(feed_kernel, grid=(hidden // TILE,), out_shape=[tokens(BF)...  39.2 us
    all_to_all x1, blocking collectives, spread(): lax.all_to_all(jnp.broadcast_to(piece[None], (count,) + piece.shape), 'fs...  34.1 us
    all_to_all x3, waiting for transfers between devices, spread(): lax.all_to_all(jnp.broadcast_to(piece[None], (count,) + piece.shape), 'fs...  33.9 us
    unnamed x86, local copies, waits for them, and re-layouts  31 us
    pallas_call x1, Pallas kernels, middle_back(): pl.pallas_call(functools.partial(middle_back_kernel, head_count), grid=(1...  29.7 us
    pallas_call x1, Pallas kernels, middle_forward(): pl.pallas_call(functools.partial(middle_kernel, head_count), grid=(1,), o...  29.4 us
    all_to_all x3, waiting for transfers between devices, collect(): parts = lax.all_to_all(parts, 'fsdp', 0, 0, tiled=True)  29.1 us
  transfers between devices with their start and end apart: 27, of which 13 were waited for; matrix products, arithmetic and copies ran while one was open for 9% of the time, Pallas kernels for 44%

profile of v3, /device:TPU:0, one launch (start us, length us, event | category | flops | bytes accessed | tf_op | source)
XLA Modules:
  0.0 612.7 jit_solution(5232110817063248067)
XLA Ops:
  7.3 2.7 copy.114.refs_0_
  13.5 6.3 %all-to-all-start = ((bf16[4,272,384]{2,1,0:T(8,128)(2,1)}), bf16[4,272,384]{2,1,0:T(8,128)(2,1)S(1)}, u32[]{:S(2)}, u32[]{:S(2)}) async-start(bf16[4,272,384]{2,1,0:T(8,128)(2,1)} %broadcast_in_dim.19), calls=%async_computation | async-start | bytes 1671168 | tf_op jit(solution)/shard_map/all_to_all | solution.py:819
  22.7 8.1 %all-reduce.2 = s32[32]{0:T(128)S(1)} all-reduce(s32[32]{0:T(128)S(1)} %fusion.38), channel_id=1, replica_groups=mesh['plane'=4,'core'=2,'fsdp'=4] {'plane','core'}, use_global_device_ids=true, to_apply=%add.2 | all-reduce | flops 32 | bytes 256
  35.7 5.3 all-to-all-done.refs_1_
  43.0 34.1 %all_to_all.50.refs_1_ = bf16[4,5,32,1024]{3,2,1,0:T(8,128)(2,1)} all-to-all(bf16[4,5,32,1024]{3,2,1,0:T(8,128)(2,1)S(1)} %broadcast_in_dim.20), channel_id=1, replica_groups=mesh['plane'=4,'core'=2,'fsdp'=4] {'fsdp'}, dimensions={0} | all-to-all | bytes 2621440 | tf_op jit(solution)/shard_map/all_to_all | solution.py:819
  84.2 3.6 all-to-all-start.3
  88.1 11.0 %first_projection.1 = bf16[4096,384]{1,0:T(8,128)(2,1)} custom-call(bf16[8,576,1024]{2,1,0:T(8,128)(2,1)} %bitcast.131, f32[1,1024]{1,0:T(1,128)} %bitcast.191, bf16[1024,384]{1,0:T(8,128)(2,1)} %bitcast.147), custom_call_target="tpu_custom_call" | custom-call | flops 3221225472 | bytes 11534336 | tf_op jit(solution)/shard_map/first_projection/pallas_call | solution.py:728
  99.1 28.2 %self_attention_forward.1 = (bf16[32,128,128]{2,1,0:T(8,128)(2,1)}, f32[128,4096]{1,0:T(8,128)}, f32[2,4096]{1,0:T(2,128)}) custom-call(s32[32]{0:T(128)} %get-tuple-element.58.slots.refs_2_, f32[64]{0:T(128)} %reshape.162.tab, bf16[32,128,384]{2,1,0:T(8,128)(2,1)} %bitcast.171), custom_call_target="tpu_custom_call" | custom-call | flops 32000000000 | bytes 12582912 | tf_op jit(solution)/shard_map/self_attention_forward/pallas_call | solution.py:131
  127.3 22.5 %all_to_all.51.o_ref.refs_1_ = bf16[8,512,128]{2,1,0:T(8,128)(2,1)} all-to-all(bf16[8,512,128]{2,1,0:T(8,128)(2,1)} %bitcast.184), channel_id=1, replica_groups=mesh['plane'=4,'core'=2,'fsdp'=4] {'plane','core'}, dimensions={0} | all-to-all | bytes 2097152 | tf_op jit(solution)/shard_map/all_to_all | solution.py:952
  153.0 2.3 slice.117
  158.3 4.6 all-to-all-start.4
  163.2 5.4 source_projection.1.ckv_ref
  168.6 29.4 %middle_forward.1 = (bf16[512,1024]{1,0:T(8,128)(2,1)}, f32[512,1024]{1,0:T(8,128)}, bf16[512,1024]{1,0:T(8,128)(2,1)}, bf16[512,1024]{1,0:T(8,128)(2,1)}, f32[8...) custom-call(bf16[8,512,128]{2,1,0:T(8,128)(2,1)} %all_to_all.51.o_ref.refs_1_, ...), custom_call_target="tpu_custom_call" | custom-call | flops 32212254720 | bytes 12582912 | tf_op jit(solution)/shard_map/middle_forward/pallas_call | solution.py:439
  198.1 28.6 %all-to-all-done.4 = bf16[4,704,512]{2,1,0:T(8,128)(2,1)S(1)} async-done(((bf16[4,704,512]{2,1,0:T(8,128)(2,1)}), bf16[4,704,512]{2,1,0:T(8,128)(2,1)S(1)}, u32[]{:S(2)}, u32[]{:S(2)}) %all-to-all-start.4) | async-done | bytes 2883616 | tf_op jit(solution)/shard_map/all_to_all | solution.py:819
  226.7 5.4 collective-permute-done.other_ref
  232.1 39.2 %feed_forward.1 = (bf16[512,1024]{1,0:T(8,128)(2,1)}, f32[512,1024]{1,0:T(8,128)}, f32[1,1024]{1,0:T(1,128)}, bf16[8,4,2,32,2816]{4,3,2,1,0:T(8,128)(2,1)}, bf16...) custom-call(s32[1]{0:T(128)} %bitcast.core_ref, bf16[512,1024]{1,0:T(8,128)(2,1)} %get-tuple-element.60.n3_ref, ...), custom_call_target="tpu_custom_call" | custom-call | flops 41339060224 | bytes 34603008 | tf_op jit(solution)/shard_map/feed_forward/pallas_call | solution.py:510
  274.2 29.7 %middle_back.1 = (f32[512,1024]{1,0:T(8,128)}, f32[1,1024]{1,0:T(1,128)}, bf16[512,1024]{1,0:T(8,128)(2,1)}, bf16[2,512,1024]{2,1,0:T(8,128)(2,1)}, bf16[8,512,128]{2,1,0:T(8,128)(2,1)}) custom-call(f32[512,1024]{1,0:T(8,128)} %after.21.dx2_ref, f32[512,1024]{1,0:T(8,128)} %get-tuple-element.64.x1_ref, f32[1,1024]{1,0:T(1,128)} %bitcast.196, ...), custom_call_target="tpu_custom_call" | custom-call | flops 32212254720 | bytes 12582912 | tf_op jit(solution)/shard_map/middle_back/pallas_call | solution.py:607
  303.9 23.2 %middle_grads.1.refs_2_ = bf16[8,704,1024]{2,1,0:T(8,128)(2,1)} custom-call(f32[512,1024]{1,0:T(8,128)} %get-tuple-element.63.dx2_ref, f32[512,1024]{1,0:T(8,128)} %get-tuple-element.64.x1_ref, f32[1,1024]{1,0:T(1,128)} %bitcast.197, bf16[512,1024]{1,0:T(8,128)(2,1)} %get-tuple-element.74.cob_ref, bf16[512,1024]{1,0:T(8,128)(2,1)} %get-tuple-element.75.dcq_ref, ...), custom_call_target="tpu_custom_call" | custom-call | flops 24696061952 | bytes 12582912 | tf_op jit(solution)/shard_map/middle_grads/pallas_call | solution.py:670
  327.2 3.6 all-to-all-start.5
  332.8 3.5 add_convert_fusion
  339.4 8.7 %all-to-all-done.5 = bf16[8,512,128]{2,1,0:T(8,128)(2,1)S(1)} async-done(((bf16[8,512,128]{2,1,0:T(8,128)(2,1)}), bf16[8,512,128]{2,1,0:T(8,128)(2,1)S(1)}, u32[]{:S(2)}, u32[]{:S(2)}) %all-to-all-start.5) | async-done | bytes 1048608 | tf_op jit(solution)/shard_map/all_to_all | solution.py:970
  349.2 3.9 all-to-all-start.6
  353.0 2.3 copy.103.refs_0_
  355.4 39.8 %self_attention_backward.2 = (bf16[2560,128]{1,0:T(8,128)(2,1)}, f32[4096,256]{1,0:T(8,128)}, f32[2,2,128,128]{3,2,1,0:T(8,128)}, f32[2,8,256]{2,1,0:T(8,128)}) custom-call(s32[32]{0:T(128)} %get-tuple-element.58.slots.refs_2_, f32[64]{0:T(128)} %reshape.162.tab, bf16[32,128,384]{2,1,0:T(8,128)(2,1)} %bitcast.172, bf16[32,128,128]{2,1,0:T(8,128)(2,1)} %after.23.do_ref, ...), custom_call_target="tpu_custom_call" | custom-call | flops 43000000512 | bytes 18874368 | tf_op jit(solution)/shard_map/self_attention_backward/pallas_call | solution.py:268
  395.1 19.7 %all-to-all-done.6.refs_0_ = bf16[4,704,512]{2,1,0:T(8,128)(2,1)S(1)} async-done(((bf16[4,704,512]{2,1,0:T(8,128)(2,1)}), bf16[4,704,512]{2,1,0:T(8,128)(2,1)S(1)}, u32[]{:S(2)}, u32[]{:S(2)}) %all-to-all-start.6) | async-done | bytes 2883616 | tf_op jit(solution)/shard_map/all_to_all | solution.py:823
  416.4 3.3 reduce_sum.45.refs_1_
  419.7 3.6 all-to-all-start.7
  423.3 40.0 %self_attention_backward.3 = (bf16[32,128,384]{2,1,0:T(8,128)(2,1)}, f32[2,32,128]{2,1,0:T(8,128)}) custom-call(s32[32]{0:T(128)} %get-tuple-element.58.slots.refs_2_, f32[64]{0:T(128)} %reshape.162.tab, bf16[32,128,384]{2,1,0:T(8,128)(2,1)} %bitcast.173, bf16[32,128,128]{2,1,0:T(8,128)(2,1)} %after.22.do_ref, f32[128,4096]{1,0:T(8,128)} %get-tuple-element.70.ot_ref, ...), custom_call_target="tpu_custom_call" | custom-call | flops 43000000512 | bytes 18874368 | tf_op jit(solution)/shard_map/self_attention_backward/pallas_call | solution.py:268
  464.4 2.4 reduce_sum.46.refs_1_
  466.9 2.5 slice.118
  469.4 5.0 all-to-all-start.8
  474.5 3.8 collective-permute-start.8
  478.3 11.2 %collective-permute-done.8 = bf16[2,176,512]{2,1,0:T(8,128)(2,1)S(1)} collective-permute-done((bf16[2,176,512]{2,1,0:T(8,128)(2,1)S(1)}, bf16[2,176,512]{2,1,0:T(8,128)(2,1)S(1)}, u32[]{:S(2)}, u32[]{:S(2)}) %collective-permute-start.8) | collective-permute-done | bytes 360480 | tf_op jit(solution)/shard_map/ppermute | solution.py:885
  489.7 5.4 collective-permute-done.9
  495.2 9.5 %all-to-all-done.8 = bf16[4,160,1024]{2,1,0:T(8,128)(2,1)S(1)} async-done(((bf16[4,160,1024]{2,1,0:T(8,128)(2,1)}), bf16[4,160,1024]{2,1,0:T(8,128)(2,1)S(1)}, u32[]{:S(2)}, u32[]{:S(2)}) %all-to-all-start.8) | async-done | bytes 1310752 | tf_op jit(solution)/shard_map/all_to_all | solution.py:823
  509.4 5.4 all-to-all-start.9
  515.0 12.5 %last_projection.1 = (bf16[1024,384]{1,0:T(8,128)(2,1)}, f32[1024,1]{1,0:T(8,128)}) custom-call(bf16[8,576,1024]{2,1,0:T(8,128)(2,1)} %bitcast.133, f32[1,1024]{1,0:T(1,128)} %bitcast.192, bf16[1024,384]{1,0:T(8,128)(2,1)} %bitcast.148, bf16[4096,384]{1,0:T(8,128)(2,1)} %bitcast.135), custom_call_target="tpu_custom_call" | custom-call | flops 3221225472 | bytes 11534336 | tf_op jit(solution)/shard_map/last_projection/pallas_call | solution.py:766
  529.9 2.3 fusion.12
  535.1 5.9 collective-permute-start.4
  542.2 8.9 %collective-permute-start.6 = (bf16[272,384]{1,0:T(8,128)(2,1)}, bf16[272,384]{1,0:T(8,128)(2,1)}, u32[]{:S(2)}, u32[]{:S(2)}) collective-permute-start(bf16[272,384]{1,0:T(8,128)(2,1)} %get-tuple-element.104), channel_id=1, source_target_pairs={{0,3},{4,7},{8,11},{12,15},{16,19},{20,23},{24,27},{28,31}} | collective-permute-start | bytes 626696 | tf_op jit(solution)/shard_map/ppermute | solution.py:838
  553.1 2.5 collective-permute-done.5
  555.6 6.3 %collective-permute-done.7 = bf16[272,384]{1,0:T(8,128)(2,1)} collective-permute-done((bf16[272,384]{1,0:T(8,128)(2,1)S(1)}, bf16[272,384]{1,0:T(8,128)(2,1)}, u32[]{:S(2)}, u32[]{:S(2)}) %collective-permute-start.7) | collective-permute-done | bytes 208928 | tf_op jit(solution)/shard_map/ppermute | solution.py:838
  561.8 2.3 fusion.6.refs_0_
  564.1 4.6 all-to-all-done.9.d_ref.refs_2_
  572.0 13.1 %final_back.1 = f32[512,1024]{1,0:T(8,128)} custom-call(bf16[8,512,384]{2,1,0:T(8,128)(2,1)} %copy-done.1, bf16[8,1024,384]{2,1,0:T(8,128)(2,1)} %bitcast.139, bf16[512,1024]{1,0:T(8,128)(2,1)} %bitcast.165, f32[1,1024]{1,0:T(1,128)} %bitcast.193, f32[512,1024]{1,0:T(8,128)} %get-tuple-element.78.dx1_ref), custom_call_target="tpu_custom_call" | custom-call | flops 3221225472 | bytes 6291456 | tf_op jit(solution)/shard_map/final_back/pallas_call | solution.py:701
  585.7 3.1 fusion.40
  588.8 7.7 %all-gather.27.cloned.1.call-done = bf16[2176,384]{1,0:T(8,128)(2,1)} async-done(((bf16[272,384]{1,0:T(8,128)(2,1)}), bf16[2176,384]{1,0:T(8,128)(2,1)}) %all-gather.27.cloned.1.call-update) | async-done | bytes 1671184 | tf_op jit(solution)/shard_map/all_gather | solution.py:1004
  596.5 7.3 %unpack.1 = (f32[256,1024]{1,0:T(8,128)}, f32[256,1024]{1,0:T(8,128)}, f32[256,1024]{1,0:T(8,128)}, f32[256,1024]{1,0:T(8,128)}, f32[256,1024]{1,0:T(8,128)}, /*...) custom-call(bf16[8,248,1024]{2,1,0:T(8,128)(2,1)} %bitcast.144, ...), custom_call_target="tpu_custom_call" | custom-call | bytes 12189696 | tf_op jit(solution)/shard_map/unpack/pallas_call | solution.py:802
  (192 shorter events, 58.1 us)
Async XLA Ops:
  7.2 2.7 copy-start.12
  7.2 2.7 copy-start.21
  7.2 80.9 %all-gather.15.cloned.1.call-start = ((), (), s32[]{:S(2)}) async-start(), calls=%async_computation.14 | async-start | bytes 10616832 | tf_op jit(solution)/shard_map/all_gather | solution.py:921
  9.9 1.2 copy-start.17
  9.9 1.6 copy-start.18
  9.9 1.8 copy-start.19
  12.2 9.1 %copy-start.30 = (u32[32]{0:T(128)S(1)}, u32[32]{0:T(128)}, u32[]{:S(2)}) copy-start(u32[32]{0:T(128)} %constant.159) | copy-start | bytes 388
  13.5 27.5 %all-to-all-start = ((bf16[4,272,384]{2,1,0:T(8,128)(2,1)}), bf16[4,272,384]{2,1,0:T(8,128)(2,1)S(1)}, u32[]{:S(2)}, u32[]{:S(2)}) async-start(bf16[4,272,384]{2,1,0:T(8,128)(2,1)} %broadcast_in_dim.19), calls=%async_computation | async-start | bytes 1671168 | tf_op jit(solution)/shard_map/all_to_all | solution.py:819
  19.8 143.4 %all-gather.17.cloned.1.call-start = ((), (), s32[]{:S(2)}) async-start(), calls=%async_computation.15 | async-start | bytes 11796480 | tf_op jit(solution)/shard_map/all_gather | solution.py:947
  35.1 5.9 copy-start.16
  43.0 36.0 %copy-start.10 = (bf16[4,272,384]{2,1,0:T(8,128)(2,1)S(1)}, bf16[4,272,384]{2,1,0:T(8,128)(2,1)}, u32[]{:S(2)}) copy-start(bf16[4,272,384]{2,1,0:T(8,128)(2,1)} %copy-done.9) | copy-start | bytes 2506756
  84.2 43.1 %all-to-all-start.3 = ((bf16[4,2,32,2816]{3,2,1,0:T(8,128)(2,1)}), bf16[4,2,32,2816]{3,2,1,0:T(8,128)(2,1)S(1)}, u32[]{:S(2)}, u32[]{:S(2)}) async-start(bf16[4,2,32,2816]{3,2,1,0:T(8,128)(2,1)} %broadcast_in_dim.21), calls=%async_computation.3 | async-start | bytes 2883584 | tf_op jit(solution)/shard_map/all_to_all | solution.py:819
  87.8 144.2 %all-gather.19.cloned.1.call-start = ((), (), s32[]{:S(2)}) async-start(), calls=%async_computation.16 | async-start | bytes 12976128 | tf_op jit(solution)/shard_map/all_gather | solution.py:954
  127.3 22.5 %copy-start.6 = (bf16[4,2,32,2816]{3,2,1,0:T(8,128)(2,1)}, bf16[4,2,32,2816]{3,2,1,0:T(8,128)(2,1)S(1)}, u32[]{:S(2)}) copy-start(bf16[4,2,32,2816]{3,2,1,0:T(8,128)(2,1)S(1)} %all-to-all-done.3.refs_0_) | copy-start | bytes 4325380
  149.8 1.1 copy-start.7
  158.3 68.3 %all-to-all-start.4 = ((bf16[4,704,512]{2,1,0:T(8,128)(2,1)}), bf16[4,704,512]{2,1,0:T(8,128)(2,1)S(1)}, u32[]{:S(2)}, u32[]{:S(2)}) async-start(bf16[4,704,512]{2,1,0:T(8,128)(2,1)} %broadcast_in_dim.44), calls=%async_computation.4 | async-start | bytes 5767168 | tf_op jit(solution)/shard_map/all_to_all | solution.py:819
  162.9 111.3 %all-gather.21.cloned.1.call-start = ((), (), s32[]{:S(2)}) async-start(), calls=%async_computation.17 | async-start | bytes 7077888 | tf_op jit(solution)/shard_map/all_gather | solution.py:961
  198.0 221.7 %reduce-scatter.3.cloned.1.call-start = ((), (), s32[]{:S(2)}) async-start(), calls=%async_computation.12 | async-start | bytes 12976128 | tf_op jit(solution)/shard_map/reduce_scatter | solution.py:965
  226.7 5.4 copy-start.14
  226.7 5.4 collective-permute-start
  271.3 1.6 copy-start.15
  271.3 195.5 %reduce-scatter.5.cloned.1.call-start = ((), (), s32[]{:S(2)}) async-start(), calls=%async_computation.13 | async-start | bytes 12976128 | tf_op jit(solution)/shard_map/reduce_scatter | solution.py:978
  327.1 5.7 collective-permute-start.1
  327.2 21.0 %all-to-all-start.5 = ((bf16[8,512,128]{2,1,0:T(8,128)(2,1)}), bf16[8,512,128]{2,1,0:T(8,128)(2,1)S(1)}, u32[]{:S(2)}, u32[]{:S(2)}) async-start(bf16[8,512,128]{2,1,0:T(8,128)(2,1)} %get-tuple-element.68), calls=%async_computation.5 | async-start | bytes 2097152 | tf_op jit(solution)/shard_map/all_to_all | solution.py:970
  336.3 1.6 copy-start.3
  349.2 65.6 %all-to-all-start.6 = ((bf16[4,704,512]{2,1,0:T(8,128)(2,1)}), bf16[4,704,512]{2,1,0:T(8,128)(2,1)S(1)}, u32[]{:S(2)}, u32[]{:S(2)}) async-start(bf16[4,704,512]{2,1,0:T(8,128)(2,1)} %after.24), calls=%async_computation.8 | async-start | bytes 5767168 | tf_op jit(solution)/shard_map/all_to_all | solution.py:823
  414.8 1.6 copy-start.2
  419.7 43.6 %all-to-all-start.7 = ((bf16[4,2,32,2816]{3,2,1,0:T(8,128)(2,1)}), bf16[4,2,32,2816]{3,2,1,0:T(8,128)(2,1)S(1)}, u32[]{:S(2)}, u32[]{:S(2)}) async-start(bf16[4,2,32,2816]{3,2,1,0:T(8,128)(2,1)} %after.26), calls=%async_computation.9 | async-start | bytes 2883584 | tf_op jit(solution)/shard_map/all_to_all | solution.py:823
  423.3 82.6 %all-gather.23.cloned.1.call-start = ((), (), s32[]{:S(2)}) async-start(), calls=%async_computation.18 | async-start | bytes 3244032 | tf_op jit(solution)/shard_map/all_gather | solution.py:989
  466.9 7.6 %copy-start.11 = (bf16[704,512]{1,0:T(8,128)(2,1)S(1)}, bf16[704,512]{1,0:T(8,128)(2,1)}, u32[]{:S(2)}) copy-start(bf16[704,512]{1,0:T(8,128)(2,1)} %reduce_sum.45.refs_1_) | copy-start | bytes 2162692
  469.4 35.3 %all-to-all-start.8 = ((bf16[4,160,1024]{2,1,0:T(8,128)(2,1)}), bf16[4,160,1024]{2,1,0:T(8,128)(2,1)S(1)}, u32[]{:S(2)}, u32[]{:S(2)}) async-start(bf16[4,160,1024]{2,1,0:T(8,128)(2,1)} %bitcast.33), calls=%async_computation.10 | async-start | bytes 2621440 | tf_op jit(solution)/shard_map/all_to_all | solution.py:823
  474.4 94.3 %all-gather.25.cloned.1.call-start = ((), (), s32[]{:S(2)}) async-start(), calls=%async_computation.19 | async-start | bytes 4571136 | tf_op jit(solution)/shard_map/all_gather | solution.py:1003
  474.5 15.0 %collective-permute-start.8 = (bf16[2,176,512]{2,1,0:T(8,128)(2,1)S(1)}, bf16[2,176,512]{2,1,0:T(8,128)(2,1)S(1)}, u32[]{:S(2)}, u32[]{:S(2)}) collective-permute-start(bf16[2,176,512]{2,1,0:T(8,128)(2,1)S(1)} %dynamic-slice_bitcast_fusion), channel_id=1, source_target_pairs={{0,8},{8,0},{16,24},{24,16},{1,9},{9,1},{17,25},{25,17},{2,10},{10... | collective-permute-start | bytes 1081352 | tf_op jit(solution)/shard_map/ppermute | solution.py:885
  489.6 5.6 collective-permute-start.9
  505.9 1.9 copy-start
  509.4 5.5 copy-start.25
  509.4 5.5 copy-start.24
  509.4 59.3 %all-to-all-start.9 = ((bf16[8,512,384]{2,1,0:T(8,128)(2,1)}), bf16[8,512,384]{2,1,0:T(8,128)(2,1)S(1)}, u32[]{:S(2)}, u32[]{:S(2)}) async-start(bf16[8,512,384]{2,1,0:T(8,128)(2,1)} %bitcast.134), calls=%async_computation.11 | async-start | bytes 6291456 | tf_op jit(solution)/shard_map/all_to_all | solution.py:987
  514.8 81.7 %all-gather.27.cloned.1.call-start = ((), (), s32[]{:S(2)}) async-start(), calls=%async_computation.20 | async-start | bytes 1880064 | tf_op jit(solution)/shard_map/all_gather | solution.py:1004
  514.9 13.8 %copy-start.23 = (f32[2,32,128]{2,1,0:T(8,128)S(1)}, f32[2,32,128]{2,1,0:T(8,128)}, u32[]{:S(2)}) copy-start(f32[2,32,128]{2,1,0:T(8,128)} %get-tuple-element.88) | copy-start | bytes 98308
  532.2 18.9 %collective-permute-start.2 = (bf16[272,384]{1,0:T(8,128)(2,1)S(1)}, bf16[272,384]{1,0:T(8,128)(2,1)S(1)}, u32[]{:S(2)}, u32[]{:S(2)}) collective-permute-start(bf16[272,384]{1,0:T(8,128)(2,1)S(1)} %get-tuple-element.100), channel_id=1, source_target_pairs={{0,1},{1,2},{2,3},{4,5},{5,6},{6,7},{8,9},{9,10},{10,11},{12,13},{... | collective-permute-start | bytes 626696 | tf_op jit(solution)/shard_map/ppermute | solution.py:838
  533.5 19.5 %collective-permute-start.3 = (bf16[272,384]{1,0:T(8,128)(2,1)}, bf16[272,384]{1,0:T(8,128)(2,1)}, u32[]{:S(2)}, u32[]{:S(2)}) collective-permute-start(bf16[272,384]{1,0:T(8,128)(2,1)} %get-tuple-element.101), channel_id=1, source_target_pairs={{1,0},{2,1},{3,2},{5,4},{6,5},{7,6},{9,8},{10,9},{11,10},{13,12},{... | collective-permute-start | bytes 626696 | tf_op jit(solution)/shard_map/ppermute | solution.py:838
  535.1 18.0 %collective-permute-start.4 = (bf16[272,384]{1,0:T(8,128)(2,1)}, bf16[272,384]{1,0:T(8,128)(2,1)}, u32[]{:S(2)}, u32[]{:S(2)}) collective-permute-start(bf16[272,384]{1,0:T(8,128)(2,1)} %get-tuple-element.102), channel_id=1, source_target_pairs={{0,2},{1,3},{4,6},{5,7},{8,10},{9,11},{12,14},{13,15},{16,18},{17,... | collective-permute-start | bytes 626696 | tf_op jit(solution)/shard_map/ppermute | solution.py:838
  540.9 14.7 %collective-permute-start.5 = (bf16[272,384]{1,0:T(8,128)(2,1)}, bf16[272,384]{1,0:T(8,128)(2,1)}, u32[]{:S(2)}, u32[]{:S(2)}) collective-permute-start(bf16[272,384]{1,0:T(8,128)(2,1)} %get-tuple-element.103), channel_id=1, source_target_pairs={{2,0},{3,1},{6,4},{7,5},{10,8},{11,9},{14,12},{15,13},{18,16},{19,... | collective-permute-start | bytes 626696 | tf_op jit(solution)/shard_map/ppermute | solution.py:838
  542.2 13.4 %collective-permute-start.6 = (bf16[272,384]{1,0:T(8,128)(2,1)}, bf16[272,384]{1,0:T(8,128)(2,1)}, u32[]{:S(2)}, u32[]{:S(2)}) collective-permute-start(bf16[272,384]{1,0:T(8,128)(2,1)} %get-tuple-element.104), channel_id=1, source_target_pairs={{0,3},{4,7},{8,11},{12,15},{16,19},{20,23},{24,27},{28,31}} | collective-permute-start | bytes 626696 | tf_op jit(solution)/shard_map/ppermute | solution.py:838
  551.8 10.0 %collective-permute-start.7 = (bf16[272,384]{1,0:T(8,128)(2,1)S(1)}, bf16[272,384]{1,0:T(8,128)(2,1)}, u32[]{:S(2)}, u32[]{:S(2)}) collective-permute-start(bf16[272,384]{1,0:T(8,128)(2,1)S(1)} %get-tuple-element.105), channel_id=1, source_target_pairs={{3,0},{7,4},{11,8},{15,12},{19,16},{23,20},{27,24},{31,28}} | collective-permute-start | bytes 626696 | tf_op jit(solution)/shard_map/ppermute | solution.py:838
  568.7 1.6 copy-start.1
  572.0 13.1 %copy-start.8 = (bf16[16,32,2816]{2,1,0:T(8,128)(2,1)S(1)}, bf16[16,32,2816]{2,1,0:T(8,128)(2,1)}, u32[]{:S(2)}) copy-start(bf16[16,32,2816]{2,1,0:T(8,128)(2,1)} %all-gather.23.cloned.1.call-done) | copy-start | bytes 8650756
  (10 other events, 9.2 us)
Sparse Core Ops, SparseCore 0:
  11.2 61.6 all-gather.14
  77.3 66.7 all-gather.16
  150.0 66.7 all-gather.18
  219.1 45.5 all-gather.20
  271.5 91.6 reduce-scatter.2
  366.5 84.4 reduce-scatter.4
  466.9 37.5 all-gather.22
  507.0 59.5 all-gather.24
  570.5 25.9 all-gather.26

commit v4 on v3

--- a/solution.py
+++ b/solution.py
@@ -32,6 +32,12 @@
     return lax.dot_general(a,b,(((1,),(1,)),((),())),preferred_element_type=F32)
 def nn(a,b):
     return lax.dot_general(a,b,(((1,),(0,)),((),())),preferred_element_type=F32)
+
+def leaving_out(kernel,count):
+    return lambda *refs: kernel(*refs[count:])
+
+def unread(operands):
+    return [pl.BlockSpec(memory_space=pl.ANY)]*len(operands)
 
 def head_mask(value,head,heads):
     if heads==1: return value
@@ -135,11 +141,11 @@
         out_specs=[pl.BlockSpec(memory_space=pltpu.VMEM)]*3,
         scratch_shapes=[pltpu.VMEM((heads,TILE,TILE),F32),pltpu.VMEM((n,w),BF),pltpu.VMEM((tiles,w,TILE),BF),pltpu.VMEM((8,128),F32),pltpu.VMEM((heads,prompt_tiles+1,TILE,TILE),F32)],
         compiler_params=pltpu.CompilerParams(vmem_limit_bytes=VMEM_LIMIT),
-        cost_estimate=pl.CostEstimate(flops=32 * 10**9, bytes_accessed=8 * n * w3, transcendentals=0),
+        cost_estimate=cost(32 * 10**9, 8 * n * w3),
         name="self_attention_forward",
     )(slots,tab,qkv)
 
-def bwd_kernel(heads,prompt_tiles,unroll,low,high,slots,tab,qkv,do_ref,ot_ref,lse_ref,*refs):
+def bwd_kernel(heads,prompt_tiles,low,high,slots,tab,qkv,do_ref,ot_ref,lse_ref,*refs):
     if low:
         dq_in,dkv_in,near_in,far_in,dqkv_ref,dtab_ref,bias,kc,vc,kt,dqt,dkv,near,far=refs
     else:
@@ -170,52 +176,63 @@
         delta=[jnp.sum(dot[h*size:(h+1)*size],axis=0,keepdims=True) for h in range(heads)]
         dqt[...]=jnp.zeros_like(dqt)
 
-        def piece(j,kind):
-            rows=pl.ds(pl.multiple_of(j*TILE,TILE),TILE)
-            k=kc[rows,:]; v=vc[rows,:]
-            dv=None; dk=None
+        def group(*pieces):
+            spans=[pl.ds(pl.multiple_of(j*TILE,TILE),TILE) for j,_ in pieces]
+            keys=[kc[rows,:] for rows in spans]
+            values=[vc[rows,:] for rows in spans]
+            turned=[kt[j] for j,_ in pieces]
+            dk=[None]*len(pieces); dv=[None]*len(pieces)
+            dq_parts=[]; far_parts=[]
             for h in range(heads):
-                s=nt(k,qh[h])
-                if kind=="own":
-                    s=s+bias[h]
-                elif kind=="prev":
-                    low=jnp.concatenate([s[BLK:,:BLK]+bias[h,0:BLK,BLK:],s[BLK:,BLK:]],axis=1)
-                    s=jnp.concatenate([s[:BLK],low],axis=0)
-                p=jnp.exp(s-lse[h])
-                dp=nt(v,doh[h])
-                ds=p*(dp-delta[h])
-                if kind=="own":
-                    near[h,0]+=ds[:BLK,:BLK]+ds[BLK:,BLK:]
-                    near[h,1]+=ds[:BLK,BLK:]
-                elif kind=="prev":
-                    near[h,1]+=ds[BLK:,:BLK]
-                    f=jnp.sum(ds[:BLK].reshape(BLK//8,8,TILE),axis=0)
-                    f2=jnp.sum(ds[BLK:,BLK:].reshape(BLK//8,8,BLK),axis=0)
-                    far[h]+=f
-                    far[h,:,BLK:]+=f2
-                else:
-                    far[h]+=jnp.sum(ds.reshape(TILE//8,8,TILE),axis=0)
-                pb=p.astype(BF); db=ds.astype(BF)
-                a=nn(pb,doh[h]); dv=a if dv is None else dv+a
-                b=nn(db,qh[h]); dk=b if dk is None else dk+b
-                dqt[h*size:(h+1)*size,:]+=nn(kt[j,h*size:(h+1)*size,:],db)
-            dkv[rows,0:width]+=dk
-            dkv[rows,width:2*width]+=dv
-        n_far=jnp.maximum(jnp.minimum(t,prompt_tiles)-1,0)
-        def far_step(j,_):
-            piece(j,"far"); return 0
-        def far_many(j,_):
-            for u in range(unroll): piece(j*unroll+u,"far")
+                dq=None; sums=None
+                for i,(j,kind) in enumerate(pieces):
+                    s=nt(keys[i],qh[h])
+                    if kind=="own":
+                        s=s+bias[h]
+                    elif kind=="prev":
+                        lower=jnp.concatenate([s[BLK:,:BLK]+bias[h,0:BLK,BLK:],s[BLK:,BLK:]],axis=1)
+                        s=jnp.concatenate([s[:BLK],lower],axis=0)
+                    p=jnp.exp(s-lse[h])
+                    ds=p*(nt(values[i],doh[h])-delta[h])
+                    if kind=="own":
+                        near[h,0]+=ds[:BLK,:BLK]+ds[BLK:,BLK:]
+                        near[h,1]+=ds[:BLK,BLK:]
+                    else:
+                        if kind=="prev":
+                            near[h,1]+=ds[BLK:,:BLK]
+                            rest=jnp.concatenate([jnp.zeros((BLK,BLK),F32),ds[BLK:,BLK:]],axis=1)
+                            part=jnp.sum((ds[:BLK]+rest).reshape(BLK//8,8,TILE),axis=0)
+                        else:
+                            part=jnp.sum(ds.reshape(TILE//8,8,TILE),axis=0)
+                        sums=part if sums is None else sums+part
+                    pb=p.astype(BF); db=ds.astype(BF)
+                    a=nn(pb,doh[h]); dv[i]=a if dv[i] is None else dv[i]+a
+                    b=nn(db,qh[h]); dk[i]=b if dk[i] is None else dk[i]+b
+                    c=nn(turned[i][h*size:(h+1)*size,:],db); dq=c if dq is None else dq+c
+                dq_parts.append(dq); far_parts.append(sums)
+            for h in range(heads):
+                dqt[h*size:(h+1)*size,:]+=dq_parts[h]
+                if far_parts[h] is not None:
+                    far[h]+=far_parts[h]
+            for i,rows in enumerate(spans):
+                dkv[rows,0:width]+=dk[i]
+                dkv[rows,width:2*width]+=dv[i]
+        count=jnp.minimum(t,prompt_tiles)
+        pairs=jnp.maximum(count-1,0)//2
+        def far_pair(i,_):
+            group((2*i,"far"),(2*i+1,"far"))
             return 0
-        if unroll>1:
-            lax.fori_loop(0,n_far//unroll,far_many,0)
-            lax.fori_loop((n_far//unroll)*unroll,n_far,far_step,0)
-        else:
-            lax.fori_loop(0,n_far,far_step,0)
-        @pl.when(t>0)
+        lax.fori_loop(0,pairs,far_pair,0)
+        left=count-2*pairs
+        @pl.when(left==0)
         def _():
-            piece(n_far,"prev")
-        piece(t,"own")
+            group((t,"own"))
+        @pl.when(left==1)
+        def _():
+            group((count-1,"prev"),(t,"own"))
+        @pl.when(left==2)
+        def _():
+            group((count-2,"far"),(count-1,"prev"),(t,"own"))
         dq=jnp.transpose(dqt[...],(1,0)).astype(BF)
         if low:
             dqkv_ref[slots[2*t],:,0:width]=dq[:BLK]
@@ -254,7 +271,7 @@
             row=jnp.sum(total,axis=0,keepdims=True)
             dtab_ref[h,b:b+1,:]=jnp.broadcast_to(jnp.sum(row,axis=1,keepdims=True),(1,BLK))
 
-def sa_bwd(slots,tab,qkv,do,ot,lse,heads,prompt_tiles,low,high,held=(),unroll=2):
+def sa_bwd(earlier,slots,tab,qkv,do,ot,lse,heads,prompt_tiles,low,high,held=()):
     nb,_,w3=qkv.shape; w=w3//3; n=nb*BLK; tiles=n//TILE
     shape=jax.ShapeDtypeStruct
     sums=[shape((n,2*w),F32),shape((heads,2,BLK,BLK),F32),shape((heads,8,TILE),F32)]
@@ -266,15 +283,15 @@
     if low:
         scratch+=[pltpu.VMEM(v.shape,F32) for v in sums]
     return pl.pallas_call(
-        functools.partial(bwd_kernel,heads,prompt_tiles,unroll,low,high),
+        leaving_out(functools.partial(bwd_kernel,heads,prompt_tiles,low,high),len(earlier)),
         out_shape=out,
-        in_specs=[pl.BlockSpec(memory_space=pltpu.SMEM)]*2+[pl.BlockSpec(memory_space=pltpu.VMEM)]*(4+len(held)),
+        in_specs=unread(earlier)+[pl.BlockSpec(memory_space=pltpu.SMEM)]*2+[pl.BlockSpec(memory_space=pltpu.VMEM)]*(4+len(held)),
         out_specs=[pl.BlockSpec(memory_space=pltpu.VMEM)]*len(out),
         scratch_shapes=scratch,
         compiler_params=pltpu.CompilerParams(vmem_limit_bytes=VMEM_LIMIT),
-        cost_estimate=pl.CostEstimate(flops=43 * 10**9, bytes_accessed=12 * n * w3, transcendentals=0),
+        cost_estimate=cost((250 if low else 43) * 10**9, 12 * n * w3),
         name="self_attention_backward",
-    )(slots,tab,qkv,do,ot,lse,*held)
+    )(*earlier,slots,tab,qkv,do,ot,lse,*held)
 
 
 def line_tile(step, size=TILE):
@@ -292,9 +309,9 @@
 def store_rows(ref, layout, which, cols, value):
     parts, shards, matrices, rows = layout
     for z in range(shards):
+        place = (z * matrices + which) * rows
         for c in range(parts):
             start = (z * parts + c) * rows
-            place = (z * matrices + which) * rows
             ref[c, place : place + rows, cols] = value[start : start + rows]
 
 
@@ -454,64 +471,72 @@
 
 def feed_kernel(
     core_ref, n3_ref, cot_ref, x2_ref, gain_ref, w_ref, mine_ref, other_ref,
-    out_ref, dx2_ref, gain_out_ref, gw_ref, keep_ref, give_ref, n3t, acc, dn, wg, wu, down,
+    hidden_ref, dx2_ref, gain_out_ref, gw_ref, keep_ref, give_ref, n3t, wg, wu, dgate, dup, down,
 ):
+    step = pl.program_id(0)
     half = mine_ref.shape[1]
     own_half = pl.ds(pl.multiple_of(core_ref[0] * half, half), half)
     other_half = pl.ds(pl.multiple_of((1 - core_ref[0]) * half, half), half)
     down[:, own_half] = mine_ref[...]
     down[:, other_half] = other_ref[...]
-    step = pl.program_id(0)
 
     @pl.when(step == 0)
     def _():
         n3t[...] = jnp.transpose(n3_ref[...], (1, 0))
-        acc[...] = jnp.zeros_like(acc)
-        dn[...] = jnp.zeros_like(dn)
 
     parts, shards, _, rows, _ = w_ref.shape
     for z in range(shards):
         for c in range(parts):
             start = (z * parts + c) * rows
-            wg[start : start + rows, :] = w_ref[c, z, 0]
-            wu[start : start + rows, :] = w_ref[c, z, 1]
+            wg[step, start : start + rows, :] = w_ref[c, z, 0]
+            wu[step, start : start + rows, :] = w_ref[c, z, 1]
     n3, cot, wd = n3_ref[...], cot_ref[...], down[...]
-    gate, up = nn(n3, wg[...]), nn(n3, wu[...])
+    gate, up = nn(n3, wg[step]), nn(n3, wu[step])
     dh = nt(cot, wd)
     t = jnp.tanh(gelu_scale * (gate + 0.044715 * gate * gate * gate))
     gelu = 0.5 * gate * (1.0 + t)
     slope = 0.5 * (1.0 + t) + 0.5 * gate * (1.0 - t * t) * (gelu_scale * (1.0 + 3 * 0.044715 * gate * gate))
     hidden = (gelu * up).astype(BF)
-    dgate = (dh * up * slope).astype(BF)
-    dup = (dh * gelu).astype(BF)
-    acc[...] += nn(hidden, wd)
+    hidden_ref[...] = hidden
+    dgate_low = (dh * up * slope).astype(BF)
+    dup_low = (dh * gelu).astype(BF)
+    dgate[step] = dgate_low
+    dup[step] = dup_low
     down[...] = nn(jnp.transpose(hidden, (1, 0)), cot).astype(BF)
     keep_ref[...] = down[:, own_half]
     give_ref[...] = down[:, other_half]
     everything = slice(None)
-    store_grad(gw_ref, 0, everything, nn(n3t[...], dgate).astype(BF))
-    store_grad(gw_ref, 1, everything, nn(n3t[...], dup).astype(BF))
-    dn[...] += nt(dgate, wg[...]) + nt(dup, wu[...])
+    store_grad(gw_ref, 0, everything, nn(n3t[...], dgate_low).astype(BF))
+    store_grad(gw_ref, 1, everything, nn(n3t[...], dup_low).astype(BF))
 
     @pl.when(step == pl.num_programs(0) - 1)
     def _():
-        x2 = x2_ref[...]
-        out_ref[...] = (x2 + acc[...]).astype(BF)
-        dv, gain_out_ref[...] = norm_back(x2, gain_ref[...], dn[...])
+        def tile(i, _):
+            span = line_tile(i)
+            total = None
+            for s in range(dgate.shape[0]):
+                term = nt(dgate[s], wg[s, span, :]) + nt(dup[s], wu[s, span, :])
+                total = term if total is None else total + term
+            dx2_ref[:, span] = total
+            return 0
+
+        lax.fori_loop(0, dx2_ref.shape[1] // TILE, tile, 0)
+        dv, gain_out_ref[...] = norm_back(x2_ref[...], gain_ref[...], dx2_ref[...])
         dx2_ref[...] = cot_ref[...].astype(F32) + dv
 
 
 def feed_forward(core, n3, cot, x2, gain, wide, mine, other):
     rows, width = n3.shape
     parts, shards, _, own, hidden = wide.shape
+    steps = hidden // TILE
     tokens = lambda dtype: jax.ShapeDtypeStruct((rows, width), dtype)
     part = pl.BlockSpec((TILE, width // 2), lambda i: (i, 0))
     piece = pl.BlockSpec((parts, shards, 2, own, TILE), lambda i: (0, 0, 0, 0, i))
     return pl.pallas_call(
         feed_kernel,
-        grid=(hidden // TILE,),
+        grid=(steps,),
         out_shape=[
-            tokens(BF), tokens(F32), jax.ShapeDtypeStruct((1, width), F32),
+            jax.ShapeDtypeStruct((rows, hidden), BF), tokens(F32), jax.ShapeDtypeStruct((1, width), F32),
             jax.ShapeDtypeStruct(wide.shape, BF), jax.ShapeDtypeStruct(mine.shape, BF), jax.ShapeDtypeStruct(mine.shape, BF),
         ],
         in_specs=[
@@ -519,17 +544,45 @@
             whole((rows, width)), whole((rows, width)), whole((rows, width)), whole((1, width)), piece, part, part,
         ],
         out_specs=[
-            whole((rows, width)), whole((rows, width)), whole((1, width)),
+            pl.BlockSpec((rows, TILE), lambda i: (0, i)), whole((rows, width)), whole((1, width)),
             piece, part, part,
         ],
         scratch_shapes=[
-            pltpu.VMEM((width, rows), BF), pltpu.VMEM((rows, width), F32), pltpu.VMEM((rows, width), F32),
-            pltpu.VMEM((width, TILE), BF), pltpu.VMEM((width, TILE), BF), pltpu.VMEM((TILE, width), BF),
+            pltpu.VMEM((width, rows), BF), pltpu.VMEM((steps, width, TILE), BF), pltpu.VMEM((steps, width, TILE), BF),
+            pltpu.VMEM((steps, rows, TILE), BF), pltpu.VMEM((steps, rows, TILE), BF), pltpu.VMEM((TILE, width), BF),
         ],
         compiler_params=params(),
         cost_estimate=cost(28 * rows * width * hidden, 12 * width * hidden),
         name="feed_forward",
     )(core, n3, cot, x2, gain, wide, mine, other)
+
+
+def output_kernel(core_ref, hidden_ref, x2_ref, mine_ref, other_ref, out_ref):
+    half = mine_ref.shape[1]
+    own_half = pl.ds(pl.multiple_of(core_ref[0] * half, half), half)
+    other_half = pl.ds(pl.multiple_of((1 - core_ref[0]) * half, half), half)
+    hidden = hidden_ref[...]
+    out_ref[:, own_half] = (x2_ref[:, own_half] + nn(hidden, mine_ref[...])).astype(BF)
+    out_ref[:, other_half] = (x2_ref[:, other_half] + nn(hidden, other_ref[...])).astype(BF)
+
+
+def layer_output(earlier, core, hidden, x2, mine, other, tile=128):
+    rows, width = x2.shape
+    units = hidden.shape[1]
+    return pl.pallas_call(
+        leaving_out(output_kernel, len(earlier)),
+        grid=(rows // tile,),
+        out_shape=jax.ShapeDtypeStruct((rows, width), BF),
+        in_specs=unread(earlier) + [
+            pl.BlockSpec(memory_space=pltpu.SMEM),
+            pl.BlockSpec((tile, units), lambda i: (i, 0)), pl.BlockSpec((tile, width), lambda i: (i, 0)),
+            whole(mine.shape), whole(mine.shape),
+        ],
+        out_specs=pl.BlockSpec((tile, width), lambda i: (i, 0)),
+        compiler_params=params(),
+        cost_estimate=cost(4 * rows * width * units, 4 * width * units),
+        name="layer_output",
+    )(*earlier, core, hidden, x2, mine, other)
 
 
 def middle_back_kernel(
@@ -595,7 +648,7 @@
             dso_ref[t * per + u] = tile[:, u * inner : (u + 1) * inner]
 
 
-def middle_back(dx2, x1, gain, packed, cq, ckv, cot, lse, head_count, parts):
+def middle_back(earlier, dx2, x1, gain, packed, cq, ckv, cot, lse, head_count, parts):
     rows, width = dx2.shape
     size = width // head_count
     count = ckv.shape[1]
@@ -605,10 +658,10 @@
         jax.ShapeDtypeStruct((parts, rows, width // parts), BF),
     ]
     return pl.pallas_call(
-        functools.partial(middle_back_kernel, head_count),
+        leaving_out(functools.partial(middle_back_kernel, head_count), len(earlier)),
         grid=(1,),
         out_shape=shapes,
-        in_specs=[
+        in_specs=unread(earlier) + [
             whole((rows, width)), whole((rows, width)), whole((1, width)),
             packed_spec(packed, 0), packed_spec(packed, 1), packed_spec(packed, 2),
             whole((rows, width)), whole(ckv.shape), whole(cot.shape), whole(lse.shape),
@@ -621,7 +674,7 @@
         compiler_params=params(),
         cost_estimate=cost(60 * rows * width * width, 24 * rows * width),
         name="middle_back",
-    )(dx2, x1, gain, packed, packed, packed, cq, ckv, cot, lse)
+    )(*earlier, dx2, x1, gain, packed, packed, packed, cq, ckv, cot, lse)
 
 
 def middle_grad_kernel(
@@ -734,7 +787,7 @@
         ],
         out_specs=pl.BlockSpec((rows, cols), lambda i: (i, 0)),
         compiler_params=params(),
-        cost_estimate=cost(2 * parts * rows * width * cols, 2 * parts * rows * (width + cols)),
+        cost_estimate=cost(4 * parts * rows * width * cols, 2 * parts * rows * (width + cols)),
         name="first_projection",
     )(gathered, gain, weight)
 
@@ -756,67 +809,89 @@
     @pl.when(step == pl.num_programs(0) - 1)
     def _():
         total = acc_ref[...]
-        gw_ref[...] = total.astype(BF)
+        if len(gw_ref.shape) == 2:
+            gw_ref[...] = total.astype(BF)
+        else:
+            shards, piece, wide = gw_ref.shape
+            rows = total.shape[0] // shards
+            for z in range(shards):
+                block = total[z * rows : (z + 1) * rows].astype(BF)
+                stacked = jnp.concatenate([block[:, i * 128 : (i + 1) * 128] for i in range(3)], axis=0)
+                for b in range(wide // 128):
+                    gw_ref[z, :, b * 128 : (b + 1) * 128] = stacked[b * piece : (b + 1) * piece]
         gain_out_ref[...] = jnp.sum(total * w_ref[...].astype(F32), axis=1, keepdims=True)
 
 
-def last_projection(gathered, gain, weight, grads, rows):
+def last_projection(gathered, gain, weight, grads, rows, shards):
     parts, _, width = gathered.shape
     cols = weight.shape[1]
+    shape = (shards, cols // shards, width) if shards else (width, cols)
     return pl.pallas_call(
         last_kernel,
         grid=(parts,),
-        out_shape=(jax.ShapeDtypeStruct((width, cols), BF), jax.ShapeDtypeStruct((width, 1), F32)),
+        out_shape=(jax.ShapeDtypeStruct(shape, BF), jax.ShapeDtypeStruct((width, 1), F32)),
         in_specs=[
             pl.BlockSpec((1, rows, width), lambda i: (i, 0, 0)), whole((1, width)), whole((width, cols)),
             pl.BlockSpec((rows, cols), lambda i: (i, 0)),
         ],
-        out_specs=[whole((width, cols)), whole((width, 1))],
+        out_specs=[whole(shape), whole((width, 1))],
         scratch_shapes=[pltpu.VMEM((width, cols), F32)],
         compiler_params=params(),
-        cost_estimate=cost(2 * parts * rows * width * cols, 2 * parts * rows * (width + cols)),
+        cost_estimate=cost(4 * parts * rows * width * cols, 2 * parts * rows * (width + cols)),
         name="last_projection",
     )(gathered, gain, weight, grads)
 
 
-def unpack_kernel(own, rest_ref, last_ref, *outs):
-    parts = rest_ref.shape[0]
-    down = outs[5].shape[0] // parts
-    rows, inner = outs[0].shape[0], last_ref.shape[2] // 3
+def unpack_kernel(own, piece, rest_ref, *outs):
+    parts, total, width = rest_ref.shape
+    first = 5 * own
+    rows, inner = outs[6].shape[0], width // parts
+    down_at = first + piece + 16
+    down, half = total - down_at, width // 2
     for c in range(parts):
         for i in range(5):
             outs[i][c * own : (c + 1) * own, :] = rest_ref[c, i * own : (i + 1) * own, :].astype(F32)
-        half = rest_ref.shape[2] // 2
         for i in range(2):
             start = ((c // 2) * 2 + i) * down
-            value = rest_ref[c, 5 * own : 5 * own + down, i * half : (i + 1) * half]
+            value = rest_ref[c, down_at:total, i * half : (i + 1) * half]
             outs[5][start : start + down, (c % 2) * half : (c % 2 + 1) * half] = value.astype(F32)
-        for i in range(3):
-            outs[6 + i][:, c * inner : (c + 1) * inner] = last_ref[c, 0:rows, i * inner : (i + 1) * inner].astype(F32)
-
-
-def unpack(rest, last, own, down_rows):
-    parts, _, width = rest.shape
-    square = jax.ShapeDtypeStruct((own * parts, width), F32)
+        for b in range(width // 128):
+            low, end = b * piece, (b + 1) * piece
+            while low < end:
+                which, row = low // rows, low % rows
+                count = min(end - low, rows - row)
+                at = first + low - b * piece
+                value = rest_ref[c, at : at + count, b * 128 : (b + 1) * 128]
+                outs[6 + which][row : row + count, c * inner : (c + 1) * inner] = value.astype(F32)
+                low += count
+
+
+def unpack(rest, own, piece, rows, inner):
+    parts, total, width = rest.shape
+    down_rows = (total - 5 * own - piece - 16) * parts
+    square = jax.ShapeDtypeStruct((rows, width), F32)
     shapes = [square] * 5 + [jax.ShapeDtypeStruct((down_rows, width), F32)] + [square] * 3
     return pl.pallas_call(
-        functools.partial(unpack_kernel, own),
+        functools.partial(unpack_kernel, own, piece),
         grid=(1,),
         out_shape=shapes,
-        in_specs=[whole(rest.shape), whole(last.shape)],
+        in_specs=[whole(rest.shape)],
         out_specs=[whole(v.shape) for v in shapes],
         compiler_params=params(),
         cost_estimate=cost(0, 6 * rest.size),
         name="unpack",
-    )(rest, last)
+    )(rest)
 
 
 CTX = ("plane", "core")
 
 
+def copies(piece):
+    return jnp.broadcast_to(piece[None], (lax.axis_size("fsdp"),) + piece.shape)
+
+
 def spread(piece):
-    count = lax.axis_size("fsdp")
-    return lax.all_to_all(jnp.broadcast_to(piece[None], (count,) + piece.shape), "fsdp", 0, 0, tiled=True)
+    return lax.all_to_all(copies(piece), "fsdp", 0, 0, tiled=True)
 
 
 def collect(parts, *earlier):
@@ -867,24 +942,25 @@
     return lax.dynamic_index_in_dim(value, index, axis, keepdims=False)
 
 
-def gather_down(shard):
+def gather_down(shard, earlier):
     rows, width = shard.shape
     start = lax.axis_index("core") * (width // 2)
-    mine = spread(lax.dynamic_slice_in_dim(shard, start, width // 2, 1)).reshape(-1, width // 2)
+    mine = spread(after(lax.dynamic_slice_in_dim(shard, start, width // 2, 1), earlier)).reshape(-1, width // 2)
     return mine, swap(mine, "core")
 
 
-def reduce_planes(half):
+def reduce_planes(half, later):
     planes, width = lax.axis_size("plane"), half.shape[1]
     if planes != 4:
         return lax.psum_scatter(half, "plane", scatter_dimension=0, tiled=True)
     plane = lax.axis_index("plane")
-    for bit, size in ((1, 2), (2, 1)):
-        side = (plane // bit) % 2
-        split = half.reshape(size, 2, -1, width)
-        got = lax.ppermute(take(split, 1 - side, 1), "plane", [(i, i ^ bit) for i in range(4)])
-        half = (take(split, side, 1).astype(F32) + got.astype(F32)).astype(BF)
-    return half.reshape(-1, width)
+    quarters = half.reshape(planes, -1, width)
+    total = take(quarters, plane, 0).astype(F32)
+    for step in range(1, planes):
+        message = take(quarters, plane ^ step, 0)
+        got = lax.ppermute(message, "plane", [(i, i ^ step) for i in range(planes)])
+        total = total + after(got, later).astype(F32)
+    return total.astype(BF)
 
 
 def on_device(
@@ -895,6 +971,7 @@
 ):
     parts, shards = lax.axis_size(CTX), lax.axis_size("fsdp")
     place = lax.axis_index(CTX)
+    core = lax.axis_index("core").astype(jnp.int32).reshape(1)
     local, width = states.shape[1:]
     head_count = bias_table.shape[1]
     size = width // head_count
@@ -926,12 +1003,6 @@
     small = jnp.concatenate([self_gain, cross_gain, feed_gain, bias_table.reshape(-1)])
     small_width = small.shape[0]
     small = jnp.pad(small, (0, 16 * 3 * inner - small_width)).reshape(16, 3 * inner)
-    line = spread(jnp.concatenate([columns, small], axis=0))
-    qkv_weight = line[:, :shard_width].reshape(width, 3 * inner)
-    small = line[:, shard_width:].reshape(shards, -1)[:, :small_width].astype(F32)
-    gains = [small[:, i * shard_width : (i + 1) * shard_width].reshape(1, width) for i in range(3)]
-    table = small[:, 3 * shard_width :].reshape(BUCKETS, head_count)
-    own_table = lax.dynamic_slice_in_dim(table, place * heads, heads, 1).reshape(-1)
     first_pos, first_seg = positions[0, ::BLK], segments[0, ::BLK]
     canon = jnp.where(
         first_seg == 0,
@@ -940,10 +1011,20 @@
     )
     canon_all = lax.all_gather(canon, CTX, axis=0, tiled=True)
     slots = jnp.argmax(canon_all[None, :] == jnp.arange(blocks * parts)[:, None], axis=1).astype(jnp.int32)
-
-    squares = jnp.stack([own_rows(w) for w in (self_output, cross_query, cross_output, cross_key, cross_value)], axis=0)
-    squares = spread(after(squares, line, slots))
-    wide = spread(after(jnp.stack([own_rows(gate_weight), own_rows(up_weight)], axis=0), squares))
+    line = jnp.concatenate([columns, small], axis=0)
+    squares = [own_rows(w) for w in (self_output, cross_query, cross_output, cross_key, cross_value)]
+    wide = copies(jnp.stack([own_rows(gate_weight), own_rows(up_weight)], axis=0))
+    squares = spread(jnp.concatenate(squares + [line.reshape(-1, width)], axis=0))
+    squares = after(squares, slots, wide)
+    line = squares[:, 5 * own :].reshape((shards,) + line.shape)
+    squares = squares[:, : 5 * own].reshape(shards, 5, own, width)
+    qkv_weight = line[:, :shard_width].reshape(width, 3 * inner)
+    small = line[:, shard_width:].reshape(shards, -1)[:, :small_width].astype(F32)
+    gains = [small[:, i * shard_width : (i + 1) * shard_width].reshape(1, width) for i in range(3)]
+    table = small[:, 3 * shard_width :].reshape(BUCKETS, head_count)
+    own_table = lax.dynamic_slice_in_dim(table, place * heads, heads, 1).reshape(-1)
+
+    wide = lax.all_to_all(after(wide, squares), "fsdp", 0, 0, tiled=True)
     squares = lax.all_gather(squares, CTX, axis=0, tiled=False)
 
     prompt_tiles = PROMPT // TILE
@@ -953,67 +1034,78 @@
 
     wide = lax.all_gather(after(wide, o), CTX, axis=0, tiled=False)
     squares, wide = arranged(squares), arranged(wide)
-    down, other_down = gather_down(after(down_weight, o))
+    down, other_down = gather_down(down_weight, o)
     ckv = source_projection(encoded_all, squares)
     ob, x1, cq, cob, cot, cross_lse, x2, n3 = middle_forward(
         o, states[0], gains[1], gains[2], squares, ckv, head_count
     )
     qkv_all = lax.all_gather(after(qkv_weight, x2), CTX, axis=0, tiled=False)
-    layer_out, dx2, feed_gain_part, g_wide, g_down, g_other = feed_forward(
-        lax.axis_index("core").astype(jnp.int32).reshape(1), n3, cotangent[0], x2, gains[2], wide, down, other_down
+    hidden, dx2, feed_gain_part, g_wide, g_down, g_other = feed_forward(
+        core, n3, cotangent[0], x2, gains[2], wide, down, other_down
     )
     g_wide = lax.psum_scatter(scattered(g_wide), CTX, scatter_dimension=0, tiled=False)
     g_down = (g_down.astype(F32) + swap(g_other, "core").astype(F32)).astype(BF).reshape(shards, -1, width // 2)
     dx1, cross_gain_part, dcq, dckv, dso = middle_back(
-        after(dx2, qkv_all), x1, gains[1], squares, cq, ckv, cot, cross_lse, head_count, parts
+        (qkv_all,), dx2, x1, gains[1], squares, cq, ckv, cot, cross_lse, head_count, parts
     )
     dso = lax.all_to_all(dso, CTX, 0, 0, tiled=True).reshape(parts * blocks, BLK, inner)
-    g_squares = middle_grads(dx2, x1, gains[1], cob, dcq, dckv, encoded_all, ob, dx1, squares)
+    g_squares = middle_grads(dx2, x1, gains[1], cob, after(dcq, g_down), dckv, encoded_all, ob, dx1, squares)
     if not aligned:
         encoded_part = g_squares[0, 5 * width :].reshape(parts, -1, width)
         g_squares = scattered(g_squares[0, : 5 * width].reshape(1, 1, 5, width, width)).reshape(parts, -1, width)
         g_squares = jnp.concatenate([g_squares, encoded_part], axis=1)
     middle = prompt_tiles + (blocks * parts * BLK // TILE - prompt_tiles) // 4
-    held = sa_bwd(slots, own_table, qkv, after(dso, g_down, g_squares), ot, lse, heads, prompt_tiles, 0, middle)
+    g_squares = after(g_squares, dso)
+    held = sa_bwd((g_squares,), slots, own_table, qkv, dso, ot, lse, heads, prompt_tiles, 0, middle)
     g_squares = lax.psum_scatter(g_squares, CTX, scatter_dimension=0, tiled=False)
     g_down = collect(after(g_down, dso), held[0])
     dqkv, dtable = sa_bwd(
-        slots, own_table, qkv, after(dso, g_wide), ot, lse, heads, prompt_tiles, middle,
+        (g_wide,), slots, own_table, qkv, dso, ot, lse, heads, prompt_tiles, middle,
         blocks * parts * BLK // TILE, held,
     )
     g_wide = collect(after(g_wide, g_down), dqkv)
-    g_squares = after(g_squares, g_wide)
-    g_squares_sum = collect(g_squares[: shards * 5 * own].reshape(shards, 5 * own, width))
-    dqkv_local = lax.all_to_all(after(dqkv, g_squares_sum).reshape(parts, local, 3 * inner), CTX, 0, 0, tiled=True)
-    states_grad = final_back(dqkv_local, qkv_all, states[0], gains[0], dx1)
-    g_wide = lax.all_gather(g_wide, CTX, axis=0, tiled=False)
+    g_down = reduce_planes(g_down, dqkv)
+    dqkv_local = lax.all_to_all(after(dqkv, g_wide, g_down).reshape(parts, local, 3 * inner), CTX, 0, 0, tiled=True)
+    g_down = jnp.concatenate([g_down[: g_down.shape[0] // 2], g_down[g_down.shape[0] // 2 :]], axis=1)
     grads = dqkv.reshape(parts * local, 3 * inner)
-    g_qkv, self_gain_part = last_projection(gathered, gains[0], qkv_weight, grads, local)
-    g_down = reduce_planes(g_down)
-    encoded_grad = g_squares[shards * 5 * own :].astype(F32)
+    compact = aligned and inner == 128 and (3 * inner // shards) % 16 == 0
+    g_qkv, self_gain_part = last_projection(gathered, gains[0], qkv_weight, grads, local, shards if compact else 0)
     table_part = jnp.zeros((BUCKETS, head_count), F32)
     table_part = lax.dynamic_update_slice_in_dim(table_part, dtable[:, :, 0].T, place * heads, 1)
     sums = [self_gain_part[:, 0] / gains[0][0], cross_gain_part[0], feed_gain_part[0]]
     sums = jnp.concatenate([v.reshape(shards, shard_width) for v in sums] + [table_part.reshape(shards, -1)], axis=1)
-    sums = jnp.pad(sums, ((0, 0), (0, 16 * 3 * inner - small_width))).reshape(shards, 16, 3 * inner).astype(BF)
-    last = jnp.concatenate([g_qkv.reshape(shards, shard_width, 3 * inner), sums], axis=1)
-    last = collect_far(last).astype(BF)
-    g_down = jnp.concatenate([g_down[: g_down.shape[0] // 2], g_down[g_down.shape[0] // 2 :]], axis=1)
-    rest = jnp.concatenate([g_squares_sum, g_down], axis=0)
-    rest = lax.all_gather(after(rest, g_wide), CTX, axis=0, tiled=False)
-    last = lax.all_gather(after(last, rest, dqkv_local), CTX, axis=0, tiled=False)
-    sums = jnp.sum(last[:, shard_width:].reshape(parts, -1)[:, :small_width].astype(F32), axis=0)
-    gain_grads = [sums[i * shard_width : (i + 1) * shard_width] for i in range(3)]
-    table_grad = sums[3 * shard_width :].reshape(-1, head_count)
-    g_wide = g_wide.astype(F32).transpose(1, 0, 2, 3).reshape(2, shard_width, hidden_width)
-    if aligned:
-        *g_squares, g_down, g_query, g_key, g_value = unpack(rest, last, own, down_weight.shape[0])
+    if compact:
+        sums = jnp.pad(sums, ((0, 0), (0, 16 * width - small_width))).reshape(shards, 16, width).astype(BF)
+        last = jnp.concatenate([g_qkv, sums], axis=1)
     else:
+        sums = jnp.pad(sums, ((0, 0), (0, 16 * 3 * inner - small_width))).reshape(shards, 16, 3 * inner).astype(BF)
+        last = jnp.concatenate([g_qkv.reshape(shards, shard_width, 3 * inner), sums], axis=1).reshape(shards, -1, width)
+    g_squares = after(g_squares, g_wide, g_qkv)
+    encoded_grad = g_squares[shards * 5 * own :].astype(F32)
+    last_rows = last.shape[1]
+    rest = jnp.concatenate([g_squares[: shards * 5 * own].reshape(shards, 5 * own, width), last], axis=1)
+    rest = collect_far(rest).astype(BF)
+    layer_out = layer_output((dqkv,), core, hidden, x2, down, other_down)
+    states_grad = final_back(dqkv_local, qkv_all, states[0], gains[0], dx1)
+    g_wide = lax.all_gather(g_wide, CTX, axis=0, tiled=False)
+    rest = jnp.concatenate([rest, g_down], axis=0)
+    rest = lax.all_gather(after(rest, g_wide, dqkv_local), CTX, axis=0, tiled=False)
+    if compact:
+        sums_at = 5 * own + g_qkv.shape[1]
+        *g_squares, g_down, g_query, g_key, g_value = unpack(rest, own, g_qkv.shape[1], shard_width, inner)
+        sums = jnp.sum(rest[:, sums_at].astype(F32), axis=0)
+    else:
+        last = rest[:, 5 * own : 5 * own + last_rows].reshape(parts, -1, 3 * inner)
+        sums = jnp.sum(last[:, shard_width:].reshape(parts, -1).astype(F32), axis=0)
         rest = rest.astype(F32)
         g_squares = rest[:, : 5 * own].reshape(parts, 5, own, width).transpose(1, 0, 2, 3).reshape(5, shard_width, width)
-        g_down = rest[:, 5 * own :].reshape(parts // 2, 2, -1, 2, width // 2).transpose(0, 3, 2, 1, 4).reshape(-1, width)
+        g_down = rest[:, 5 * own + last_rows :].reshape(parts // 2, 2, -1, 2, width // 2).transpose(0, 3, 2, 1, 4)
+        g_down = g_down.reshape(-1, width)
         g_qkv = last[:, :shard_width].astype(F32).reshape(parts, shard_width, 3, inner).transpose(2, 1, 0, 3)
         g_query, g_key, g_value = g_qkv.reshape(3, shard_width, width)
+    gain_grads = [sums[i * shard_width : (i + 1) * shard_width] for i in range(3)]
+    table_grad = sums[3 * shard_width : small_width].reshape(-1, head_count)
+    g_wide = g_wide.astype(F32).transpose(1, 0, 2, 3).reshape(2, shard_width, hidden_width)
     return (
         layer_out[None], states_grad[None], encoded_grad[None],
         gain_grads[0], g_query, g_key, g_value, g_squares[0], table_grad,

time: 618 us -> 604 us (0.977)
  waiting for transfers between devices: 117 us -> 153 us
  blocking collectives: 64.8 us -> 32.7 us
  local copies, waits for them, and re-layouts: 53.6 us -> 43.7 us
  starting transfers between devices: 61.3 us -> 55.1 us
    all_to_all x1 -> x0, blocking collectives: 34.1 us -> none  [spread(): lax.all_to_all(jnp.broadcast_to(piece[None], (count,) + piece.shape), 'fs...]
    all_to_all x4, waiting for transfers between devices: 38.4 us -> 66 us  [the longest x2 66 us: spread(): return lax.all_to_all(copies(piece), 'fsdp', 0, 0, tiled=True)]
    all_to_all x3 -> x2, waiting for transfers between devices: 29.1 us -> 3.03 us  [collect(): parts = lax.all_to_all(parts, 'fsdp', 0, 0, tiled=True)]
    all_gather x2 -> x1, waiting for transfers between devices: 7.72 us -> 30.6 us  [on_device(): lax.all_gather(after(rest, g_wide, dqkv_local), CTX, axis=0, tiled=False)]
    ppermute x6, waiting for transfers between devices: 8.73 us -> 25.9 us  [collect_far(): total = total + lax.ppermute(message, 'fsdp', pairs).astype(F32)]
    ppermute x2 -> x3, waiting for transfers between devices: 16.6 us -> 0.01 us  [reduce_planes(): got = lax.ppermute(message, 'plane', [(i, i ^ step) for i in range(planes)])]
    unnamed x86 -> x80, local copies, waits for them, and re-layouts: 31 us -> 16.5 us
    all_to_all x1, waiting for transfers between devices: 8.73 us -> 21.1 us  [on_device(): lax.all_to_all(dso, CTX, 0, 0, tiled=True)]
  transfers between devices with their start and end apart: 27 -> 26, of which waited for: 13 -> 10; matrix products, arithmetic and copies ran while one was open for 9% -> 10% of each run, Pallas kernels for 44% -> 45%
where the time goes in v4:
time: 604 us; the launch traced here: 598 us
  Pallas kernels  273 us (45%)
  waiting for transfers between devices  153 us (25%)
  starting transfers between devices  55.1 us (9%)
  local copies, waits for them, and re-layouts  43.7 us (7%)
  blocking collectives  32.7 us (5%)
  other arithmetic  25 us (4%)
  between operations  15.7 us (3%)
    pallas_call x2, Pallas kernels, sa_bwd(): pl.pallas_call(leaving_out(functools.partial(bwd_kernel, heads, prompt_ti...  73.1 us
    all_to_all x2, waiting for transfers between devices, spread(): return lax.all_to_all(copies(piece), 'fsdp', 0, 0, tiled=True)  66 us
    pallas_call x1, Pallas kernels, feed_forward(): pl.pallas_call(feed_kernel, grid=(steps,), out_shape=[jax.ShapeDtypeStruc...  36.1 us
    all_gather x1, waiting for transfers between devices, on_device(): lax.all_gather(after(rest, g_wide, dqkv_local), CTX, axis=0, tiled=False)  30.6 us
    pallas_call x1, Pallas kernels, middle_forward(): pl.pallas_call(functools.partial(middle_kernel, head_count), grid=(1,), o...  29.4 us
    pallas_call x1, Pallas kernels, sa_fwd(): pl.pallas_call(functools.partial(fwd_kernel, heads, prompt_tiles), out_sh...  28.1 us
    pallas_call x1, Pallas kernels, middle_back(): pl.pallas_call(leaving_out(functools.partial(middle_back_kernel, head_cou...  26.5 us
    ppermute x6, waiting for transfers between devices, collect_far(): total = total + lax.ppermute(message, 'fsdp', pairs).astype(F32)  25.9 us
  transfers between devices with their start and end apart: 26, of which 10 were waited for; matrix products, arithmetic and copies ran while one was open for 10% of the time, Pallas kernels for 45%

profile of v4, /device:TPU:0, one launch (start us, length us, event | category | flops | bytes accessed | tf_op | source)
XLA Modules:
  0.0 598.0 jit_solution(16809147621144989712)
XLA Ops:
  7.3 2.5 pad_maximum_fusion.1
  17.1 1.6 broadcast_in_dim.17
  18.7 6.4 %all-to-all-start = ((bf16[4,262,1024]{2,1,0:T(8,128)(2,1)}), bf16[4,262,1024]{2,1,0:T(8,128)(2,1)}, u32[]{:S(2)}, u32[]{:S(2)}) async-start(bf16[4,262,1024]{2,1,0:T(8,128)(2,1)} %broadcast_in_dim.17), calls=%async_computation | async-start | bytes 4325376 | tf_op jit(solution)/shard_map/all_to_all | solution.py:894
  28.1 8.1 %all-reduce.2 = s32[32]{0:T(128)S(1)} all-reduce(s32[32]{0:T(128)S(1)} %fusion.27), channel_id=1, replica_groups=mesh['plane'=4,'core'=2,'fsdp'=4] {'plane','core'}, use_global_device_ids=true, to_apply=%add.2 | all-reduce | flops 32 | bytes 256
  37.9 37.0 %all-to-all-done.refs_0_ = bf16[4,262,1024]{2,1,0:T(8,128)(2,1)} async-done(((bf16[4,262,1024]{2,1,0:T(8,128)(2,1)}), bf16[4,262,1024]{2,1,0:T(8,128)(2,1)}, u32[]{:S(2)}, u32[]{:S(2)}) %all-to-all-start) | async-done | bytes 2146336 | tf_op jit(solution)/shard_map/all_to_all | solution.py:894
  76.1 2.5 slice.114
  83.2 3.6 all-to-all-start.2
  87.4 11.1 %first_projection.1 = bf16[4096,384]{1,0:T(8,128)(2,1)} custom-call(bf16[8,576,1024]{2,1,0:T(8,128)(2,1)} %bitcast.154, f32[1,1024]{1,0:T(1,128)} %bitcast.158, bf16[1024,384]{1,0:T(8,128)(2,1)} %bitcast.138), custom_call_target="tpu_custom_call" | custom-call | flops 6442450944 | bytes 11534336 | tf_op jit(solution)/shard_map/first_projection/pallas_call | solution.py:781
  98.5 28.1 %self_attention_forward.1 = (bf16[32,128,128]{2,1,0:T(8,128)(2,1)}, f32[128,4096]{1,0:T(8,128)}, f32[2,4096]{1,0:T(2,128)}) custom-call(s32[32]{0:T(128)} %get-tuple-element.58.refs_1_.slots, f32[64]{0:T(128)} %reshape.157.tab.refs_2_, bf16[32,128,384]{2,1,0:T(8,128)(2,1)} %bitcast.169), custom_call_target="tpu_custom_call" | custom-call | flops 32000000000 | bytes 12582912 | tf_op jit(solution)/shard_map/self_attention_forward/pallas_call | solution.py:137
  126.7 24.5 %all_to_all.40.o_ref.refs_1_ = bf16[8,512,128]{2,1,0:T(8,128)(2,1)} all-to-all(bf16[8,512,128]{2,1,0:T(8,128)(2,1)} %bitcast.149), channel_id=1, replica_groups=mesh['plane'=4,'core'=2,'fsdp'=4] {'plane','core'}, dimensions={0} | all-to-all | bytes 2097152 | tf_op jit(solution)/shard_map/all_to_all | solution.py:1033
  154.7 2.3 slice.115
  156.9 2.9 broadcast_in_dim.37
  159.9 4.6 all-to-all-start.3
  164.8 5.4 source_projection.1.ckv_ref.refs_8_
  170.2 29.4 %middle_forward.1 = (bf16[512,1024]{1,0:T(8,128)(2,1)}, f32[512,1024]{1,0:T(8,128)}, bf16[512,1024]{1,0:T(8,128)(2,1)}, bf16[512,1024]{1,0:T(8,128)(2,1)}, f32[8...) custom-call(bf16[8,512,128]{2,1,0:T(8,128)(2,1)} %all_to_all.40.o_ref.refs_1_, ...), custom_call_target="tpu_custom_call" | custom-call | flops 32212254720 | bytes 12582912 | tf_op jit(solution)/shard_map/middle_forward/pallas_call | solution.py:456
  199.6 29.1 %all-to-all-done.3 = bf16[4,704,512]{2,1,0:T(8,128)(2,1)} async-done(((bf16[4,704,512]{2,1,0:T(8,128)(2,1)}), bf16[4,704,512]{2,1,0:T(8,128)(2,1)}, u32[]{:S(2)}, u32[]{:S(2)}) %all-to-all-start.3) | async-done | bytes 2883616 | tf_op jit(solution)/shard_map/all_to_all | solution.py:894
  228.7 5.6 collective-permute-done.other_ref.refs_5_
  234.3 36.1 %feed_forward.1 = (bf16[512,2816]{1,0:T(8,128)(2,1)}, f32[512,1024]{1,0:T(8,128)}, f32[1,1024]{1,0:T(1,128)}, bf16[8,4,2,32,2816]{4,3,2,1,0:T(8,128)(2,1)}, bf16...) custom-call(s32[1]{0:T(128)} %bitcast.core_ref.refs_1_, bf16[512,1024]{1,0:T(8,128)(2,1)} %get-tuple-element.60.n3_ref, ...), custom_call_target="tpu_custom_call" | custom-call | flops 41339060224 | bytes 34603008 | tf_op jit(solution)/shard_map/feed_forward/pallas_call | solution.py:535
  270.7 26.5 %middle_back.1 = (f32[512,1024]{1,0:T(8,128)}, f32[1,1024]{1,0:T(1,128)}, bf16[512,1024]{1,0:T(8,128)(2,1)}, bf16[2,512,1024]{2,1,0:T(8,128)(2,1)}, bf16[8,512,128]{2,1,0:T(8,128)(2,1)}) custom-call(bf16[8,1024,384]{2,1,0:T(8,128)(2,1)} %bitcast.127, f32[512,1024]{1,0:T(8,128)} %get-tuple-element.63.refs_1_.dx2_ref, ...), custom_call_target="tpu_custom_call" | custom-call | flops 32212254720 | bytes 12582912 | tf_op jit(solution)/shard_map/middle_back/pallas_call | solution.py:660
  297.2 3.6 all-to-all-start.4
  301.5 5.1 add_convert_fusion
  306.6 21.1 %all-to-all-done.4 = bf16[8,512,128]{2,1,0:T(8,128)(2,1)S(1)} async-done(((bf16[8,512,128]{2,1,0:T(8,128)(2,1)}), bf16[8,512,128]{2,1,0:T(8,128)(2,1)S(1)}, u32[]{:S(2)}, u32[]{:S(2)}) %all-to-all-start.4) | async-done | bytes 1048608 | tf_op jit(solution)/shard_map/all_to_all | solution.py:1051
  328.7 4.6 all-to-all-start.5
  333.6 22.6 %middle_grads.1.refs_0_ = bf16[8,704,1024]{2,1,0:T(8,128)(2,1)} custom-call(f32[512,1024]{1,0:T(8,128)} %get-tuple-element.63.refs_1_.dx2_ref, f32[512,1024]{1,0:T(8,128)} %get-tuple-element.64.refs_2_.x1_ref, f32[1,1024]{1,0:T(1,128)} %bitcast.163, bf16[512,1024]{1,0:T(8,128)(2,1)} %get-tuple-element.71.cob_ref, bf16[512,1024]{1,0:T(8,128)(2,1)} %after.22.dcq_ref, ...), custom_call_target="tpu_custom_call" | custom-call | flops 24696061952 | bytes 12582912 | tf_op jit(solution)/shard_map/middle_grads/pallas_call | solution.py:723
  356.2 36.3 %self_attention_backward.2 = (bf16[2560,128]{1,0:T(8,128)(2,1)}, f32[4096,256]{1,0:T(8,128)}, f32[2,2,128,128]{3,2,1,0:T(8,128)}, f32[2,8,256]{2,1,0:T(8,128)}) custom-call(bf16[8,704,1024]{2,1,0:T(8,128)(2,1)} %after.23.refs_0_, s32[32]{0:T(128)} %get-tuple-element.58.refs_1_.slots, f32[64]{0:T(128)} %reshape.157.tab.refs_2_, ...), custom_call_target="tpu_custom_call" | custom-call | flops 43000000512 | bytes 18874368 | tf_op jit(solution)/shard_map/self_attention_backward/pallas_call | solution.py:285
  392.5 3.0 all-to-all-done.5.refs_0_
  395.6 3.3 reduce_sum.33.refs_1_
  398.9 2.6 copy.100.refs_0_
  401.5 4.3 all-to-all-start.6
  406.2 36.8 %self_attention_backward.3 = (bf16[32,128,384]{2,1,0:T(8,128)(2,1)}, f32[2,32,128]{2,1,0:T(8,128)}) custom-call(bf16[4,2,32,2816]{3,2,1,0:T(8,128)(2,1)} %bitcast.148, s32[32]{0:T(128)} %get-tuple-element.58.refs_1_.slots, f32[64]{0:T(128)} %reshape.157.tab.refs_2_, bf16[32,128,384]{2,1,0:T(8,128)(2,1)} %bitcast.171, bf16[32,128,128]{2,1,0:T(8,128)(2,1)} %bitcast.124, ...), custom_call_target="tpu_custom_call" | custom-call | flops 249999998976 | bytes 18874368 | tf_op jit(solution)/shard_map/self_attention_backward/pallas_call | solution.py:285
  443.1 2.5 reduce_sum.34.refs_1_
  445.7 2.6 collective-permute-start.4
  449.3 12.5 %last_projection.1 = (bf16[4,96,1024]{2,1,0:T(8,128)(2,1)}, f32[1024,1]{1,0:T(8,128)}) custom-call(bf16[8,576,1024]{2,1,0:T(8,128)(2,1)} %bitcast.156, f32[1,1024]{1,0:T(1,128)} %bitcast.159, bf16[1024,384]{1,0:T(8,128)(2,1)} %bitcast.139, bf16[4096,384]{1,0:T(8,128)(2,1)} %bitcast.113), custom_call_target="tpu_custom_call" | custom-call | flops 6442450944 | bytes 11534336 | tf_op jit(solution)/shard_map/last_projection/pallas_call | solution.py:829
  461.8 1.6 copy.105.refs_0_
  466.9 1.7 fusion.8.refs_2_
  468.6 4.4 all-to-all-start.7
  478.5 6.4 %collective-permute-start.9 = (bf16[272,1024]{1,0:T(8,128)(2,1)}, bf16[272,1024]{1,0:T(8,128)(2,1)S(1)}, u32[]{:S(2)}, u32[]{:S(2)}) collective-permute-start(bf16[272,1024]{1,0:T(8,128)(2,1)} %get-tuple-element.102), channel_id=1, source_target_pairs={{0,3},{4,7},{8,11},{12,15},{16,19},{20,23},{24,27},{28,31}} | collective-permute-start | bytes 1671176 | tf_op jit(solution)/shard_map/ppermute | solution.py:913
  486.2 5.5 collective-permute-start.7
  493.0 3.4 collective-permute-done.10
  496.4 2.2 collective-permute-start.5
  498.7 21.0 %collective-permute-done.8 = bf16[272,1024]{1,0:T(8,128)(2,1)S(1)} collective-permute-done((bf16[272,1024]{1,0:T(8,128)(2,1)}, bf16[272,1024]{1,0:T(8,128)(2,1)S(1)}, u32[]{:S(2)}, u32[]{:S(2)}) %collective-permute-start.8) | collective-permute-done | bytes 557088 | tf_op jit(solution)/shard_map/ppermute | solution.py:913
  521.2 2.2 fusion.5
  524.3 8.1 %layer_output.1 = bf16[512,1024]{1,0:T(8,128)(2,1)} custom-call(bf16[32,128,384]{2,1,0:T(8,128)(2,1)} %get-tuple-element.82.refs_0_.refs_1_, s32[1]{0:T(128)} %bitcast.core_ref.refs_1_, bf16[512,2816]{1,0:T(8,128)(2,1)} %get-tuple-element.83.refs_2_, f32[512,1024]{1,0:T(8,128)} %get-tuple-element.61.x2_ref.refs_1_.refs_3_, ...), custom_call_target="tpu_custom_call" | custom-call | flops 5905580032 | bytes 11534336 | tf_op jit(solution)/shard_map/layer_output/pallas_call | solution.py:572
  532.4 1.6 fusion.18
  534.0 13.1 %final_back.1 = f32[512,1024]{1,0:T(8,128)} custom-call(bf16[8,512,384]{2,1,0:T(8,128)(2,1)} %all-to-all-done.7.d_ref.refs_2_, bf16[8,1024,384]{2,1,0:T(8,128)(2,1)} %bitcast.128, bf16[512,1024]{1,0:T(8,128)(2,1)} %bitcast.135, f32[1,1024]{1,0:T(1,128)} %bitcast.160, f32[512,1024]{1,0:T(8,128)} %get-tuple-element.77.dx1_ref), custom_call_target="tpu_custom_call" | custom-call | flops 3221225472 | bytes 6291456 | tf_op jit(solution)/shard_map/final_back/pallas_call | solution.py:754
  547.7 3.1 fusion.29
  550.8 30.6 %all-gather.22.cloned.1.call-done = bf16[2880,1024]{1,0:T(8,128)(2,1)} async-done(((bf16[360,1024]{1,0:T(8,128)(2,1)}), bf16[2880,1024]{1,0:T(8,128)(2,1)}) %all-gather.22.cloned.1.call-update) | async-done | bytes 5898256 | tf_op jit(solution)/shard_map/all_gather | solution.py:1092
  582.5 7.3 %unpack.1 = (f32[256,1024]{1,0:T(8,128)}, f32[256,1024]{1,0:T(8,128)}, f32[256,1024]{1,0:T(8,128)}, f32[256,1024]{1,0:T(8,128)}, f32[256,1024]{1,0:T(8,128)}, /*...) custom-call(bf16[8,360,1024]{2,1,0:T(8,128)(2,1)} %bitcast.130), custom_call_target="tpu_custom_call" | custom-call | bytes 17694720 | tf_op jit(solution)/shard_map/unpack/pallas_call | solution.py:874
  (185 shorter events, 41.6 us)
Async XLA Ops:
  7.2 144.1 %copy-start = (bf16[704,1024]{1,0:T(8,128)(2,1)S(1)}, bf16[704,1024]{1,0:T(8,128)(2,1)}, u32[]{:S(2)}) copy-start(bf16[704,1024]{1,0:T(8,128)(2,1)} %param.39) | copy-start | bytes 4325380
  7.2 2.7 copy-start.25
  7.2 2.8 copy-start.26
  7.2 2.8 copy-start.27
  7.2 2.8 copy-start.28
  7.2 3.5 copy-start.17
  7.3 80.1 %all-gather.14.cloned.1.call-start = ((), (), s32[]{:S(2)}) async-start(), calls=%async_computation.13 | async-start | bytes 10616832 | tf_op jit(solution)/shard_map/all_gather | solution.py:998
  7.3 3.7 copy-start.18
  18.7 8.0 %copy-start.29 = (u32[32]{0:T(128)S(1)}, u32[32]{0:T(128)}, u32[]{:S(2)}) copy-start(u32[32]{0:T(128)} %constant.123) | copy-start | bytes 388
  18.7 56.2 %all-to-all-start = ((bf16[4,262,1024]{2,1,0:T(8,128)(2,1)}), bf16[4,262,1024]{2,1,0:T(8,128)(2,1)}, u32[]{:S(2)}, u32[]{:S(2)}) async-start(bf16[4,262,1024]{2,1,0:T(8,128)(2,1)} %broadcast_in_dim.17), calls=%async_computation | async-start | bytes 4325376 | tf_op jit(solution)/shard_map/all_to_all | solution.py:894
  25.2 139.6 %all-gather.12.cloned.1.call-start = ((), (), s32[]{:S(2)}) async-start(), calls=%async_computation.10 | async-start | bytes 11796480 | tf_op jit(solution)/shard_map/all_gather | solution.py:1028
  81.8 1.4 copy-start.20
  83.2 43.5 %all-to-all-start.2 = ((bf16[4,2,32,2816]{3,2,1,0:T(8,128)(2,1)}), bf16[4,2,32,2816]{3,2,1,0:T(8,128)(2,1)S(1)}, u32[]{:S(2)}, u32[]{:S(2)}) async-start(bf16[4,2,32,2816]{3,2,1,0:T(8,128)(2,1)} %after.18), calls=%async_computation.2 | async-start | bytes 2883584 | tf_op jit(solution)/shard_map/all_to_all | solution.py:1027
  86.8 147.5 %all-gather.16.cloned.1.call-start = ((), (), s32[]{:S(2)}) async-start(), calls=%async_computation.14 | async-start | bytes 12976128 | tf_op jit(solution)/shard_map/all_gather | solution.py:1035
  126.7 24.5 %copy-start.4 = (bf16[4,2,32,2816]{3,2,1,0:T(8,128)(2,1)}, bf16[4,2,32,2816]{3,2,1,0:T(8,128)(2,1)S(1)}, u32[]{:S(2)}) copy-start(bf16[4,2,32,2816]{3,2,1,0:T(8,128)(2,1)S(1)} %all-to-all-done.2.refs_0_) | copy-start | bytes 4325380
  159.9 68.8 %all-to-all-start.3 = ((bf16[4,704,512]{2,1,0:T(8,128)(2,1)}), bf16[4,704,512]{2,1,0:T(8,128)(2,1)}, u32[]{:S(2)}, u32[]{:S(2)}) async-start(bf16[4,704,512]{2,1,0:T(8,128)(2,1)} %broadcast_in_dim.37), calls=%async_computation.3 | async-start | bytes 5767168 | tf_op jit(solution)/shard_map/all_to_all | solution.py:894
  164.5 106.2 %all-gather.18.cloned.1.call-start = ((), (), s32[]{:S(2)}) async-start(), calls=%async_computation.15 | async-start | bytes 7077888 | tf_op jit(solution)/shard_map/all_gather | solution.py:1042
  199.6 199.3 %reduce-scatter.3.cloned.1.call-start = ((), (), s32[]{:S(2)}) async-start(), calls=%async_computation.11 | async-start | bytes 12976128 | tf_op jit(solution)/shard_map/reduce_scatter | solution.py:1046
  228.7 5.6 collective-permute-start
  270.5 30.9 %collective-permute-start.1 = (bf16[2816,512]{1,0:T(8,128)(2,1)}, bf16[2816,512]{1,0:T(8,128)(2,1)}, u32[]{:S(2)}, u32[]{:S(2)}) collective-permute-start(bf16[2816,512]{1,0:T(8,128)(2,1)} %get-tuple-element.74), channel_id=1, source_target_pairs={{0,4},{4,0},{1,5},{5,1},{2,6},{6,2},{3,7},{7,3},{8,12},{12,8},{9,1... | collective-permute-start | bytes 8650760 | tf_op jit(solution)/shard_map/ppermute | solution.py:938
  270.7 30.1 %copy-start.24 = (f32[1,1024]{1,0:T(1,128)S(1)}, f32[1,1024]{1,0:T(1,128)}, u32[]{:S(2)}) copy-start(f32[1,1024]{1,0:T(1,128)} %get-tuple-element.87) | copy-start | bytes 12292
  297.2 30.5 %all-to-all-start.4 = ((bf16[8,512,128]{2,1,0:T(8,128)(2,1)}), bf16[8,512,128]{2,1,0:T(8,128)(2,1)S(1)}, u32[]{:S(2)}, u32[]{:S(2)}) async-start(bf16[8,512,128]{2,1,0:T(8,128)(2,1)} %get-tuple-element.68), calls=%async_computation.5 | async-start | bytes 2097152 | tf_op jit(solution)/shard_map/all_to_all | solution.py:1051
  328.7 66.9 %all-to-all-start.5 = ((bf16[4,704,512]{2,1,0:T(8,128)(2,1)}), bf16[4,704,512]{2,1,0:T(8,128)(2,1)}, u32[]{:S(2)}, u32[]{:S(2)}) async-start(bf16[4,704,512]{2,1,0:T(8,128)(2,1)} %after.24), calls=%async_computation.6 | async-start | bytes 5767168 | tf_op jit(solution)/shard_map/all_to_all | solution.py:898
  333.3 139.9 %reduce-scatter.5.cloned.1.call-start = ((), (), s32[]{:S(2)}) async-start(), calls=%async_computation.12 | async-start | bytes 12976128 | tf_op jit(solution)/shard_map/reduce_scatter | solution.py:1060
  401.5 41.6 %all-to-all-start.6 = ((bf16[4,2,32,2816]{3,2,1,0:T(8,128)(2,1)}), bf16[4,2,32,2816]{3,2,1,0:T(8,128)(2,1)}, u32[]{:S(2)}, u32[]{:S(2)}) async-start(bf16[4,2,32,2816]{3,2,1,0:T(8,128)(2,1)} %after.26), calls=%async_computation.7 | async-start | bytes 2883584 | tf_op jit(solution)/shard_map/all_to_all | solution.py:898
  405.8 118.5 %all-gather.20.cloned.1.call-start = ((), (), s32[]{:S(2)}) async-start(), calls=%async_computation.16 | async-start | bytes 3244032 | tf_op jit(solution)/shard_map/all_gather | solution.py:1090
  443.1 2.5 copy-start.23
  443.1 2.5 copy-start.22
  443.1 2.6 copy-start.7
  445.7 18.4 %collective-permute-start.4 = (bf16[176,512]{1,0:T(8,128)(2,1)S(1)}, bf16[176,512]{1,0:T(8,128)(2,1)S(1)}, u32[]{:S(2)}, u32[]{:S(2)}) collective-permute-start(bf16[176,512]{1,0:T(8,128)(2,1)S(1)} %get-tuple-element.107), channel_id=1, source_target_pairs={{0,24},{8,16},{16,8},{24,0},{1,25},{9,17},{17,9},{25,1},{2,26},{10... | collective-permute-start | bytes 540680 | tf_op jit(solution)/shard_map/ppermute | solution.py:961
  448.3 16.5 %collective-permute-start.3 = (bf16[176,512]{1,0:T(8,128)(2,1)S(1)}, bf16[176,512]{1,0:T(8,128)(2,1)S(1)}, u32[]{:S(2)}, u32[]{:S(2)}) collective-permute-start(bf16[176,512]{1,0:T(8,128)(2,1)S(1)} %get-tuple-element.108), channel_id=1, source_target_pairs={{0,16},{8,24},{16,0},{24,8},{1,17},{9,25},{17,1},{25,9},{2,18},{10... | collective-permute-start | bytes 540680 | tf_op jit(solution)/shard_map/ppermute | solution.py:961
  449.0 16.5 %collective-permute-start.2 = (bf16[176,512]{1,0:T(8,128)(2,1)S(1)}, bf16[176,512]{1,0:T(8,128)(2,1)S(1)}, u32[]{:S(2)}, u32[]{:S(2)}) collective-permute-start(bf16[176,512]{1,0:T(8,128)(2,1)S(1)} %get-tuple-element.106), channel_id=1, source_target_pairs={{0,8},{8,0},{16,24},{24,16},{1,9},{9,1},{17,25},{25,17},{2,10},{10... | collective-permute-start | bytes 540680 | tf_op jit(solution)/shard_map/ppermute | solution.py:961
  449.3 12.5 %copy-start.2 = (bf16[32,128,384]{2,1,0:T(8,128)(2,1)S(1)}, bf16[32,128,384]{2,1,0:T(8,128)(2,1)}, u32[]{:S(2)}) copy-start(bf16[32,128,384]{2,1,0:T(8,128)(2,1)} %get-tuple-element.82.refs_0_.refs_1_) | copy-start | bytes 9437188
  461.8 1.6 copy-start.21
  461.8 2.1 copy-start.16
  468.6 55.7 %all-to-all-start.7 = ((bf16[8,512,384]{2,1,0:T(8,128)(2,1)}), bf16[8,512,384]{2,1,0:T(8,128)(2,1)}, u32[]{:S(2)}, u32[]{:S(2)}) async-start(bf16[8,512,384]{2,1,0:T(8,128)(2,1)} %bitcast.116), calls=%async_computation.8 | async-start | bytes 6291456 | tf_op jit(solution)/shard_map/all_to_all | solution.py:1068
  473.0 108.4 %all-gather.22.cloned.1.call-start = ((), (), s32[]{:S(2)}) async-start(), calls=%async_computation.17 | async-start | bytes 6635520 | tf_op jit(solution)/shard_map/all_gather | solution.py:1092
  473.2 1.5 copy-start.9
  474.9 2.3 copy-start.3
  474.9 23.7 %copy-start.10 = (bf16[176,512]{1,0:T(8,128)(2,1)S(1)}, bf16[176,512]{1,0:T(8,128)(2,1)}, u32[]{:S(2)}) copy-start(bf16[176,512]{1,0:T(8,128)(2,1)} %fusion.8.refs_2_) | copy-start | bytes 540676
  477.2 19.2 %collective-permute-start.10 = (bf16[272,1024]{1,0:T(8,128)(2,1)S(1)}, bf16[272,1024]{1,0:T(8,128)(2,1)S(1)}, u32[]{:S(2)}, u32[]{:S(2)}) collective-permute-start(bf16[272,1024]{1,0:T(8,128)(2,1)S(1)} %get-tuple-element.101), channel_id=1, source_target_pairs={{3,0},{7,4},{11,8},{15,12},{19,16},{23,20},{27,24},{31,28}} | collective-permute-start | bytes 1671176 | tf_op jit(solution)/shard_map/ppermute | solution.py:913
  478.5 20.2 %collective-permute-start.9 = (bf16[272,1024]{1,0:T(8,128)(2,1)}, bf16[272,1024]{1,0:T(8,128)(2,1)S(1)}, u32[]{:S(2)}, u32[]{:S(2)}) collective-permute-start(bf16[272,1024]{1,0:T(8,128)(2,1)} %get-tuple-element.102), channel_id=1, source_target_pairs={{0,3},{4,7},{8,11},{12,15},{16,19},{20,23},{24,27},{28,31}} | collective-permute-start | bytes 1671176 | tf_op jit(solution)/shard_map/ppermute | solution.py:913
  484.9 34.8 %collective-permute-start.8 = (bf16[272,1024]{1,0:T(8,128)(2,1)}, bf16[272,1024]{1,0:T(8,128)(2,1)S(1)}, u32[]{:S(2)}, u32[]{:S(2)}) collective-permute-start(bf16[272,1024]{1,0:T(8,128)(2,1)} %get-tuple-element.103), channel_id=1, source_target_pairs={{2,0},{3,1},{6,4},{7,5},{10,8},{11,9},{14,12},{15,13},{18,16},{19,... | collective-permute-start | bytes 1671176 | tf_op jit(solution)/shard_map/ppermute | solution.py:913
  486.2 33.5 %collective-permute-start.7 = (bf16[272,1024]{1,0:T(8,128)(2,1)}, bf16[272,1024]{1,0:T(8,128)(2,1)S(1)}, u32[]{:S(2)}, u32[]{:S(2)}) collective-permute-start(bf16[272,1024]{1,0:T(8,128)(2,1)} %get-tuple-element.104), channel_id=1, source_target_pairs={{0,2},{1,3},{4,6},{5,7},{8,10},{9,11},{12,14},{13,15},{16,18},{17,... | collective-permute-start | bytes 1671176 | tf_op jit(solution)/shard_map/ppermute | solution.py:913
  491.7 28.2 %collective-permute-start.6 = (bf16[272,1024]{1,0:T(8,128)(2,1)}, bf16[272,1024]{1,0:T(8,128)(2,1)}, u32[]{:S(2)}, u32[]{:S(2)}) collective-permute-start(bf16[272,1024]{1,0:T(8,128)(2,1)} %get-tuple-element.105), channel_id=1, source_target_pairs={{1,0},{2,1},{3,2},{5,4},{6,5},{7,6},{9,8},{10,9},{11,10},{13,12},{... | collective-permute-start | bytes 1671176 | tf_op jit(solution)/shard_map/ppermute | solution.py:913
  496.4 24.8 %collective-permute-start.5 = (bf16[272,1024]{1,0:T(8,128)(2,1)}, bf16[272,1024]{1,0:T(8,128)(2,1)}, u32[]{:S(2)}, u32[]{:S(2)}) collective-permute-start(bf16[272,1024]{1,0:T(8,128)(2,1)} %get-tuple-element.100), channel_id=1, source_target_pairs={{0,1},{1,2},{2,3},{4,5},{5,6},{6,7},{8,9},{9,10},{10,11},{12,13},{... | collective-permute-start | bytes 1671176 | tf_op jit(solution)/shard_map/ppermute | solution.py:913
  534.0 13.1 %copy-start.5 = (bf16[16,32,2816]{2,1,0:T(8,128)(2,1)S(1)}, bf16[16,32,2816]{2,1,0:T(8,128)(2,1)}, u32[]{:S(2)}) copy-start(bf16[16,32,2816]{2,1,0:T(8,128)(2,1)} %all-gather.20.cloned.1.call-done) | copy-start | bytes 8650756
  581.4 9.6 %copy-start.1 = (bf16[704,1024]{1,0:T(8,128)(2,1)S(1)}, bf16[704,1024]{1,0:T(8,128)(2,1)}, u32[]{:S(2)}) copy-start(bf16[704,1024]{1,0:T(8,128)(2,1)} %param.39) | copy-start | bytes 4325380
  (8 other events, 8.5 us)
Sparse Core Ops, SparseCore 0:
  10.6 61.6 all-gather.13
  78.7 70.8 all-gather.11
  152.1 68.9 all-gather.15
  223.4 45.5 all-gather.17
  272.3 98.0 reduce-scatter.2
  373.7 94.5 reduce-scatter.4
  470.7 46.8 all-gather.19
  524.4 56.9 all-gather.21

commit v5 on v4

--- a/solution.py
+++ b/solution.py
@@ -93,33 +93,34 @@
 
     def tile_body(t,n_far,own_static):
         q=load_tile(qkv,slots,t,0,width)
+        qh=[head_mask(q,h,heads) for h in range(heads)]
+        own_rows_at=pl.ds(t*TILE if own_static else pl.multiple_of(t*TILE,TILE),TILE)
+        def make(h,j):
+            rows=pl.ds(j*TILE,TILE) if j<n_far else own_rows_at
+            s=scores(rows,h,"own" if j==n_far else "prev" if j==n_far-1 else "far",qh[h])
+            s_scr[h,j]=s
+            return jnp.max(s.reshape(TILE//8,8,TILE),axis=0)
         outs=[]
+        peak=None
+        for j in range(n_far+1):
+            part=make(0,j)
+            peak=part if peak is None else jnp.maximum(peak,part)
         for h in range(heads):
-            qh=head_mask(q,h,heads)
-            m=None
+            m=jnp.max(peak,axis=0,keepdims=True)
+            l=None; acc=None; peak=None
             for j in range(n_far+1):
-                if j<n_far:
-                    rows=pl.ds(j*TILE,TILE); kind="prev" if j==n_far-1 else "far"
-                else:
-                    rows=pl.ds(pl.multiple_of(t*TILE,TILE),TILE) if not own_static else pl.ds(t*TILE,TILE); kind="own"
-                s=scores(rows,h,kind,qh)
-                s_scr[h,j]=s
-                part=jnp.max(s.reshape(TILE//8,8,TILE),axis=0)
-                m=part if m is None else jnp.maximum(m,part)
-            m=jnp.max(m,axis=0,keepdims=True)
-            l=None; acc=None
-            for j in range(n_far+1):
+                if h+1<heads:
+                    part=make(h+1,j)
+                    peak=part if peak is None else jnp.maximum(peak,part)
                 p=jnp.exp(s_scr[h,j]-m)
                 part=jnp.sum(p.reshape(TILE//8,8,TILE),axis=0)
                 l=part if l is None else l+part
-                vrow=j if j<n_far else t
-                a=nn(vt[vrow,h*size:(h+1)*size,:],p.astype(BF))
+                a=nn(vt[j if j<n_far else t,h*size:(h+1)*size,:],p.astype(BF))
                 acc=a if acc is None else acc+a
             l=jnp.sum(l,axis=0,keepdims=True)
             o=acc*(1.0/l)
-            cols=pl.ds(t*TILE if own_static else pl.multiple_of(t*TILE,TILE),TILE)
-            ot_ref[h*size:(h+1)*size,cols]=o
-            lse_ref[h:h+1,cols]=m+jnp.log(l)
+            ot_ref[h*size:(h+1)*size,own_rows_at]=o
+            lse_ref[h:h+1,own_rows_at]=m+jnp.log(l)
             outs.append(o)
         o=jnp.concatenate(outs,axis=0) if heads>1 else outs[0]
         o=jnp.transpose(o,(1,0)).astype(BF)
@@ -352,23 +353,29 @@
     return pl.CostEstimate(flops=flops, bytes_accessed=size, transcendentals=0)
 
 
+def encoder_rows(gathered, rows):
+    parts, total, width = gathered.shape
+    return pl.BlockSpec((parts, total - rows, width), lambda *_: (0, rows // (total - rows), 0))
+
+
 def source_kernel(source_ref, w_ref, out_ref, weight):
     whole_weight(w_ref, weight)
-    source = source_ref[...]
+    source = source_ref[...].reshape(-1, source_ref.shape[-1])
     for t in range(out_ref.shape[-1] // TILE):
         cols = slice(t * TILE, (t + 1) * TILE)
         out_ref[0, :, cols] = nn(source, weight[:, cols]).astype(BF)
 
 
-def source_projection(source, packed):
-    rows, width = source.shape
+def source_projection(gathered, local, packed):
+    width = gathered.shape[2]
+    rows = gathered.shape[0] * (gathered.shape[1] - local)
     parts, shards, _, own, _ = packed.shape
     return pl.pallas_call(
         source_kernel,
         grid=(2,),
         out_shape=jax.ShapeDtypeStruct((2, rows, width), BF),
         in_specs=[
-            whole((rows, width)),
+            encoder_rows(gathered, local),
             pl.BlockSpec((parts, shards, 1, own, width), lambda i: (0, 0, 3 + i, 0, 0)),
         ],
         out_specs=pl.BlockSpec((1, rows, width), lambda i: (i, 0, 0)),
@@ -376,7 +383,7 @@
         compiler_params=params(),
         cost_estimate=cost(4 * rows * width * width, 8 * width * width),
         name="source_projection",
-    )(source, packed)
+    )(gathered, packed)
 
 
 def middle_kernel(
@@ -685,7 +692,7 @@
     parts, shards, _, own, _ = wk_ref.shape
     layout = (parts, shards, 5, own)
     tail = shards * 5 * own
-    piece = source_ref.shape[0] // parts
+    piece = g_ref.shape[1] - tail
     whole_weight(wk_ref, wk)
     whole_weight(wv_ref, wv)
     for t in range(width // TILE):
@@ -709,14 +716,14 @@
     product(1, left, lambda cols: dcq_ref[:, cols])
     left[...] = jnp.transpose(cob_ref[...], (1, 0))
     product(2, left, lambda cols: dx2_ref[:, cols].astype(BF))
-    left_source[...] = jnp.transpose(source_ref[...], (1, 0))
+    left_source[...] = jnp.transpose(source_ref[...].reshape(-1, width), (1, 0))
     product(3, left_source, lambda cols: dckv_ref[0, :, cols])
     product(4, left_source, lambda cols: dckv_ref[1, :, cols])
 
 
-def middle_grads(dx2, x1, gain, cob, dcq, dckv, source, ob, dx1, packed):
+def middle_grads(dx2, x1, gain, cob, dcq, dckv, gathered, ob, dx1, packed):
     rows, width = dx2.shape
-    count = source.shape[0]
+    count = dckv.shape[1]
     parts, shards, _, own, _ = packed.shape
     tokens = whole((rows, width))
     shape = (parts, shards * 5 * own + count // parts, width)
@@ -725,7 +732,7 @@
         grid=(1,),
         out_shape=jax.ShapeDtypeStruct(shape, BF),
         in_specs=[
-            tokens, tokens, whole((1, width)), tokens, tokens, whole(dckv.shape), whole((count, width)), tokens, tokens,
+            tokens, tokens, whole((1, width)), tokens, tokens, whole(dckv.shape), encoder_rows(gathered, rows), tokens, tokens,
             packed_spec(packed, 3), packed_spec(packed, 4),
         ],
         out_specs=whole(shape),
@@ -736,7 +743,7 @@
         compiler_params=params(),
         cost_estimate=cost(46 * rows * width * width, 24 * rows * width),
         name="middle_grads",
-    )(dx2, x1, gain, cob, dcq, dckv, source, ob, dx1, packed, packed)
+    )(dx2, x1, gain, cob, dcq, dckv, gathered, ob, dx1, packed, packed)
 
 
 def final_kernel(d_ref, w_ref, states_ref, gain_ref, dx1_ref, out_ref):
@@ -796,7 +803,7 @@
     step = pl.program_id(0)
     x = states_ref[0].astype(F32)
     n = (x * inverse_rms(x) * gain_ref[...]).astype(BF)
-    g = lax.dot_general(n, d_ref[...], (((0,), (0,)), ((), ())), preferred_element_type=F32)
+    g = lax.dot_general(d_ref[...], n, (((0,), (0,)), ((), ())), preferred_element_type=F32)
 
     @pl.when(step == 0)
     def _():
@@ -808,7 +815,7 @@
 
     @pl.when(step == pl.num_programs(0) - 1)
     def _():
-        total = acc_ref[...]
+        total = jnp.transpose(acc_ref[...], (1, 0))
         if len(gw_ref.shape) == 2:
             gw_ref[...] = total.astype(BF)
         else:
@@ -835,7 +842,7 @@
             pl.BlockSpec((rows, cols), lambda i: (i, 0)),
         ],
         out_specs=[whole(shape), whole((width, 1))],
-        scratch_shapes=[pltpu.VMEM((width, cols), F32)],
+        scratch_shapes=[pltpu.VMEM((cols, width), F32)],
         compiler_params=params(),
         cost_estimate=cost(4 * parts * rows * width * cols, 2 * parts * rows * (width + cols)),
         name="last_projection",
@@ -945,7 +952,8 @@
 def gather_down(shard, earlier):
     rows, width = shard.shape
     start = lax.axis_index("core") * (width // 2)
-    mine = spread(after(lax.dynamic_slice_in_dim(shard, start, width // 2, 1), earlier)).reshape(-1, width // 2)
+    mine = after(copies(lax.dynamic_slice_in_dim(shard, start, width // 2, 1)), earlier)
+    mine = lax.all_to_all(mine, "fsdp", 0, 0, tiled=True).reshape(-1, width // 2)
     return mine, swap(mine, "core")
 
 
@@ -996,7 +1004,6 @@
         return grads.reshape(matrices, shards, parts, own, columns).transpose(2, 1, 0, 3, 4)
 
     gathered = lax.all_gather(jnp.concatenate([states[0], encoded[0]], axis=0), CTX, axis=0, tiled=False)
-    encoded_all = gathered[:, local:].reshape(-1, width)
     columns = lax.dynamic_slice_in_dim(
         jnp.stack([self_query, self_key, self_value], axis=1), place * inner, inner, 2
     ).reshape(shard_width, 3 * inner)
@@ -1012,19 +1019,17 @@
     canon_all = lax.all_gather(canon, CTX, axis=0, tiled=True)
     slots = jnp.argmax(canon_all[None, :] == jnp.arange(blocks * parts)[:, None], axis=1).astype(jnp.int32)
     line = jnp.concatenate([columns, small], axis=0)
-    squares = [own_rows(w) for w in (self_output, cross_query, cross_output, cross_key, cross_value)]
+    squares = jnp.stack([own_rows(w) for w in (self_output, cross_query, cross_output, cross_key, cross_value)], axis=0)
+    squares = after(spread(squares), slots)
     wide = copies(jnp.stack([own_rows(gate_weight), own_rows(up_weight)], axis=0))
-    squares = spread(jnp.concatenate(squares + [line.reshape(-1, width)], axis=0))
-    squares = after(squares, slots, wide)
-    line = squares[:, 5 * own :].reshape((shards,) + line.shape)
-    squares = squares[:, : 5 * own].reshape(shards, 5, own, width)
+    line = after(spread(after(line, squares)), wide)
     qkv_weight = line[:, :shard_width].reshape(width, 3 * inner)
     small = line[:, shard_width:].reshape(shards, -1)[:, :small_width].astype(F32)
     gains = [small[:, i * shard_width : (i + 1) * shard_width].reshape(1, width) for i in range(3)]
     table = small[:, 3 * shard_width :].reshape(BUCKETS, head_count)
     own_table = lax.dynamic_slice_in_dim(table, place * heads, heads, 1).reshape(-1)
 
-    wide = lax.all_to_all(after(wide, squares), "fsdp", 0, 0, tiled=True)
+    wide = lax.all_to_all(after(wide, line), "fsdp", 0, 0, tiled=True)
     squares = lax.all_gather(squares, CTX, axis=0, tiled=False)
 
     prompt_tiles = PROMPT // TILE
@@ -1035,7 +1040,7 @@
     wide = lax.all_gather(after(wide, o), CTX, axis=0, tiled=False)
     squares, wide = arranged(squares), arranged(wide)
     down, other_down = gather_down(down_weight, o)
-    ckv = source_projection(encoded_all, squares)
+    ckv = source_projection(gathered, local, squares)
     ob, x1, cq, cob, cot, cross_lse, x2, n3 = middle_forward(
         o, states[0], gains[1], gains[2], squares, ckv, head_count
     )
@@ -1049,7 +1054,7 @@
         (qkv_all,), dx2, x1, gains[1], squares, cq, ckv, cot, cross_lse, head_count, parts
     )
     dso = lax.all_to_all(dso, CTX, 0, 0, tiled=True).reshape(parts * blocks, BLK, inner)
-    g_squares = middle_grads(dx2, x1, gains[1], cob, after(dcq, g_down), dckv, encoded_all, ob, dx1, squares)
+    g_squares = middle_grads(dx2, x1, gains[1], cob, after(dcq, g_down), dckv, gathered, ob, dx1, squares)
     if not aligned:
         encoded_part = g_squares[0, 5 * width :].reshape(parts, -1, width)
         g_squares = scattered(g_squares[0, : 5 * width].reshape(1, 1, 5, width, width)).reshape(parts, -1, width)

time: 604 us -> 606 us (level)
    all_to_all x1 -> x2, waiting for transfers between devices: 0.01 us -> 29.7 us  [the longest x1 29.7 us: gather_down(): lax.all_to_all(mine, 'fsdp', 0, 0, tiled=True).reshape(-1, width // 2)]
    all_to_all x2, waiting for transfers between devices: 66 us -> 39 us  [spread(): return lax.all_to_all(copies(piece), 'fsdp', 0, 0, tiled=True)]
    unnamed x80 -> x79, local copies, waits for them, and re-layouts: 16.5 us -> 20.2 us
  transfers between devices with their start and end apart: 26 -> 27, of which waited for: 10 -> 12; matrix products, arithmetic and copies ran while one was open for 10% -> 9% of each run, Pallas kernels for 45% -> 44%
where the time goes in v5:
time: 606 us; the launch traced here: 595 us
  Pallas kernels  272 us (45%)
  waiting for transfers between devices  154 us (25%)
  starting transfers between devices  57.9 us (10%)
  local copies, waits for them, and re-layouts  41.2 us (7%)
  blocking collectives  28.1 us (5%)
  other arithmetic  25.9 us (4%)
  between operations  15.9 us (3%)
    pallas_call x2, Pallas kernels, sa_bwd(): pl.pallas_call(leaving_out(functools.partial(bwd_kernel, heads, prompt_ti...  73 us
    all_to_all x2, waiting for transfers between devices, spread(): return lax.all_to_all(copies(piece), 'fsdp', 0, 0, tiled=True)  39 us
    pallas_call x1, Pallas kernels, feed_forward(): pl.pallas_call(feed_kernel, grid=(steps,), out_shape=[jax.ShapeDtypeStruc...  36.3 us
    all_gather x1, waiting for transfers between devices, on_device(): lax.all_gather(after(rest, g_wide, dqkv_local), CTX, axis=0, tiled=False)  30.6 us
    all_to_all x1, waiting for transfers between devices, gather_down(): lax.all_to_all(mine, 'fsdp', 0, 0, tiled=True).reshape(-1, width // 2)  29.7 us
    pallas_call x1, Pallas kernels, middle_forward(): pl.pallas_call(functools.partial(middle_kernel, head_count), grid=(1,), o...  29.4 us
    pallas_call x1, Pallas kernels, middle_back(): pl.pallas_call(leaving_out(functools.partial(middle_back_kernel, head_cou...  26.5 us
    pallas_call x1, Pallas kernels, sa_fwd(): pl.pallas_call(functools.partial(fwd_kernel, heads, prompt_tiles), out_sh...  26.2 us
  transfers between devices with their start and end apart: 27, of which 12 were waited for; matrix products, arithmetic and copies ran while one was open for 9% of the time, Pallas kernels for 44%

profile of v5, /device:TPU:0, one launch (start us, length us, event | category | flops | bytes accessed | tf_op | source)
XLA Modules:
  0.0 595.4 jit_solution(17976353910738907585)
XLA Ops:
  7.3 2.5 pad_maximum_fusion.1
  15.2 6.3 %all-to-all-start = ((bf16[4,5,32,1024]{3,2,1,0:T(8,128)(2,1)}), bf16[4,5,32,1024]{3,2,1,0:T(8,128)(2,1)S(1)}, u32[]{:S(2)}, u32[]{:S(2)}) async-start(bf16[4,5,32,1024]{3,2,1,0:T(8,128)(2,1)} %broadcast_in_dim.19), calls=%async_computation | async-start | bytes 2621440 | tf_op jit(solution)/shard_map/all_to_all | solution.py:901
  24.6 8.1 %all-reduce.2 = s32[32]{0:T(128)S(1)} all-reduce(s32[32]{0:T(128)S(1)} %fusion.27), channel_id=1, replica_groups=mesh['plane'=4,'core'=2,'fsdp'=4] {'plane','core'}, use_global_device_ids=true, to_apply=%add.2 | all-reduce | flops 32 | bytes 256
  33.4 19.5 %all-to-all-done.refs_0_ = bf16[4,5,32,1024]{3,2,1,0:T(8,128)(2,1)S(1)} async-done(((bf16[4,5,32,1024]{3,2,1,0:T(8,128)(2,1)}), bf16[4,5,32,1024]{3,2,1,0:T(8,128)(2,1)S(1)}, u32[]{:S(2)}, u32[]{:S(2)}) %all-to-all-start) | async-done | bytes 1310752 | tf_op jit(solution)/shard_map/all_to_all | solution.py:901
  57.8 1.9 broadcast_in_dim.20
  59.7 3.5 all-to-all-start.1
  64.3 19.6 %all-to-all-done.1.refs_0_ = bf16[4,272,384]{2,1,0:T(8,128)(2,1)S(1)} async-done(((bf16[4,272,384]{2,1,0:T(8,128)(2,1)}), bf16[4,272,384]{2,1,0:T(8,128)(2,1)S(1)}, u32[]{:S(2)}, u32[]{:S(2)}) %all-to-all-start.1) | async-done | bytes 835616 | tf_op jit(solution)/shard_map/all_to_all | solution.py:901
  85.2 2.1 slice.98
  89.5 3.6 all-to-all-start.3
  93.2 11.0 %first_projection.1 = bf16[4096,384]{1,0:T(8,128)(2,1)} custom-call(bf16[8,576,1024]{2,1,0:T(8,128)(2,1)} %bitcast.140, f32[1,1024]{1,0:T(1,128)} %bitcast.172, bf16[1024,384]{1,0:T(8,128)(2,1)} %bitcast.155), custom_call_target="tpu_custom_call" | custom-call | flops 6442450944 | bytes 11534336 | tf_op jit(solution)/shard_map/first_projection/pallas_call | solution.py:788
  104.2 26.2 %self_attention_forward.1 = (bf16[32,128,128]{2,1,0:T(8,128)(2,1)}, f32[128,4096]{1,0:T(8,128)}, f32[2,4096]{1,0:T(2,128)}) custom-call(s32[32]{0:T(128)} %get-tuple-element.58.refs_1_.slots, f32[64]{0:T(128)} %reshape.144.tab.refs_2_, bf16[32,128,384]{2,1,0:T(8,128)(2,1)} %bitcast.183), custom_call_target="tpu_custom_call" | custom-call | flops 32000000000 | bytes 12582912 | tf_op jit(solution)/shard_map/self_attention_forward/pallas_call | solution.py:138
  130.4 19.9 %all_to_all.45.o_ref.refs_1_ = bf16[8,512,128]{2,1,0:T(8,128)(2,1)} all-to-all(bf16[8,512,128]{2,1,0:T(8,128)(2,1)} %bitcast.166), channel_id=1, replica_groups=mesh['plane'=4,'core'=2,'fsdp'=4] {'plane','core'}, dimensions={0} | all-to-all | bytes 2097152 | tf_op jit(solution)/shard_map/all_to_all | solution.py:1038
  153.6 1.8 broadcast_in_dim.44.refs_0_
  155.4 5.0 all-to-all-start.4
  160.4 5.4 source_projection.1.ckv_ref.refs_8_
  165.8 29.4 %middle_forward.1 = (bf16[512,1024]{1,0:T(8,128)(2,1)}, f32[512,1024]{1,0:T(8,128)}, bf16[512,1024]{1,0:T(8,128)(2,1)}, bf16[512,1024]{1,0:T(8,128)(2,1)}, f32[8...) custom-call(bf16[8,512,128]{2,1,0:T(8,128)(2,1)} %all_to_all.45.o_ref.refs_1_, ...), custom_call_target="tpu_custom_call" | custom-call | flops 32212254720 | bytes 12582912 | tf_op jit(solution)/shard_map/middle_forward/pallas_call | solution.py:463
  195.3 29.7 %all-to-all-done.4 = bf16[4,704,512]{2,1,0:T(8,128)(2,1)} async-done(((bf16[4,704,512]{2,1,0:T(8,128)(2,1)}), bf16[4,704,512]{2,1,0:T(8,128)(2,1)}, u32[]{:S(2)}, u32[]{:S(2)}) %all-to-all-start.4) | async-done | bytes 2883616 | tf_op jit(solution)/shard_map/all_to_all | solution.py:956
  225.0 5.6 collective-permute-done.other_ref.refs_5_
  230.6 36.3 %feed_forward.1 = (bf16[512,2816]{1,0:T(8,128)(2,1)}, f32[512,1024]{1,0:T(8,128)}, f32[1,1024]{1,0:T(1,128)}, bf16[8,4,2,32,2816]{4,3,2,1,0:T(8,128)(2,1)}, bf16...) custom-call(s32[1]{0:T(128)} %bitcast.core_ref.refs_1_, bf16[512,1024]{1,0:T(8,128)(2,1)} %get-tuple-element.60.n3_ref, ...), custom_call_target="tpu_custom_call" | custom-call | flops 41339060224 | bytes 34603008 | tf_op jit(solution)/shard_map/feed_forward/pallas_call | solution.py:542
  267.2 26.5 %middle_back.1 = (f32[512,1024]{1,0:T(8,128)}, f32[1,1024]{1,0:T(1,128)}, bf16[512,1024]{1,0:T(8,128)(2,1)}, bf16[2,512,1024]{2,1,0:T(8,128)(2,1)}, bf16[8,512,128]{2,1,0:T(8,128)(2,1)}) custom-call(bf16[8,1024,384]{2,1,0:T(8,128)(2,1)} %bitcast.146, f32[512,1024]{1,0:T(8,128)} %get-tuple-element.63.refs_1_.dx2_ref, ...), custom_call_target="tpu_custom_call" | custom-call | flops 32212254720 | bytes 12582912 | tf_op jit(solution)/shard_map/middle_back/pallas_call | solution.py:667
  293.7 3.6 all-to-all-start.5
  297.9 6.0 %add_convert_fusion = bf16[2816,512]{1,0:T(8,128)(2,1)} fusion(bf16[2816,512]{1,0:T(8,128)(2,1)} %collective-permute-done.1, bf16[2816,512]{1,0:T(8,128)(2,1)} %get-tuple-element.73), kind=kLoop, calls=%fused_computation.1 | loop fusion | flops 5767168 | bytes 8650752 | tf_op jit(solution)/shard_map/convert_element_type | solution.py:1052
  303.9 19.9 %all-to-all-done.5 = bf16[8,512,128]{2,1,0:T(8,128)(2,1)S(1)} async-done(((bf16[8,512,128]{2,1,0:T(8,128)(2,1)}), bf16[8,512,128]{2,1,0:T(8,128)(2,1)S(1)}, u32[]{:S(2)}, u32[]{:S(2)}) %all-to-all-start.5) | async-done | bytes 1048608 | tf_op jit(solution)/shard_map/all_to_all | solution.py:1056
  324.8 4.7 all-to-all-start.6
  329.6 23.1 %middle_grads.1.refs_0_ = bf16[8,704,1024]{2,1,0:T(8,128)(2,1)} custom-call(f32[512,1024]{1,0:T(8,128)} %get-tuple-element.63.refs_1_.dx2_ref, f32[512,1024]{1,0:T(8,128)} %get-tuple-element.64.refs_2_.x1_ref, f32[1,1024]{1,0:T(1,128)} %bitcast.177, bf16[512,1024]{1,0:T(8,128)(2,1)} %get-tuple-element.71.cob_ref, bf16[512,1024]{1,0:T(8,128)(2,1)} %after.26.dcq_ref, ...), custom_call_target="tpu_custom_call" | custom-call | flops 24696061952 | bytes 12582912 | tf_op jit(solution)/shard_map/middle_grads/pallas_call | solution.py:730
  352.8 36.6 %self_attention_backward.2 = (bf16[2560,128]{1,0:T(8,128)(2,1)}, f32[4096,256]{1,0:T(8,128)}, f32[2,2,128,128]{3,2,1,0:T(8,128)}, f32[2,8,256]{2,1,0:T(8,128)}) custom-call(bf16[8,704,1024]{2,1,0:T(8,128)(2,1)} %after.27.refs_0_, s32[32]{0:T(128)} %get-tuple-element.58.refs_1_.slots, f32[64]{0:T(128)} %reshape.144.tab.refs_2_, ...), custom_call_target="tpu_custom_call" | custom-call | flops 43000000512 | bytes 18874368 | tf_op jit(solution)/shard_map/self_attention_backward/pallas_call | solution.py:286
  389.3 3.3 all-to-all-done.6.refs_0_
  392.6 3.3 reduce_sum.33.refs_1_
  396.0 2.6 copy.97.refs_0_
  398.5 4.3 all-to-all-start.7
  403.1 36.5 %self_attention_backward.3 = (bf16[32,128,384]{2,1,0:T(8,128)(2,1)}, f32[2,32,128]{2,1,0:T(8,128)}) custom-call(bf16[4,2,32,2816]{3,2,1,0:T(8,128)(2,1)} %bitcast.165, s32[32]{0:T(128)} %get-tuple-element.58.refs_1_.slots, f32[64]{0:T(128)} %reshape.144.tab.refs_2_, bf16[32,128,384]{2,1,0:T(8,128)(2,1)} %bitcast.185, bf16[32,128,128]{2,1,0:T(8,128)(2,1)} %bitcast.139, ...), custom_call_target="tpu_custom_call" | custom-call | flops 249999998976 | bytes 18874368 | tf_op jit(solution)/shard_map/self_attention_backward/pallas_call | solution.py:286
  439.6 2.7 reduce_sum.34.refs_1_
  442.5 2.8 collective-permute-start.4
  446.1 12.6 %last_projection.1 = (bf16[4,96,1024]{2,1,0:T(8,128)(2,1)}, f32[1024,1]{1,0:T(8,128)}) custom-call(bf16[8,576,1024]{2,1,0:T(8,128)(2,1)} %bitcast.143, f32[1,1024]{1,0:T(1,128)} %bitcast.173, bf16[1024,384]{1,0:T(8,128)(2,1)} %bitcast.156, bf16[4096,384]{1,0:T(8,128)(2,1)} %bitcast.121), custom_call_target="tpu_custom_call" | custom-call | flops 6442450944 | bytes 11534336 | tf_op jit(solution)/shard_map/last_projection/pallas_call | solution.py:836
  458.7 1.6 copy.102.refs_0_
  464.0 1.7 fusion.8.refs_2_
  465.7 4.5 all-to-all-start.8
  475.6 6.4 %collective-permute-start.9 = (bf16[272,1024]{1,0:T(8,128)(2,1)}, bf16[272,1024]{1,0:T(8,128)(2,1)S(1)}, u32[]{:S(2)}, u32[]{:S(2)}) collective-permute-start(bf16[272,1024]{1,0:T(8,128)(2,1)} %get-tuple-element.102), channel_id=1, source_target_pairs={{0,3},{4,7},{8,11},{12,15},{16,19},{20,23},{24,27},{28,31}} | collective-permute-start | bytes 1671176 | tf_op jit(solution)/shard_map/ppermute | solution.py:920
  483.3 5.5 collective-permute-start.7
  490.1 3.4 collective-permute-done.10
  493.5 2.3 collective-permute-start.5
  495.9 21.0 %collective-permute-done.8 = bf16[272,1024]{1,0:T(8,128)(2,1)S(1)} collective-permute-done((bf16[272,1024]{1,0:T(8,128)(2,1)}, bf16[272,1024]{1,0:T(8,128)(2,1)S(1)}, u32[]{:S(2)}, u32[]{:S(2)}) %collective-permute-start.8) | collective-permute-done | bytes 557088 | tf_op jit(solution)/shard_map/ppermute | solution.py:920
  518.3 2.2 fusion.5
  521.4 8.0 %layer_output.1 = bf16[512,1024]{1,0:T(8,128)(2,1)} custom-call(bf16[32,128,384]{2,1,0:T(8,128)(2,1)} %get-tuple-element.82.refs_0_.refs_1_, s32[1]{0:T(128)} %bitcast.core_ref.refs_1_, bf16[512,2816]{1,0:T(8,128)(2,1)} %get-tuple-element.83.refs_2_, f32[512,1024]{1,0:T(8,128)} %get-tuple-element.61.x2_ref.refs_1_.refs_3_, ...), custom_call_target="tpu_custom_call" | custom-call | flops 5905580032 | bytes 11534336 | tf_op jit(solution)/shard_map/layer_output/pallas_call | solution.py:579
  531.1 13.1 %final_back.1 = f32[512,1024]{1,0:T(8,128)} custom-call(bf16[8,512,384]{2,1,0:T(8,128)(2,1)} %all-to-all-done.8.d_ref.refs_2_, bf16[8,1024,384]{2,1,0:T(8,128)(2,1)} %bitcast.147, bf16[512,1024]{1,0:T(8,128)(2,1)} %bitcast.154, f32[1,1024]{1,0:T(1,128)} %bitcast.174, f32[512,1024]{1,0:T(8,128)} %get-tuple-element.77.dx1_ref), custom_call_target="tpu_custom_call" | custom-call | flops 3221225472 | bytes 6291456 | tf_op jit(solution)/shard_map/final_back/pallas_call | solution.py:761
  544.8 3.1 fusion.29
  547.9 30.6 %all-gather.23.cloned.1.call-done = bf16[2880,1024]{1,0:T(8,128)(2,1)} async-done(((bf16[360,1024]{1,0:T(8,128)(2,1)}), bf16[2880,1024]{1,0:T(8,128)(2,1)}) %all-gather.23.cloned.1.call-update) | async-done | bytes 5898256 | tf_op jit(solution)/shard_map/all_gather | solution.py:1097
  579.6 7.3 %unpack.1 = (f32[256,1024]{1,0:T(8,128)}, f32[256,1024]{1,0:T(8,128)}, f32[256,1024]{1,0:T(8,128)}, f32[256,1024]{1,0:T(8,128)}, f32[256,1024]{1,0:T(8,128)}, /*...) custom-call(bf16[8,360,1024]{2,1,0:T(8,128)(2,1)} %bitcast.149), custom_call_target="tpu_custom_call" | custom-call | bytes 17694720 | tf_op jit(solution)/shard_map/unpack/pallas_call | solution.py:881
  (183 shorter events, 43.0 us)
Async XLA Ops:
  7.2 143.2 %copy-start = (bf16[704,1024]{1,0:T(8,128)(2,1)S(1)}, bf16[704,1024]{1,0:T(8,128)(2,1)}, u32[]{:S(2)}) copy-start(bf16[704,1024]{1,0:T(8,128)(2,1)} %param.39) | copy-start | bytes 4325380
  7.2 85.9 %all-gather.13.cloned.1.call-start = ((), (), s32[]{:S(2)}) async-start(), calls=%async_computation.13 | async-start | bytes 10616832 | tf_op jit(solution)/shard_map/all_gather | solution.py:1006
  13.2 10.1 %copy-start.29 = (u32[32]{0:T(128)S(1)}, u32[32]{0:T(128)}, u32[]{:S(2)}) copy-start(u32[32]{0:T(128)} %constant.123) | copy-start | bytes 388
  15.2 37.7 %all-to-all-start = ((bf16[4,5,32,1024]{3,2,1,0:T(8,128)(2,1)}), bf16[4,5,32,1024]{3,2,1,0:T(8,128)(2,1)S(1)}, u32[]{:S(2)}, u32[]{:S(2)}) async-start(bf16[4,5,32,1024]{3,2,1,0:T(8,128)(2,1)} %broadcast_in_dim.19), calls=%async_computation | async-start | bytes 2621440 | tf_op jit(solution)/shard_map/all_to_all | solution.py:901
  21.6 32.4 %copy-start.25 = (bf16[8,16]{1,0:T(8,128)(2,1)S(1)}, bf16[8,16]{1,0:T(8,128)(2,1)}, u32[]{:S(2)}) copy-start(bf16[8,16]{1,0:T(8,128)(2,1)} %param.30) | copy-start | bytes 772
  21.6 32.5 %copy-start.26 = (bf16[256]{0:T(256)(128)(2,1)S(1)}, bf16[256]{0:T(256)(128)(2,1)}, u32[]{:S(2)}) copy-start(bf16[256]{0:T(256)(128)(2,1)} %param.36) | copy-start | bytes 1540
  21.6 32.5 %copy-start.27 = (bf16[256]{0:T(256)(128)(2,1)S(1)}, bf16[256]{0:T(256)(128)(2,1)}, u32[]{:S(2)}) copy-start(bf16[256]{0:T(256)(128)(2,1)} %param.31) | copy-start | bytes 1540
  21.6 32.5 %copy-start.28 = (bf16[256]{0:T(256)(128)(2,1)S(1)}, bf16[256]{0:T(256)(128)(2,1)}, u32[]{:S(2)}) copy-start(bf16[256]{0:T(256)(128)(2,1)} %param.25) | copy-start | bytes 1540
  21.6 32.6 %copy-start.19 = (bf16[256,1024]{1,0:T(8,128)(2,1)S(1)}, bf16[256,1024]{1,0:T(8,128)(2,1)}, u32[]{:S(2)}) copy-start(bf16[256,1024]{1,0:T(8,128)(2,1)} %param.28) | copy-start | bytes 1572868
  21.6 138.8 %all-gather.15.cloned.1.call-start = ((), (), s32[]{:S(2)}) async-start(), calls=%async_computation.14 | async-start | bytes 11796480 | tf_op jit(solution)/shard_map/all_gather | solution.py:1033
  59.7 24.2 %all-to-all-start.1 = ((bf16[4,272,384]{2,1,0:T(8,128)(2,1)}), bf16[4,272,384]{2,1,0:T(8,128)(2,1)S(1)}, u32[]{:S(2)}, u32[]{:S(2)}) async-start(bf16[4,272,384]{2,1,0:T(8,128)(2,1)} %broadcast_in_dim.20), calls=%async_computation.1 | async-start | bytes 1671168 | tf_op jit(solution)/shard_map/all_to_all | solution.py:901
  89.5 40.9 %all-to-all-start.3 = ((bf16[4,2,32,2816]{3,2,1,0:T(8,128)(2,1)}), bf16[4,2,32,2816]{3,2,1,0:T(8,128)(2,1)S(1)}, u32[]{:S(2)}, u32[]{:S(2)}) async-start(bf16[4,2,32,2816]{3,2,1,0:T(8,128)(2,1)} %after.22), calls=%async_computation.3 | async-start | bytes 2883584 | tf_op jit(solution)/shard_map/all_to_all | solution.py:1032
  93.1 137.5 %all-gather.17.cloned.1.call-start = ((), (), s32[]{:S(2)}) async-start(), calls=%async_computation.15 | async-start | bytes 12976128 | tf_op jit(solution)/shard_map/all_gather | solution.py:1040
  130.4 20.0 %copy-start.6 = (bf16[4,2,32,2816]{3,2,1,0:T(8,128)(2,1)}, bf16[4,2,32,2816]{3,2,1,0:T(8,128)(2,1)S(1)}, u32[]{:S(2)}) copy-start(bf16[4,2,32,2816]{3,2,1,0:T(8,128)(2,1)S(1)} %all-to-all-done.3.refs_0_) | copy-start | bytes 4325380
  155.4 69.6 %all-to-all-start.4 = ((bf16[4,704,512]{2,1,0:T(8,128)(2,1)}), bf16[4,704,512]{2,1,0:T(8,128)(2,1)}, u32[]{:S(2)}, u32[]{:S(2)}) async-start(bf16[4,704,512]{2,1,0:T(8,128)(2,1)} %after.24), calls=%async_computation.4 | async-start | bytes 5767168 | tf_op jit(solution)/shard_map/all_to_all | solution.py:956
  160.4 106.8 %all-gather.19.cloned.1.call-start = ((), (), s32[]{:S(2)}) async-start(), calls=%async_computation.16 | async-start | bytes 7077888 | tf_op jit(solution)/shard_map/all_gather | solution.py:1047
  195.2 200.8 %reduce-scatter.3.cloned.1.call-start = ((), (), s32[]{:S(2)}) async-start(), calls=%async_computation.11 | async-start | bytes 12976128 | tf_op jit(solution)/shard_map/reduce_scatter | solution.py:1051
  225.0 5.6 collective-permute-start
  267.0 30.9 %collective-permute-start.1 = (bf16[2816,512]{1,0:T(8,128)(2,1)}, bf16[2816,512]{1,0:T(8,128)(2,1)}, u32[]{:S(2)}, u32[]{:S(2)}) collective-permute-start(bf16[2816,512]{1,0:T(8,128)(2,1)} %get-tuple-element.74), channel_id=1, source_target_pairs={{0,4},{4,0},{1,5},{5,1},{2,6},{6,2},{3,7},{7,3},{8,12},{12,8},{9,1... | collective-permute-start | bytes 8650760 | tf_op jit(solution)/shard_map/ppermute | solution.py:945
  267.2 30.1 %copy-start.24 = (f32[1,1024]{1,0:T(1,128)S(1)}, f32[1,1024]{1,0:T(1,128)}, u32[]{:S(2)}) copy-start(f32[1,1024]{1,0:T(1,128)} %get-tuple-element.87) | copy-start | bytes 12292
  293.7 30.1 %all-to-all-start.5 = ((bf16[8,512,128]{2,1,0:T(8,128)(2,1)}), bf16[8,512,128]{2,1,0:T(8,128)(2,1)S(1)}, u32[]{:S(2)}, u32[]{:S(2)}) async-start(bf16[8,512,128]{2,1,0:T(8,128)(2,1)} %get-tuple-element.68), calls=%async_computation.6 | async-start | bytes 2097152 | tf_op jit(solution)/shard_map/all_to_all | solution.py:1056
  324.8 67.9 %all-to-all-start.6 = ((bf16[4,704,512]{2,1,0:T(8,128)(2,1)}), bf16[4,704,512]{2,1,0:T(8,128)(2,1)}, u32[]{:S(2)}, u32[]{:S(2)}) async-start(bf16[4,704,512]{2,1,0:T(8,128)(2,1)} %after.28), calls=%async_computation.7 | async-start | bytes 5767168 | tf_op jit(solution)/shard_map/all_to_all | solution.py:905
  329.4 140.8 %reduce-scatter.5.cloned.1.call-start = ((), (), s32[]{:S(2)}) async-start(), calls=%async_computation.12 | async-start | bytes 12976128 | tf_op jit(solution)/shard_map/reduce_scatter | solution.py:1065
  398.5 41.1 %all-to-all-start.7 = ((bf16[4,2,32,2816]{3,2,1,0:T(8,128)(2,1)}), bf16[4,2,32,2816]{3,2,1,0:T(8,128)(2,1)}, u32[]{:S(2)}, u32[]{:S(2)}) async-start(bf16[4,2,32,2816]{3,2,1,0:T(8,128)(2,1)} %after.30), calls=%async_computation.8 | async-start | bytes 2883584 | tf_op jit(solution)/shard_map/all_to_all | solution.py:905
  402.9 118.5 %all-gather.21.cloned.1.call-start = ((), (), s32[]{:S(2)}) async-start(), calls=%async_computation.17 | async-start | bytes 3244032 | tf_op jit(solution)/shard_map/all_gather | solution.py:1095
  439.6 2.8 copy-start.23
  439.6 2.8 copy-start.22
  439.6 2.8 copy-start.9
  442.5 18.5 %collective-permute-start.4 = (bf16[176,512]{1,0:T(8,128)(2,1)S(1)}, bf16[176,512]{1,0:T(8,128)(2,1)S(1)}, u32[]{:S(2)}, u32[]{:S(2)}) collective-permute-start(bf16[176,512]{1,0:T(8,128)(2,1)S(1)} %get-tuple-element.107), channel_id=1, source_target_pairs={{0,24},{8,16},{16,8},{24,0},{1,25},{9,17},{17,9},{25,1},{2,26},{10... | collective-permute-start | bytes 540680 | tf_op jit(solution)/shard_map/ppermute | solution.py:969
  445.3 16.4 %collective-permute-start.3 = (bf16[176,512]{1,0:T(8,128)(2,1)S(1)}, bf16[176,512]{1,0:T(8,128)(2,1)S(1)}, u32[]{:S(2)}, u32[]{:S(2)}) collective-permute-start(bf16[176,512]{1,0:T(8,128)(2,1)S(1)} %get-tuple-element.108), channel_id=1, source_target_pairs={{0,16},{8,24},{16,0},{24,8},{1,17},{9,25},{17,1},{25,9},{2,18},{10... | collective-permute-start | bytes 540680 | tf_op jit(solution)/shard_map/ppermute | solution.py:969
  445.6 17.0 %collective-permute-start.2 = (bf16[176,512]{1,0:T(8,128)(2,1)S(1)}, bf16[176,512]{1,0:T(8,128)(2,1)S(1)}, u32[]{:S(2)}, u32[]{:S(2)}) collective-permute-start(bf16[176,512]{1,0:T(8,128)(2,1)S(1)} %get-tuple-element.106), channel_id=1, source_target_pairs={{0,8},{8,0},{16,24},{24,16},{1,9},{9,1},{17,25},{25,17},{2,10},{10... | collective-permute-start | bytes 540680 | tf_op jit(solution)/shard_map/ppermute | solution.py:969
  446.1 12.6 %copy-start.2 = (bf16[32,128,384]{2,1,0:T(8,128)(2,1)S(1)}, bf16[32,128,384]{2,1,0:T(8,128)(2,1)}, u32[]{:S(2)}) copy-start(bf16[32,128,384]{2,1,0:T(8,128)(2,1)} %get-tuple-element.82.refs_0_.refs_1_) | copy-start | bytes 9437188
  458.6 1.7 copy-start.21
  458.6 2.1 copy-start.18
  462.3 1.6 copy-start.15
  462.3 1.6 copy-start.17
  465.7 55.7 %all-to-all-start.8 = ((bf16[8,512,384]{2,1,0:T(8,128)(2,1)}), bf16[8,512,384]{2,1,0:T(8,128)(2,1)}, u32[]{:S(2)}, u32[]{:S(2)}) async-start(bf16[8,512,384]{2,1,0:T(8,128)(2,1)} %bitcast.124), calls=%async_computation.9 | async-start | bytes 6291456 | tf_op jit(solution)/shard_map/all_to_all | solution.py:1073
  470.1 108.4 %all-gather.23.cloned.1.call-start = ((), (), s32[]{:S(2)}) async-start(), calls=%async_computation.18 | async-start | bytes 6635520 | tf_op jit(solution)/shard_map/all_gather | solution.py:1097
  472.0 2.3 copy-start.4
  472.0 23.8 %copy-start.12 = (bf16[176,512]{1,0:T(8,128)(2,1)S(1)}, bf16[176,512]{1,0:T(8,128)(2,1)}, u32[]{:S(2)}) copy-start(bf16[176,512]{1,0:T(8,128)(2,1)} %fusion.8.refs_2_) | copy-start | bytes 540676
  474.3 19.2 %collective-permute-start.10 = (bf16[272,1024]{1,0:T(8,128)(2,1)S(1)}, bf16[272,1024]{1,0:T(8,128)(2,1)S(1)}, u32[]{:S(2)}, u32[]{:S(2)}) collective-permute-start(bf16[272,1024]{1,0:T(8,128)(2,1)S(1)} %get-tuple-element.101), channel_id=1, source_target_pairs={{3,0},{7,4},{11,8},{15,12},{19,16},{23,20},{27,24},{31,28}} | collective-permute-start | bytes 1671176 | tf_op jit(solution)/shard_map/ppermute | solution.py:920
  475.6 20.3 %collective-permute-start.9 = (bf16[272,1024]{1,0:T(8,128)(2,1)}, bf16[272,1024]{1,0:T(8,128)(2,1)S(1)}, u32[]{:S(2)}, u32[]{:S(2)}) collective-permute-start(bf16[272,1024]{1,0:T(8,128)(2,1)} %get-tuple-element.102), channel_id=1, source_target_pairs={{0,3},{4,7},{8,11},{12,15},{16,19},{20,23},{24,27},{28,31}} | collective-permute-start | bytes 1671176 | tf_op jit(solution)/shard_map/ppermute | solution.py:920
  482.0 34.8 %collective-permute-start.8 = (bf16[272,1024]{1,0:T(8,128)(2,1)}, bf16[272,1024]{1,0:T(8,128)(2,1)S(1)}, u32[]{:S(2)}, u32[]{:S(2)}) collective-permute-start(bf16[272,1024]{1,0:T(8,128)(2,1)} %get-tuple-element.103), channel_id=1, source_target_pairs={{2,0},{3,1},{6,4},{7,5},{10,8},{11,9},{14,12},{15,13},{18,16},{19,... | collective-permute-start | bytes 1671176 | tf_op jit(solution)/shard_map/ppermute | solution.py:920
  483.3 33.5 %collective-permute-start.7 = (bf16[272,1024]{1,0:T(8,128)(2,1)}, bf16[272,1024]{1,0:T(8,128)(2,1)S(1)}, u32[]{:S(2)}, u32[]{:S(2)}) collective-permute-start(bf16[272,1024]{1,0:T(8,128)(2,1)} %get-tuple-element.104), channel_id=1, source_target_pairs={{0,2},{1,3},{4,6},{5,7},{8,10},{9,11},{12,14},{13,15},{16,18},{17,... | collective-permute-start | bytes 1671176 | tf_op jit(solution)/shard_map/ppermute | solution.py:920
  488.8 28.2 %collective-permute-start.6 = (bf16[272,1024]{1,0:T(8,128)(2,1)}, bf16[272,1024]{1,0:T(8,128)(2,1)}, u32[]{:S(2)}, u32[]{:S(2)}) collective-permute-start(bf16[272,1024]{1,0:T(8,128)(2,1)} %get-tuple-element.105), channel_id=1, source_target_pairs={{1,0},{2,1},{3,2},{5,4},{6,5},{7,6},{9,8},{10,9},{11,10},{13,12},{... | collective-permute-start | bytes 1671176 | tf_op jit(solution)/shard_map/ppermute | solution.py:920
  493.5 24.8 %collective-permute-start.5 = (bf16[272,1024]{1,0:T(8,128)(2,1)}, bf16[272,1024]{1,0:T(8,128)(2,1)}, u32[]{:S(2)}, u32[]{:S(2)}) collective-permute-start(bf16[272,1024]{1,0:T(8,128)(2,1)} %get-tuple-element.100), channel_id=1, source_target_pairs={{0,1},{1,2},{2,3},{4,5},{5,6},{6,7},{8,9},{9,10},{10,11},{12,13},{... | collective-permute-start | bytes 1671176 | tf_op jit(solution)/shard_map/ppermute | solution.py:920
  531.1 13.1 %copy-start.7 = (bf16[16,32,2816]{2,1,0:T(8,128)(2,1)S(1)}, bf16[16,32,2816]{2,1,0:T(8,128)(2,1)}, u32[]{:S(2)}) copy-start(bf16[16,32,2816]{2,1,0:T(8,128)(2,1)} %all-gather.21.cloned.1.call-done) | copy-start | bytes 8650756
  578.5 9.6 %copy-start.1 = (bf16[704,1024]{1,0:T(8,128)(2,1)S(1)}, bf16[704,1024]{1,0:T(8,128)(2,1)}, u32[]{:S(2)}) copy-start(bf16[704,1024]{1,0:T(8,128)(2,1)} %param.39) | copy-start | bytes 4325380
  (9 other events, 9.5 us)
Sparse Core Ops, SparseCore 0:
  10.5 61.6 all-gather.12
  74.6 63.2 all-gather.14
  150.5 67.1 all-gather.16
  220.1 45.5 all-gather.18
  269.0 99.5 reduce-scatter.2
  371.9 94.5 reduce-scatter.4
  468.9 50.2 all-gather.20
  521.6 56.8 all-gather.22
